TPU v7x, 32 devices: a whole 2x2x4 slice. The times are simulated.
32 devices in a mesh: dp: 8 (over y, x, core), tensor: 4 (over z).
Axes of the slice: x: 2, y: 2, z: 4, core: 2. Of those that a mesh axis runs over, the one named last changes fastest.
Arguments:
- hidden: bfloat16 [1024, 16384], P('dp'), may hold values from -6 to 6
- context: bfloat16 [1024, 16384], P('dp', 'tensor'), may hold values from -6 to 6
- query_weight: bfloat16 [16384, 16384], P(('dp', 'tensor')), may hold values from -0.046875 to 0.046875
- key_projection_rows: bfloat16 [16384, 1024], P(('dp', 'tensor')), may hold values from -0.046875 to 0.046875
- value_weight: bfloat16 [16384, 1024], P(('dp', 'tensor')), may hold values from -0.046875 to 0.046875
- query_lower_factor: bfloat16 [16384, 64], P(('dp', 'tensor')), may hold values from -0.75 to 0.75
- key_down: bfloat16 [16384, 64], P(('dp', 'tensor')), may hold values from -0.75 to 0.75
- value_down: bfloat16 [16384, 64], P(('dp', 'tensor')), may hold values from -0.75 to 0.75
- query_up: bfloat16 [64, 16384], P(None, ('dp', 'tensor')), may hold values from -0.01171875 to 0.01171875
- key_up: bfloat16 [64, 1024], replicated, may hold values from -0.01171875 to 0.01171875
- value_up: bfloat16 [64, 1024], replicated, may hold values from -0.01171875 to 0.01171875
- output_weight: bfloat16 [16384, 16384], P(('dp', 'tensor')), may hold values from -0.046875 to 0.046875
- output_down: bfloat16 [16384, 64], P(('dp', 'tensor')), may hold values from -0.75 to 0.75
- output_up: bfloat16 [64, 16384], P(None, ('dp', 'tensor')), may hold values from -0.01171875 to 0.01171875
- slice_group: int32 [8], replicated, may hold values from 0 to 7, each once
Outputs:
- merged_qkv: bfloat16 [16384, 18432], P('dp', 'tensor')
- merged_output: bfloat16 [16384, 16384], P('tensor', 'dp')
- projections: bfloat16 [1024, 18432], P('dp', 'tensor')
- attention_output: bfloat16 [1024, 16384], P('tensor', 'dp')
Inputs may be any that keep to these rules, and one draw needn't show every extreme that they name: Serving slice t holds the key-value groups slice_group[t*2] .. slice_group[t*2 + 1]; every group appears once.
All inputs are finite; a program needn't handle non-finite values.
Results may differ from a plain program's by a relative error of at most 0.012.
Values may be sent and summed in bfloat16 or wider, within the bound.
No kernel may reach another device: no remote copies, remote signals or barrier semaphores. Data moves between devices by JAX's collectives and lax.ppermute only.
A program may use at most 320 MiB of HBM per device.

v0:
```python
import jax
import jax.numpy as jnp
from jax import lax
from jax.sharding import PartitionSpec as P

adapter_scale_factor = 2.0


def merge_adapter(frozen_base_matrix, down_factor, up_factor):
    adapter_update = jnp.dot(down_factor, up_factor, preferred_element_type=jnp.float32)
    return (frozen_base_matrix.astype(jnp.float32) + adapter_scale_factor * adapter_update).astype(
        jnp.bfloat16
    )


def body(
    hidden,
    context,
    query_weight,
    key_projection_rows,
    value_weight,
    query_lower_factor,
    key_down,
    value_down,
    query_up,
    key_up,
    value_up,
    output_weight,
    output_down,
    output_up,
    slice_group,
):
    groups = slice_group.shape[0]
    tensor_count = lax.axis_size("tensor")
    dp_count = lax.axis_size("dp")
    per_slice = groups // tensor_count
    query_up_all, output_raise_gathered = (
        lax.all_gather(query_up, ("dp", "tensor"), axis=1, tiled=True),
        lax.all_gather(output_up, ("dp", "tensor"), axis=1, tiled=True),
    )
    merged_query = merge_adapter(query_weight, query_lower_factor, query_up_all)
    merged_key = merge_adapter(key_projection_rows, key_down, key_up)
    merged_value = merge_adapter(value_weight, value_down, value_up)
    row_count = query_weight.shape[0]
    group_cols = merged_query.shape[1] // groups
    head_cols = merged_key.shape[1] // groups
    query_sel = jnp.take(merged_query.reshape(row_count, groups, group_cols), slice_group, axis=1)
    key_sel = jnp.take(merged_key.reshape(row_count, groups, head_cols), slice_group, axis=1)
    value_sel = jnp.take(merged_value.reshape(row_count, groups, head_cols), slice_group, axis=1)
    packed = jnp.concatenate((query_sel, key_sel, value_sel), axis=2)
    packed = packed.reshape(row_count, tensor_count, per_slice * (group_cols + 2 * head_cols))
    arrived = lax.all_to_all(packed, "tensor", split_axis=1, concat_axis=0, tiled=True)
    merged_qkv = arrived.reshape(tensor_count * row_count, arrived.shape[2])
    merged_out = merge_adapter(output_weight, output_down, output_raise_gathered)
    out_rows = output_weight.shape[0]
    by_source = lax.all_to_all(merged_out, "dp", split_axis=1, concat_axis=0, tiled=True)
    block_cols = by_source.shape[1]
    grouped = jnp.take(
        by_source.reshape(groups, dp_count // groups, out_rows, block_cols), slice_group, axis=0
    )
    outgoing = grouped.reshape(tensor_count, per_slice, dp_count // groups, 1, out_rows, block_cols)
    received = lax.all_to_all(outgoing, "tensor", split_axis=0, concat_axis=3, tiled=True)
    merged_output = received.reshape(
        per_slice * (dp_count // groups) * tensor_count * out_rows, block_cols
    )
    columns = lax.all_to_all(hidden, "dp", split_axis=1, concat_axis=0, tiled=True)
    projections = lax.psum_scatter(
        jnp.dot(columns, merged_qkv, preferred_element_type=jnp.float32).astype(jnp.bfloat16),
        "dp",
        scatter_dimension=0,
        tiled=True,
    )
    partial_value = jnp.dot(
        lax.all_gather(context, "dp", axis=0, tiled=True),
        merged_output,
        preferred_element_type=jnp.float32,
    )
    attention_output = lax.psum_scatter(
        partial_value.astype(jnp.bfloat16), "tensor", scatter_dimension=0, tiled=True
    )
    return (merged_qkv, merged_output, projections, attention_output)


def solution(mesh):
    placed = (
        P("dp", None),
        P("dp", "tensor"),
        P(("dp", "tensor"), None),
        P(("dp", "tensor"), None),
        P(("dp", "tensor"), None),
        P(("dp", "tensor"), None),
        P(("dp", "tensor"), None),
        P(("dp", "tensor"), None),
        P(None, ("dp", "tensor")),
        P(),
        P(),
        P(("dp", "tensor"), None),
        P(("dp", "tensor"), None),
        P(None, ("dp", "tensor")),
        P(),
    )
    return jax.shard_map(
        body,
        mesh=mesh,
        in_specs=placed,
        out_specs=(P("dp", "tensor"), P("tensor", "dp"), P("dp", "tensor"), P("tensor", "dp")),
        check_vma=False,
    )
```

profile of v0, /device:TPU:0, one launch (start us, length us, event | category | flops | bytes accessed | tf_op | source)
XLA Modules:
  0.0 1468.9 jit_solution(17139963771881586525)
XLA Ops:
  8.7 60.7 %all-gather.6.cloned.1.call-done = bf16[64,16384]{1,0:T(8,128)(2,1)} async-done(((bf16[64,512]{1,0:T(8,128)(2,1)}), bf16[64,16384]{1,0:T(8,128)(2,1)}) %all-gather.6.cloned.1.call-update) | async-done | bytes 2097168 | tf_op jit(solution)/shard_map/all_gather | solution.py:39
  69.5 12.2 add_convert_fusion
  81.7 14.2 copy.91
  101.8 6.4 copy.76
  108.3 177.4 %all-to-all-done.1 = bf16[512,8,2048]{2,0,1:T(8,128)(2,1)} async-done(((bf16[512,8,2048]{2,0,1:T(8,128)(2,1)}), bf16[512,8,2048]{2,0,1:T(8,128)(2,1)}, u32[]{:S(2)}, u32[]{:S(2)}) %all-to-all-start.1) | async-done | bytes 16777248 | tf_op jit(solution)/shard_map/all_to_all | solution.py:56
  290.3 11.7 slice_bitcast_fusion.1
  302.0 8.1 gather_fusion.2
  310.1 8.2 gather_fusion.3
  318.4 8.1 pad_maximum_fusion.1
  326.5 7.1 broadcast_select_fusion
  339.4 7.0 all-to-all-start.2
  353.7 366.0 %all-gather.4.cloned.1.call-done = bf16[64,16384]{1,0:T(8,128)(2,1)} async-done(((bf16[64,512]{1,0:T(8,128)(2,1)}), bf16[64,16384]{1,0:T(8,128)(2,1)}) %all-gather.4.cloned.1.call-update) | async-done | bytes 2097168 | tf_op jit(solution)/shard_map/all_gather | solution.py:38
  719.7 12.5 add_convert_fusion.1
  732.3 15.1 %copy.87 = bf16[64,8,8,2048]{3,2,1,0:T(8,128)(2,1)S(1)} copy(bf16[64,8,8,2048]{3,1,2,0:T(8,128)(2,1)} %bitcast.69) | data formatting | bytes 33554432
  747.3 6.3 fusion.3
  753.7 11.4 copy.82
  765.0 8.2 gather_fusion
  773.3 11.5 copy.83
  784.8 8.2 gather_fusion.1
  793.0 10.0 maximum_select_fusion
  803.0 13.7 pad_maximum_fusion
  816.6 24.6 %copy.71 = bf16[512,8,2304]{0,2,1:T(8,128)(2,1)} copy(bf16[512,8,2304]{2,0,1:T(8,128)(2,1)} %pad_maximum_fusion) | data formatting | bytes 37748736 | tf_op jit(solution)/shard_map/concatenate | solution.py:50
  841.3 7.4 all-to-all-start
  849.3 14.3 copy.75
  863.7 41.2 %all-gather.8.cloned.1.call-done = bf16[1024,4096]{1,0:T(8,128)(2,1)} async-done(((bf16[128,4096]{1,0:T(8,128)(2,1)}), bf16[1024,4096]{1,0:T(8,128)(2,1)}) %all-gather.8.cloned.1.call-update) | async-done | bytes 8388624 | tf_op jit(solution)/shard_map/all_gather | solution.py:74
  904.8 24.0 %convert_bitcast_fusion = bf16[1024,2048]{0,1:T(8,128)(2,1)} fusion(bf16[4096,2048]{1,0:T(8,128)(2,1)} %bitcast.76, bf16[1024,4096]{1,0:T(8,128)(2,1)} %all-gather.8.cloned.1.call-done), kind=kOutput, calls=%fused_computation.17 | convolution fusion | flops 17181966336 | bytes 29360128 | tf_op jit(solution)/shard_map/dot_general | solution.py:73
  928.9 6.8 copy.77
  935.6 389.0 %all-to-all-done = bf16[512,4,4608]{0,2,1:T(8,128)(2,1)} async-done(((bf16[512,4,4608]{0,2,1:T(8,128)(2,1)}), bf16[512,4,4608]{0,2,1:T(8,128)(2,1)}, u32[]{:S(2)}, u32[]{:S(2)}) %all-to-all-start) | async-done | bytes 18874400 | tf_op jit(solution)/shard_map/all_to_all | solution.py:52
  1324.6 24.6 %copy.72 = bf16[4,512,1,4608]{3,1,0,2:T(8,128)(2,1)} copy(bf16[4,512,1,4608]{1,3,0,2:T(8,128)(2,1)} %bitcast.6) | data formatting | bytes 37748736 | tf_op jit(solution)/shard_map/all_to_all | solution.py:52
  1349.2 26.0 %fusion = bf16[1024,4608]{0,1:T(8,128)(2,1)} fusion(bf16[2048,4608]{1,0:T(8,128)(2,1)} %bitcast.74, bf16[1024,2048]{1,0:T(8,128)(2,1)} %bitcast.81), kind=kOutput, calls=%fused_computation.16 | convolution fusion | flops 19332071424 | bytes 32505856 | tf_op jit(solution)/shard_map/dot_general | solution.py:68
  1375.2 12.2 copy.80
  1389.8 71.6 %reduce-scatter.7.cloned.1.call-done = bf16[128,4608]{1,0:T(8,128)(2,1)} async-done(((bf16[1024,4608]{1,0:T(8,128)(2,1)}), bf16[128,4608]{1,0:T(8,128)(2,1)}) %reduce-scatter.7.cloned.1.call-update) | async-done | bytes 1179664
  (43 shorter events, 27.2 us)
Async XLA Ops:
  8.0 339.2 %copy-start = (bf16[64,1024]{1,0:T(8,128)(2,1)S(1)}, bf16[64,1024]{1,0:T(8,128)(2,1)}, u32[]{:S(2)}) copy-start(bf16[64,1024]{1,0:T(8,128)(2,1)} %param.26) | copy-start | bytes 393220
  8.0 61.5 %all-gather.6.cloned.1.call-start = ((), (), s32[]{:S(2)}) async-start(), calls=%async_computation.7 | async-start | bytes 2162688 | tf_op jit(solution)/shard_map/all_gather | solution.py:39
  95.9 12.3 copy-start.7
  95.9 189.8 %all-to-all-start.1 = ((bf16[512,8,2048]{2,0,1:T(8,128)(2,1)}), bf16[512,8,2048]{2,0,1:T(8,128)(2,1)}, u32[]{:S(2)}, u32[]{:S(2)}) async-start(bf16[512,8,2048]{2,0,1:T(8,128)(2,1)} %bitcast.65), calls=%async_computation.1 | async-start | bytes 33554432 | tf_op jit(solution)/shard_map/all_to_all | solution.py:56
  285.7 53.7 %all-to-all-start.3 = ((bf16[128,8,2048]{0,2,1:T(8,128)(2,1)}), bf16[128,8,2048]{0,2,1:T(8,128)(2,1)}, u32[]{:S(2)}, u32[]{:S(2)}) async-start(bf16[128,8,2048]{0,2,1:T(8,128)(2,1)} %bitcast.78), calls=%async_computation.3 | async-start | bytes 8388608 | tf_op jit(solution)/shard_map/all_to_all | solution.py:66
  333.6 13.6 copy-start.2
  333.6 13.6 copy-start.5
  333.6 15.1 %copy-start.3 = (bf16[64,1024]{1,0:T(8,128)(2,1)S(1)}, bf16[64,1024]{1,0:T(8,128)(2,1)}, u32[]{:S(2)}) copy-start(bf16[64,1024]{1,0:T(8,128)(2,1)} %param.27) | copy-start | bytes 393220
  333.6 15.1 %copy-start.6 = (bf16[512,64]{0,1:T(8,128)(2,1)S(1)}, bf16[512,64]{0,1:T(8,128)(2,1)}, u32[]{:S(2)}) copy-start(bf16[512,64]{0,1:T(8,128)(2,1)} %param.24) | copy-start | bytes 196612
  339.4 501.9 %all-to-all-start.2 = ((bf16[4,2,1,1,512,2048]{5,4,1,3,2,0:T(8,128)(2,1)}), bf16[4,2,1,1,512,2048]{5,4,1,3,2,0:T(8,128)(2,1)}, u32[]{:S(2)}, u32[]{:S(2)}) async-start(bf16[4,2,1,1,512,2048]{5,4,1,3,2,0:T(8,128)(2,1)} %broadcast_select_fusion), calls=%async_computation.2 | async-start | bytes 33554432 | tf_op jit(solution)/shard_map/all_to_all | solution.py:62
  346.5 373.3 %copy-start.4 = (bf16[512,64]{0,1:T(8,128)(2,1)S(1)}, bf16[512,64]{0,1:T(8,128)(2,1)}, u32[]{:S(2)}) copy-start(bf16[512,64]{0,1:T(8,128)(2,1)} %param.22) | copy-start | bytes 196612
  346.5 373.3 %all-gather.4.cloned.1.call-start = ((), (), s32[]{:S(2)}) async-start(), calls=%async_computation.6 | async-start | bytes 2162688 | tf_op jit(solution)/shard_map/all_gather | solution.py:38
  841.3 483.3 %all-to-all-start = ((bf16[512,4,4608]{0,2,1:T(8,128)(2,1)}), bf16[512,4,4608]{0,2,1:T(8,128)(2,1)}, u32[]{:S(2)}, u32[]{:S(2)}) async-start(bf16[512,4,4608]{0,2,1:T(8,128)(2,1)} %bitcast.64), calls=%async_computation | async-start | bytes 37748736 | tf_op jit(solution)/shard_map/all_to_all | solution.py:52
  848.7 56.1 %all-gather.8.cloned.1.call-start = ((), (), s32[]{:S(2)}) async-start(), calls=%async_computation.8 | async-start | bytes 9437184 | tf_op jit(solution)/shard_map/all_gather | solution.py:74
  849.3 538.2 %reduce-scatter.5.cloned.1.call-start = ((), (), s32[]{:S(2)}) async-start(), calls=%async_computation.9 | async-start | bytes 5242880 | tf_op jit(solution)/shard_map/reduce_scatter | solution.py:78
  928.8 532.5 %reduce-scatter.7.cloned.1.call-start = ((), (), s32[]{:S(2)}) async-start(), calls=%async_computation.10 | async-start | bytes 10616832
  1375.2 86.1 %copy-start.1 = (bf16[64,1024]{1,0:T(8,128)(2,1)S(1)}, bf16[64,1024]{1,0:T(8,128)(2,1)}, u32[]{:S(2)}) copy-start(bf16[64,1024]{1,0:T(8,128)(2,1)} %param.26) | copy-start | bytes 393220
Sparse Core Ops, SparseCore 0:
  11.7 57.7 all-gather.5
  350.2 369.4 all-gather.3
  928.9 142.1 reduce-scatter.4
  1387.6 73.7 reduce-scatter.6
Sparse Core Ops, SparseCore 1:
  851.0 53.7 all-gather.7
where the time goes:
time: 1480 us; the launch traced here: 1470 us
  waiting for transfers between devices  1110 us (75%)
  local copies, waits for them, and re-layouts  197 us (13%)
  matrix products  76.9 us (5%)
  other arithmetic  40.3 us (3%)
  starting transfers between devices  25.3 us (2%)
  between operations  15.8 us (1%)
    all_to_all x1, waiting for transfers between devices, body(): lax.all_to_all(packed, 'tensor', split_axis=1, concat_axis=0, tiled=True)  389 us
    all_gather x1, waiting for transfers between devices, body(): lax.all_gather(query_up, ('dp', 'tensor'), axis=1, tiled=True)  366 us
    all_to_all x1, waiting for transfers between devices, body(): lax.all_to_all(merged_out, 'dp', split_axis=1, concat_axis=0, tiled=True)  177 us
    unnamed x6, waiting for transfers between devices  73.3 us
    all_gather x1, waiting for transfers between devices, body(): lax.all_gather(output_up, ('dp', 'tensor'), axis=1, tiled=True)  60.7 us
    unnamed x22, local copies, waits for them, and re-layouts  58.9 us
    all_gather x1, waiting for transfers between devices, body(): lax.all_gather(context, 'dp', axis=0, tiled=True)  41.2 us
  transfers between devices with their start and end apart: 9, of which 7 were waited for; matrix products, arithmetic and copies ran while one was open for 20% of the time, Pallas kernels for 0%

commit v1 on v0

v1 whole, which is shorter than its diff:
```python
import functools

import jax
import jax.numpy as jnp
from jax import lax
from jax.experimental import pallas as pl
from jax.experimental.pallas import tpu as pltpu
from jax.sharding import PartitionSpec as P

adapter_scale_factor = 2.0
f32, bf16 = jnp.float32, jnp.bfloat16
PARAMS = dict(vmem_limit_bytes=56 * 1024 * 1024)


def swap(x, axis, mask):
    n = lax.axis_size(axis)
    return lax.ppermute(x, axis, [(i, i ^ mask) for i in range(n)])


def flipped(value, bits):
    out = 0
    for b in range(bits):
        out = out | (((value >> b) & 1) << (bits - 1 - b))
    return out


def cost(flops, nbytes):
    return pl.CostEstimate(
        flops=int(flops) // 64, bytes_accessed=int(nbytes) // 64, transcendentals=0
    )


ANY = pl.BlockSpec(memory_space=pl.ANY)
VMEM = pl.BlockSpec(memory_space=pltpu.VMEM)


def merged_t(base, down_t, up):
    update = lax.dot_general(down_t, up, (((0,), (0,)), ((), ())), preferred_element_type=f32)
    return (base.astype(f32) + adapter_scale_factor * update).astype(bf16)


def call(kernel, grid, in_specs, out_specs, out_shape, name, flops, nbytes, scratch=(), alias={}):
    return pl.pallas_call(
        kernel,
        grid_spec=pltpu.PrefetchScalarGridSpec(
            num_scalar_prefetch=1,
            grid=grid,
            in_specs=in_specs,
            out_specs=out_specs,
            scratch_shapes=scratch,
        ),
        out_shape=out_shape,
        input_output_aliases=alias,
        compiler_params=pltpu.CompilerParams(**PARAMS),
        cost_estimate=cost(flops, nbytes),
        name=name,
    )


def merge_key_value(info, key_w, value_w, key_dt, value_dt, key_u, value_u):
    def kernel(info_ref, kw, vw, kd, vd, ku, vu, mk, mv):
        mk[...] = merged_t(kw[...], kd[...], ku[...])
        mv[...] = merged_t(vw[...], vd[...], vu[...])

    shape = jax.ShapeDtypeStruct(key_w.shape, bf16)
    size = key_w.size
    return call(
        kernel, (), [VMEM] * 6, [VMEM] * 2, [shape] * 2, "merge_key_value", 256 * size, 8 * size
    )(info, key_w, value_w, key_dt, value_dt, key_u, value_u)


def group_of(s, j, i, per):
    return i[1 + (i[0] ^ s) * per + j]


def pick_qkv(info, query_w, keys, values, s, j, groups, per, after):
    rb, width = query_w.shape
    hd = keys.shape[1] // groups
    cols = width // groups
    tile = 2 * hd
    wide = cols // tile

    def kernel(info_ref, q, k, v, *rest):
        last = pl.program_id(0) == wide

        @pl.when(jnp.logical_not(last))
        def _():
            rest[-1][...] = q[...]

        @pl.when(last)
        def _():
            rest[-1][:, :hd] = k[...]
            rest[-1][:, hd:] = v[...]

    def query_at(n, i):
        return (0, group_of(s, j, i, per) * wide + jnp.minimum(n, wide - 1))

    def head_at(n, i):
        return (0, group_of(s, j, i, per))

    return call(
        kernel,
        (wide + 1,),
        [
            pl.BlockSpec((rb, tile), query_at),
            pl.BlockSpec((rb, hd), head_at),
            pl.BlockSpec((rb, hd), head_at),
        ]
        + [ANY] * len(after),
        pl.BlockSpec((rb, tile), lambda n, i: (0, n)),
        jax.ShapeDtypeStruct((rb, cols + tile), bf16),
        f"pick_qkv_{s}_{j}",
        0,
        4 * rb * (cols + tile),
    )(info, query_w, keys, values, *after)


def split_columns(info, weight, tokens, nd):
    rows, width = weight.shape
    more = tokens.shape[0]
    wide = width // nd

    def kernel(info_ref, w, t, out):
        out[0, :rows, :] = w[...]
        out[0, rows:, :] = t[...]

    return call(
        kernel,
        (nd,),
        [
            pl.BlockSpec((rows, wide), lambda d, i: (0, d)),
            pl.BlockSpec((more, wide), lambda d, i: (0, d)),
        ],
        pl.BlockSpec((1, rows + more, wide), lambda d, i: (d, 0, 0)),
        jax.ShapeDtypeStruct((nd, rows + more, wide), bf16),
        "split_columns",
        0,
        4 * (rows + more) * width,
    )(info, weight, tokens)


def pick_output(info, blocks, rb, factors, ups, s, first, count, tile, per, dpg, after):
    parts = per * dpg
    nt, rank, cb = ups.shape
    bits = nt.bit_length() - 1
    piece = min(tile, cb)
    pieces = tile // piece

    def kernel(info_ref, x, d, *rest):
        up = jnp.concatenate([u[0] for u in rest[:pieces]], axis=1)
        rest[-1][0] = merged_t(x[0], d[...], up)

    def source(l, i):
        return group_of(s, l // dpg, i, per) * dpg + l % dpg

    def up_at(p, l, c, i):
        at = (first + c) * tile + p * piece
        return (flipped((at // cb) ^ i[0], bits), 0, at % cb // piece)

    return call(
        kernel,
        (parts, count),
        [
            pl.BlockSpec((1, rb, tile), lambda l, c, i: (source(l, i), 0, first + c)),
            pl.BlockSpec((rank, rb), lambda l, c, i: (source(l, i) * (nt + 1) + nt, 0)),
        ]
        + [pl.BlockSpec((1, rank, piece), functools.partial(up_at, p)) for p in range(pieces)]
        + [ANY] * len(after),
        pl.BlockSpec((1, rb, tile), lambda l, c, i: (l, 0, c)),
        jax.ShapeDtypeStruct((parts, rb, count * tile), bf16),
        f"pick_output_{s}_{first}",
        2 * parts * rb * count * tile * rank,
        4 * parts * rb * count * tile,
    )(info, blocks, factors, *[ups] * pieces, *after)


def place_qkv(info, blocks, qkv, downs, factors, gq, per, after):
    nt, rank, cb = downs.shape
    rb, width = qkv[0][0].shape
    bits = nt.bit_length() - 1
    sources, below, depth = blocks.shape
    some = below - rb
    count = sources * some
    tile = width - gq
    each = width // tile
    wide = each - 1
    cols = per * width
    piece = min(tile, cb)
    pieces = tile // piece

    def kernel(info_ref, a, d, *refs):
        u, refs = refs[:pieces], refs[pieces:]
        full, part = refs[-2:]
        place = pl.program_id(0) // each
        last = lax.rem(pl.program_id(0), each) == wide

        def put(blocks):
            total = jnp.zeros((count, tile), f32)
            for s in range(nt):
                at = pl.ds(pl.multiple_of((info_ref[0] ^ s) * rb, rb), rb)
                full[at, :] = blocks[s]
                rows = a[:, :, at].reshape(count, rb)
                total += jnp.dot(rows, blocks[s], preferred_element_type=f32)
            part[...] = total.astype(bf16)

        for j in range(per):
            q = refs[j * nt : (j + 1) * nt]

            @pl.when(jnp.logical_and(place == j, jnp.logical_not(last)))
            def _():
                up = jnp.concatenate([x[...] for x in u], axis=1)
                put([merged_t(q[s][...], d[flipped(s, bits)], up) for s in range(nt)])

            @pl.when(jnp.logical_and(place == j, last))
            def _():
                put([x[...] for x in q])

    def column(j, n, i):
        return (0, jnp.where(n // each == j, n % each, jnp.where(n // each < j, 0, wide)))

    def up_at(p, n, i):
        at = group_of(0, n // each, i, per) * gq + jnp.minimum(n % each, wide - 1) * tile
        block = at // cb + p
        return (block // nt * (nt + 1) + flipped((block % nt) ^ i[0], bits), at % cb // piece)

    return call(
        kernel,
        (per * each,),
        [
            pl.BlockSpec((sources, some, depth), lambda n, i: (0, rb // some, 0)),
            pl.BlockSpec(downs.shape, lambda n, i: (0, 0, 0)),
        ]
        + [pl.BlockSpec((rank, piece), functools.partial(up_at, p)) for p in range(pieces)]
        + [
            pl.BlockSpec((rb, tile), functools.partial(column, j))
            for j in range(per)
            for _ in range(nt)
        ]
        + [ANY] * len(after),
        [
            pl.BlockSpec((nt * rb, tile), lambda n, i: (0, n)),
            pl.BlockSpec((count, tile), lambda n, i: (0, n)),
        ],
        [
            jax.ShapeDtypeStruct((nt * rb, cols), bf16),
            jax.ShapeDtypeStruct((count, cols), bf16),
        ],
        "place_qkv",
        2 * count * depth * cols,
        4 * depth * cols + 2 * count * cols,
    )(info, blocks, downs, *[factors] * pieces, *[x for at in qkv for x in at], *after)


def place_output(info, tokens, arrived, before, first, tile, cols, nt, after):
    parts, rb, width = arrived[0].shape
    rows, depth = tokens.shape
    each = rows // nt

    def kernel(info_ref, a, *refs):
        full, send, keep, term = refs[-4:]
        total = jnp.zeros((rows, tile), f32)
        for s in range(nt):
            for l in range(parts):
                at = pl.ds(pl.multiple_of((l * nt + (info_ref[0] ^ s)) * rb, rb), rb)
                x = refs[s][l]
                full[at, :] = x
                total += jnp.dot(a[:, at], x, preferred_element_type=f32)
        term[...] = total.astype(bf16)
        for s in range(nt):
            at = pl.ds(pl.multiple_of((info_ref[0] ^ s) * each, each), each)
            (send if s % 2 else keep)[s // 2] = term[at, :]

    operands = [info, tokens, *arrived]
    alias = {}
    if before is not None:
        alias = {len(operands): 0}
        after = [before, *after]
    half = jax.ShapeDtypeStruct((nt // 2, each, width), bf16)
    half_spec = pl.BlockSpec((nt // 2, each, tile), lambda c, i: (0, 0, c))
    return call(
        kernel,
        (width // tile,),
        [pl.BlockSpec((rows, depth), lambda c, i: (0, 0))]
        + [pl.BlockSpec((parts, rb, tile), lambda c, i: (0, 0, c))] * nt
        + [ANY] * len(after),
        [
            pl.BlockSpec((depth, tile), lambda c, i: (0, first + c)),
            half_spec,
            half_spec,
        ],
        [jax.ShapeDtypeStruct((depth, cols), bf16), half, half],
        f"place_output_{first}",
        2 * rows * depth * width,
        4 * depth * width,
        [pltpu.VMEM((rows, tile), bf16)],
        alias,
    )(*operands, *after)


def body(
    hidden,
    context,
    query_weight,
    key_projection_rows,
    value_weight,
    query_lower_factor,
    key_down,
    value_down,
    query_up,
    key_up,
    value_up,
    output_weight,
    output_down,
    output_up,
    slice_group,
):
    groups = slice_group.shape[0]
    nt, nd = lax.axis_size("tensor"), lax.axis_size("dp")
    bits = nt.bit_length() - 1
    per, dpg = groups // nt, nd // groups
    rank, cb = query_up.shape
    info = jnp.concatenate((lax.axis_index("tensor").astype(jnp.int32)[None], slice_group))

    order = list(range(nt // 2, nt)) + list(range(1, nt // 2)) + [0]

    def exchange(sent):
        return {s: swap(x, "tensor", s) if s else x for s, x in sent.items()}

    outgoing = split_columns(info, output_weight, hidden, nd)
    blocks = lax.all_to_all(outgoing, "dp", split_axis=0, concat_axis=0, tiled=True)

    keys, values = merge_key_value(
        info, key_projection_rows, value_weight, key_down.T, value_down.T, key_up, value_up
    )
    qkv = []
    for j in range(per):
        sent = {
            s: pick_qkv(info, query_weight, keys, values, s, j, groups, per, []) for s in order
        }
        got = exchange(sent)
        qkv.append([got[s] for s in range(nt)])

    factors = jnp.stack((query_up, output_up, query_lower_factor.T))[None]
    for b in reversed(range(bits)):
        factors = jnp.concatenate((factors, swap(factors, "tensor", 1 << b)))
    output_ups, query_downs = factors[:, 1], factors[:, 2]
    factors = jnp.concatenate((factors[:, 0].reshape(nt * rank, cb), output_down.T))
    factors = lax.all_gather(factors, "dp", axis=0, tiled=True)

    context_all = lax.all_gather(context, "dp", axis=0, tiled=True)

    cols = blocks.shape[2]
    tile = cols // 8
    chunks = ((0, 3), (3, 3), (6, 1), (7, 1))
    merged_output = None
    sums, early, done = [], [], []
    for n, (first, count) in enumerate(chunks):
        last = n == len(chunks) - 1
        after = done[n - 2] if n >= 2 else []
        if last:
            after = after + sums[:1]
        sent = {
            s: pick_output(
                info, blocks, output_weight.shape[0], factors, output_ups, s, first, count, tile, per, dpg, after if s else []
            )
            for s in order
        }
        got = exchange(sent)
        done.append([got[s] for s in order if s])
        if n == 1:
            merged_qkv, partial = place_qkv(
                info, blocks, qkv, query_downs, factors, query_weight.shape[1] // groups, per,
                done[0],
            )
            projections = lax.psum_scatter(partial, "dp", scatter_dimension=0, tiled=True)
        merged_output, send, keep = place_output(
            info, context_all, [got[s] for s in range(nt)], merged_output, first, tile, cols, nt,
            sums[1:-1] + early[-1:] if last else [],
        )
        for b in range(bits):
            total = (keep.astype(f32) + swap(send, "tensor", 1 << b).astype(f32)).astype(bf16)
            if b == 0:
                early.append(total)
            send, keep = total[1::2], total[0::2]
        sums.append(keep[0])
    attention_output = jnp.concatenate(sums, axis=1)
    return (merged_qkv, merged_output, projections, attention_output)


def solution(mesh):
    rows = P(("dp", "tensor"), None)
    ups = P(None, ("dp", "tensor"))
    placed = (
        P("dp", None),
        P("dp", "tensor"),
        rows,
        rows,
        rows,
        rows,
        rows,
        rows,
        ups,
        P(),
        P(),
        rows,
        rows,
        ups,
        P(),
    )
    return jax.shard_map(
        body,
        mesh=mesh,
        in_specs=placed,
        out_specs=(P("dp", "tensor"), P("tensor", "dp"), P("dp", "tensor"), P("tensor", "dp")),
        check_vma=False,
    )
```

time: 1480 us -> 981 us (0.66)
  waiting for transfers between devices: 1110 us -> 509 us
  Pallas kernels: 0 us -> 227 us
  local copies, waits for them, and re-layouts: 197 us -> 4.92 us
  starting transfers between devices: 25.3 us -> 215 us
  matrix products: 76.9 us -> 0 us
  other arithmetic: 40.3 us -> 8.14 us
    all_gather x3 -> x2, waiting for transfers between devices: 468 us -> 23.2 us  [the longest x1 23.2 us: body(): factors = lax.all_gather(factors, 'dp', axis=0, tiled=True)]
    all_to_all x4 -> x1, waiting for transfers between devices: 572 us -> 137 us  [body(): lax.all_to_all(outgoing, 'dp', split_axis=0, concat_axis=0, tiled=True)]
    ppermute x0 -> x28, waiting for transfers between devices: none -> 348 us  [swap(): return lax.ppermute(x, axis, [(i, i ^ mask) for i in range(n)])]
    pallas_call x0 -> x31, Pallas kernels: none -> 227 us  [the longest x16 71.8 us: pick_output(): call(kernel, (parts, count), [pl.BlockSpec((1, rb, tile), lambda l, c, i:...]
    ppermute x0 -> x28, starting transfers between devices: none -> 209 us  [swap(): return lax.ppermute(x, axis, [(i, i ^ mask) for i in range(n)])]
    dot_general x6 -> x0, matrix products: 76.9 us -> none  [the longest x4 26.9 us: merge_adapter(): jnp.dot(down_factor, up_factor, preferred_element_type=jnp.float32)]
    unnamed x6 -> x3, waiting for transfers between devices: 73.3 us -> 0.73 us
    all_to_all x4 -> x0, local copies, waits for them, and re-layouts: 59.9 us -> none  [the longest x1 24.6 us: body(): lax.all_to_all(packed, 'tensor', split_axis=1, concat_axis=0, tiled=True)]
  transfers between devices with their start and end apart: 9 -> 32, of which waited for: 7 -> 15; matrix products, arithmetic and copies ran while one was open for 20% -> 1% of each run, Pallas kernels for 0% -> 23%
where the time goes in v1:
time: 981 us; the launch traced here: 979 us
  waiting for transfers between devices  509 us (52%)
  Pallas kernels  227 us (23%)
  starting transfers between devices  215 us (22%)
  between operations  14 us (1%)
    ppermute x28, waiting for transfers between devices, swap(): return lax.ppermute(x, axis, [(i, i ^ mask) for i in range(n)])  348 us
    ppermute x28, starting transfers between devices, swap(): return lax.ppermute(x, axis, [(i, i ^ mask) for i in range(n)])  209 us
    all_to_all x1, waiting for transfers between devices, body(): lax.all_to_all(outgoing, 'dp', split_axis=0, concat_axis=0, tiled=True)  137 us
    pallas_call x16, Pallas kernels, pick_output(): call(kernel, (parts, count), [pl.BlockSpec((1, rb, tile), lambda l, c, i:...  71.8 us
    pallas_call x8, Pallas kernels, pick_qkv(): call(kernel, (wide + 1,), [pl.BlockSpec((rb, tile), query_at), pl.BlockSp...  53.7 us
    pallas_call x4, Pallas kernels, place_output(): call(kernel, (width // tile,), [pl.BlockSpec((rows, depth), lambda c, i:...  43.5 us
    pallas_call x1, Pallas kernels, place_qkv(): call(kernel, (per * each,), [pl.BlockSpec((sources, some, depth), lambda...  37.8 us
    all_gather x1, waiting for transfers between devices, body(): factors = lax.all_gather(factors, 'dp', axis=0, tiled=True)  23.2 us
  transfers between devices with their start and end apart: 32, of which 15 were waited for; matrix products, arithmetic and copies ran while one was open for 1% of the time, Pallas kernels for 23%

profile of v1, /device:TPU:0, one launch (start us, length us, event | category | flops | bytes accessed | tf_op | source)
XLA Modules:
  0.0 978.7 jit_solution(43665156861157072)
XLA Ops:
  12.2 9.1 collective-permute-done
  23.5 16.5 %split_columns.1 = bf16[8,640,2048]{2,1,0:T(8,128)(2,1)} custom-call(s32[9]{0:T(128)} %pad_add_fusion.info_ref, bf16[512,16384]{1,0:T(8,128)(2,1)} %w.1, bf16[128,16384]{1,0:T(8,128)(2,1)} %t.1), custom_call_target="tpu_custom_call" | custom-call | bytes 655360 | tf_op jit(solution)/shard_map/split_columns/pallas_call | solution.py:127
  52.7 6.7 pick_qkv_1_0.1
  69.4 6.7 pick_qkv_3_0.1
  77.5 6.8 pick_qkv_1_1.1
  84.9 6.8 pick_qkv_2_1.1
  94.1 6.7 pick_qkv_3_1.1
  100.8 57.8 %collective-permute-done.2.refs_2_ = bf16[512,2304]{1,0:T(8,128)(2,1)} collective-permute-done((bf16[512,2304]{1,0:T(8,128)(2,1)}, bf16[512,2304]{1,0:T(8,128)(2,1)}, u32[]{:S(2)}, u32[]{:S(2)}) %collective-permute-start.2) | collective-permute-done | bytes 2359328 | tf_op jit(solution)/shard_map/ppermute | solution.py:17
  158.6 23.2 %all-gather.3.cloned.1.call-done.d.refs_0_ = bf16[2560,512]{1,0:T(8,128)(2,1)} async-done(((bf16[320,512]{1,0:T(8,128)(2,1)}), bf16[2560,512]{1,0:T(8,128)(2,1)}) %all-gather.3.cloned.1.call-update) | async-done | bytes 2621456 | tf_op jit(solution)/shard_map/all_gather | solution.py:348
  181.8 137.3 %all-to-all-done.x.a = bf16[8,640,2048]{2,1,0:T(8,128)(2,1)} async-done(((bf16[8,640,2048]{2,1,0:T(8,128)(2,1)}), bf16[8,640,2048]{2,1,0:T(8,128)(2,1)}, u32[]{:S(2)}, u32[]{:S(2)}) %all-to-all-start) | async-done | bytes 20971552 | tf_op jit(solution)/shard_map/all_to_all | solution.py:330
  341.1 105.0 %collective-permute-start.10 = (bf16[2,512,768]{2,1,0:T(8,128)(2,1)}, bf16[2,512,768]{2,1,0:T(8,128)(2,1)S(1)}, u32[]{:S(2)}, u32[]{:S(2)}) collective-permute-start(bf16[2,512,768]{2,1,0:T(8,128)(2,1)} %pick_output_1_0.1), channel_id=1, source_target_pairs={{0,1},{1,0},{2,3},{3,2},{4,5},{5,4},{6,7},{7,6},{8,9},{9,8},{10,11... | collective-permute-start | bytes 4718600 | tf_op jit(solution)/shard_map/ppermute | solution.py:17
  446.1 6.6 pick_qkv_0_0.1.refs_1_
  452.8 6.8 pick_qkv_0_1.1.refs_5_
  459.5 34.0 %collective-permute-done.6.refs_7_ = bf16[512,2304]{1,0:T(8,128)(2,1)} collective-permute-done((bf16[512,2304]{1,0:T(8,128)(2,1)}, bf16[512,2304]{1,0:T(8,128)(2,1)}, u32[]{:S(2)}, u32[]{:S(2)}) %collective-permute-start.6) | collective-permute-done | bytes 2359328 | tf_op jit(solution)/shard_map/ppermute | solution.py:17
  493.5 84.2 %collective-permute-done.8.refs_9_.refs_2_.rest_1_ = bf16[2,512,768]{2,1,0:T(8,128)(2,1)S(1)} collective-permute-done((bf16[2,512,768]{2,1,0:T(8,128)(2,1)S(1)}, bf16[2,512,768]{2,1,0:T(8,128)(2,1)S(1)}, u32[]{:S(2)}, u32[]{:S(2)}) %collective-permute-start.8) | collective-permute-done | bytes 1572896 | tf_op jit(solution)/shard_map/ppermute | solution.py:17
  579.8 37.8 %place_qkv.1 = (bf16[2048,4608]{1,0:T(8,128)(2,1)}, bf16[1024,4608]{1,0:T(8,128)(2,1)}) custom-call(s32[9]{0:T(128)} %pad_add_fusion.info_ref, bf16[8,640,2048]{2,1,0:T(8,128)(2,1)} %all-to-all-done.x.a, bf16[4,64,512]{2,1,0:T(8,128)(2,1)} %get-tuple-element.38.d, bf16[2560,512]{1,0:T(8,128)(2,1)} %all-gather.3.cloned.1.call-done.d.refs_0_, ...), custom_call_target="tpu_custom_call" | custom-call | flops 301989888 | bytes 737280 | tf_op jit(solution)/shard_map/place_qkv/pallas_call | solution.py:226
  623.7 35.0 %collective-permute-start.11 = (bf16[2,512,768]{2,1,0:T(8,128)(2,1)}, bf16[2,512,768]{2,1,0:T(8,128)(2,1)S(1)}, u32[]{:S(2)}, u32[]{:S(2)}) collective-permute-start(bf16[2,512,768]{2,1,0:T(8,128)(2,1)} %pick_output_2_3.1), channel_id=1, source_target_pairs={{0,2},{1,3},{2,0},{3,1},{4,6},{5,7},{6,4},{7,5},{8,10},{9,11},{10,... | collective-permute-start | bytes 4718600 | tf_op jit(solution)/shard_map/ppermute | solution.py:17
  677.6 13.5 %place_output_0.1 = (bf16[4096,2048]{1,0:T(8,128)(2,1)}, bf16[2,256,768]{2,1,0:T(8,128)(2,1)}, bf16[2,256,768]{2,1,0:T(8,128)(2,1)}) custom-call(s32[9]{0:T(128)} %pad_add_fusion.info_ref, bf16[1024,4096]{1,0:T(8,128)(2,1)} %all-gather.5.cloned.1.call-done.a, bf16[2,512,768]{2,1,0:T(8,128)(2,1)} %pick_output_0_0.1.refs_0_, bf16[2,512,768]{2,1,0:T(8,128)(2,1)} %copy-done.2, ...), custom_call_target="tpu_custom_call" | custom-call | flops 100663296 | bytes 196608 | tf_op jit(solution)/shard_map/place_output_0/pallas_call | solution.py:280
  699.0 61.4 %collective-permute-done.11.rest_1_.refs_2_ = bf16[2,512,768]{2,1,0:T(8,128)(2,1)S(1)} collective-permute-done((bf16[2,512,768]{2,1,0:T(8,128)(2,1)}, bf16[2,512,768]{2,1,0:T(8,128)(2,1)S(1)}, u32[]{:S(2)}, u32[]{:S(2)}) %collective-permute-start.11) | collective-permute-done | bytes 1572896 | tf_op jit(solution)/shard_map/ppermute | solution.py:17
  760.4 15.8 %collective-permute-done.13.rest_3_.refs_1_ = bf16[2,512,768]{2,1,0:T(8,128)(2,1)} collective-permute-done((bf16[2,512,768]{2,1,0:T(8,128)(2,1)}, bf16[2,512,768]{2,1,0:T(8,128)(2,1)}, u32[]{:S(2)}, u32[]{:S(2)}) %collective-permute-start.13) | collective-permute-done | bytes 1572896 | tf_op jit(solution)/shard_map/ppermute | solution.py:17
  776.2 13.7 %place_output_3.1 = (bf16[4096,2048]{1,0:T(8,128)(2,1)}, bf16[2,256,768]{2,1,0:T(8,128)(2,1)}, bf16[2,256,768]{2,1,0:T(8,128)(2,1)}) custom-call(s32[9]{0:T(128)} %pad_add_fusion.info_ref, bf16[1024,4096]{1,0:T(8,128)(2,1)} %all-gather.5.cloned.1.call-done.a, bf16[2,512,768]{2,1,0:T(8,128)(2,1)} %pick_output_0_3.1.refs_0_, ...), custom_call_target="tpu_custom_call", output_to_operand_aliasing={{0}: (6, {})} | custom-call | flops 100663296 | bytes 196608 | tf_op jit(solution)/shard_map/place_output_3/pallas_call | solution.py:280
  789.9 19.3 %collective-permute-start.22 = (bf16[2,256,768]{2,1,0:T(8,128)(2,1)}, bf16[2,256,768]{2,1,0:T(8,128)(2,1)S(1)}, u32[]{:S(2)}, u32[]{:S(2)}) collective-permute-start(bf16[2,256,768]{2,1,0:T(8,128)(2,1)} %get-tuple-element.29), channel_id=1, source_target_pairs={{0,1},{1,0},{2,3},{3,2},{4,5},{5,4},{6,7},{7,6},{8,9},{9,8},{10,11... | collective-permute-start | bytes 2359304 | tf_op jit(solution)/shard_map/ppermute | solution.py:17
  825.6 24.7 %collective-permute-done.19.refs_1_ = bf16[2,512,256]{2,1,0:T(8,128)(2,1)S(1)} collective-permute-done((bf16[2,512,256]{2,1,0:T(8,128)(2,1)}, bf16[2,512,256]{2,1,0:T(8,128)(2,1)S(1)}, u32[]{:S(2)}, u32[]{:S(2)}) %collective-permute-start.19) | collective-permute-done | bytes 524320 | tf_op jit(solution)/shard_map/ppermute | solution.py:17
  850.3 12.0 %collective-permute-done.21.refs_3_ = bf16[2,512,256]{2,1,0:T(8,128)(2,1)S(1)} collective-permute-done((bf16[2,512,256]{2,1,0:T(8,128)(2,1)}, bf16[2,512,256]{2,1,0:T(8,128)(2,1)S(1)}, u32[]{:S(2)}, u32[]{:S(2)}) %collective-permute-start.21) | collective-permute-done | bytes 524320 | tf_op jit(solution)/shard_map/ppermute | solution.py:17
  863.0 8.1 place_output_6.1
  871.1 11.5 %collective-permute-start.24 = (bf16[2,256,256]{2,1,0:T(8,128)(2,1)}, bf16[2,256,256]{2,1,0:T(8,128)(2,1)S(1)}, u32[]{:S(2)}, u32[]{:S(2)}) collective-permute-start(bf16[2,256,256]{2,1,0:T(8,128)(2,1)} %get-tuple-element.31), channel_id=1, source_target_pairs={{0,1},{1,0},{2,3},{3,2},{4,5},{5,4},{6,7},{7,6},{8,9},{9,8},{10,11... | collective-permute-start | bytes 786440 | tf_op jit(solution)/shard_map/ppermute | solution.py:17
  902.6 10.0 %collective-permute-done.16.refs_1_ = bf16[2,512,256]{2,1,0:T(8,128)(2,1)S(1)} collective-permute-done((bf16[2,512,256]{2,1,0:T(8,128)(2,1)}, bf16[2,512,256]{2,1,0:T(8,128)(2,1)S(1)}, u32[]{:S(2)}, u32[]{:S(2)}) %collective-permute-start.16) | collective-permute-done | bytes 524320 | tf_op jit(solution)/shard_map/ppermute | solution.py:17
  912.6 22.8 %collective-permute-done.17.refs_2_ = bf16[2,512,256]{2,1,0:T(8,128)(2,1)S(1)} collective-permute-done((bf16[2,512,256]{2,1,0:T(8,128)(2,1)}, bf16[2,512,256]{2,1,0:T(8,128)(2,1)S(1)}, u32[]{:S(2)}, u32[]{:S(2)}) %collective-permute-start.17) | collective-permute-done | bytes 524320 | tf_op jit(solution)/shard_map/ppermute | solution.py:17
  936.4 8.1 place_output_7.1
  944.6 10.1 %collective-permute-start.26 = (bf16[2,256,256]{2,1,0:T(8,128)(2,1)}, bf16[2,256,256]{2,1,0:T(8,128)(2,1)S(1)}, u32[]{:S(2)}, u32[]{:S(2)}) collective-permute-start(bf16[2,256,256]{2,1,0:T(8,128)(2,1)} %get-tuple-element.35), channel_id=1, source_target_pairs={{0,1},{1,0},{2,3},{3,2},{4,5},{5,4},{6,7},{7,6},{8,9},{9,8},{10,11... | collective-permute-start | bytes 786440 | tf_op jit(solution)/shard_map/ppermute | solution.py:17
  954.8 8.0 collective-permute-done.26
  964.0 7.0 collective-permute-done.27
  (125 shorter events, 131.5 us)
Async XLA Ops:
  8.1 13.2 %collective-permute-start = (bf16[1,3,64,512]{3,2,0,1:T(8,128)(2,1)S(1)}, bf16[1,3,64,512]{3,2,0,1:T(8,128)(2,1)S(1)}, u32[]{:S(2)}, u32[]{:S(2)}) collective-permute-start(bf16[1,3,64,512]{3,2,0,1:T(8,128)(2,1)S(1)} %maximum_bitcast_fusion), channel_id=1, source_target_pairs={{0,2},{1,3},{2,0},{3,1},{4,6},{5,7},{6,4},{7,5},{8,10},{9,11},{10,... | collective-permute-start | bytes 589832 | tf_op jit(solution)/shard_map/ppermute | solution.py:17
  21.4 24.7 %collective-permute-start.1 = (bf16[2,3,64,512]{3,2,0,1:T(8,128)(2,1)S(1)}, bf16[2,3,64,512]{3,2,0,1:T(8,128)(2,1)S(1)}, u32[]{:S(2)}, u32[]{:S(2)}) collective-permute-start(bf16[2,3,64,512]{3,2,0,1:T(8,128)(2,1)S(1)} %pad_maximum_fusion.2), channel_id=1, source_target_pairs={{0,1},{1,0},{2,3},{3,2},{4,5},{5,4},{6,7},{7,6},{8,9},{9,8},{10,11... | collective-permute-start | bytes 1179656 | tf_op jit(solution)/shard_map/ppermute | solution.py:17
  40.0 279.2 %all-to-all-start = ((bf16[8,640,2048]{2,1,0:T(8,128)(2,1)}), bf16[8,640,2048]{2,1,0:T(8,128)(2,1)}, u32[]{:S(2)}, u32[]{:S(2)}) async-start(bf16[8,640,2048]{2,1,0:T(8,128)(2,1)} %split_columns.1), calls=%async_computation | async-start | bytes 41943040 | tf_op jit(solution)/shard_map/all_to_all | solution.py:330
  46.0 135.8 %all-gather.3.cloned.1.call-start = ((), (), s32[]{:S(2)}) async-start(), calls=%async_computation.2 | async-start | bytes 2949120 | tf_op jit(solution)/shard_map/all_gather | solution.py:348
  47.8 629.7 %all-gather.5.cloned.1.call-start = ((), (), s32[]{:S(2)}) async-start(), calls=%async_computation.3 | async-start | bytes 9437184 | tf_op jit(solution)/shard_map/all_gather | solution.py:350
  48.6 923.5 %reduce-scatter.2.cloned.1.call-start = ((), (), s32[]{:S(2)}) async-start(), calls=%async_computation.4 | async-start | bytes 10616832 | tf_op jit(solution)/shard_map/reduce_scatter | solution.py:375
  59.4 99.3 %collective-permute-start.2 = (bf16[512,2304]{1,0:T(8,128)(2,1)}, bf16[512,2304]{1,0:T(8,128)(2,1)}, u32[]{:S(2)}, u32[]{:S(2)}) collective-permute-start(bf16[512,2304]{1,0:T(8,128)(2,1)} %pick_qkv_1_0.1), channel_id=1, source_target_pairs={{0,1},{1,0},{2,3},{3,2},{4,5},{5,4},{6,7},{7,6},{8,9},{9,8},{10,11... | collective-permute-start | bytes 7077896 | tf_op jit(solution)/shard_map/ppermute | solution.py:17
  67.3 270.0 %collective-permute-start.3 = (bf16[512,2304]{1,0:T(8,128)(2,1)}, bf16[512,2304]{1,0:T(8,128)(2,1)}, u32[]{:S(2)}, u32[]{:S(2)}) collective-permute-start(bf16[512,2304]{1,0:T(8,128)(2,1)} %pick_qkv_2_0.1), channel_id=1, source_target_pairs={{0,2},{1,3},{2,0},{3,1},{4,6},{5,7},{6,4},{7,5},{8,10},{9,11},{10,... | collective-permute-start | bytes 7077896 | tf_op jit(solution)/shard_map/ppermute | solution.py:17
  76.1 264.7 %collective-permute-start.4 = (bf16[512,2304]{1,0:T(8,128)(2,1)}, bf16[512,2304]{1,0:T(8,128)(2,1)}, u32[]{:S(2)}, u32[]{:S(2)}) collective-permute-start(bf16[512,2304]{1,0:T(8,128)(2,1)} %pick_qkv_3_0.1), channel_id=1, source_target_pairs={{0,3},{1,2},{2,1},{3,0},{4,7},{5,6},{6,5},{7,4},{8,11},{9,10},{10,... | collective-permute-start | bytes 7077896 | tf_op jit(solution)/shard_map/ppermute | solution.py:17
  84.3 256.8 %collective-permute-start.5 = (bf16[512,2304]{1,0:T(8,128)(2,1)}, bf16[512,2304]{1,0:T(8,128)(2,1)}, u32[]{:S(2)}, u32[]{:S(2)}) collective-permute-start(bf16[512,2304]{1,0:T(8,128)(2,1)} %pick_qkv_1_1.1), channel_id=1, source_target_pairs={{0,1},{1,0},{2,3},{3,2},{4,5},{5,4},{6,7},{7,6},{8,9},{9,8},{10,11... | collective-permute-start | bytes 7077896 | tf_op jit(solution)/shard_map/ppermute | solution.py:17
  91.7 401.8 %collective-permute-start.6 = (bf16[512,2304]{1,0:T(8,128)(2,1)}, bf16[512,2304]{1,0:T(8,128)(2,1)}, u32[]{:S(2)}, u32[]{:S(2)}) collective-permute-start(bf16[512,2304]{1,0:T(8,128)(2,1)} %pick_qkv_2_1.1), channel_id=1, source_target_pairs={{0,2},{1,3},{2,0},{3,1},{4,6},{5,7},{6,4},{7,5},{8,10},{9,11},{10,... | collective-permute-start | bytes 7077896 | tf_op jit(solution)/shard_map/ppermute | solution.py:17
  158.6 334.9 %collective-permute-start.7 = (bf16[512,2304]{1,0:T(8,128)(2,1)}, bf16[512,2304]{1,0:T(8,128)(2,1)}, u32[]{:S(2)}, u32[]{:S(2)}) collective-permute-start(bf16[512,2304]{1,0:T(8,128)(2,1)} %pick_qkv_3_1.1), channel_id=1, source_target_pairs={{0,3},{1,2},{2,1},{3,0},{4,7},{5,6},{6,5},{7,4},{8,11},{9,10},{10,... | collective-permute-start | bytes 7077896 | tf_op jit(solution)/shard_map/ppermute | solution.py:17
  337.3 240.3 %collective-permute-start.8 = (bf16[2,512,768]{2,1,0:T(8,128)(2,1)S(1)}, bf16[2,512,768]{2,1,0:T(8,128)(2,1)S(1)}, u32[]{:S(2)}, u32[]{:S(2)}) collective-permute-start(bf16[2,512,768]{2,1,0:T(8,128)(2,1)S(1)} %copy-done.9), channel_id=1, source_target_pairs={{0,2},{1,3},{2,0},{3,1},{4,6},{5,7},{6,4},{7,5},{8,10},{9,11},{10,... | collective-permute-start | bytes 4718600 | tf_op jit(solution)/shard_map/ppermute | solution.py:17
  340.8 236.9 %collective-permute-start.9 = (bf16[2,512,768]{2,1,0:T(8,128)(2,1)S(1)}, bf16[2,512,768]{2,1,0:T(8,128)(2,1)S(1)}, u32[]{:S(2)}, u32[]{:S(2)}) collective-permute-start(bf16[2,512,768]{2,1,0:T(8,128)(2,1)S(1)} %copy-done.8), channel_id=1, source_target_pairs={{0,3},{1,2},{2,1},{3,0},{4,7},{5,6},{6,5},{7,4},{8,11},{9,10},{10,... | collective-permute-start | bytes 4718600 | tf_op jit(solution)/shard_map/ppermute | solution.py:17
  341.1 236.6 %collective-permute-start.10 = (bf16[2,512,768]{2,1,0:T(8,128)(2,1)}, bf16[2,512,768]{2,1,0:T(8,128)(2,1)S(1)}, u32[]{:S(2)}, u32[]{:S(2)}) collective-permute-start(bf16[2,512,768]{2,1,0:T(8,128)(2,1)} %pick_output_1_0.1), channel_id=1, source_target_pairs={{0,1},{1,0},{2,3},{3,2},{4,5},{5,4},{6,7},{7,6},{8,9},{9,8},{10,11... | collective-permute-start | bytes 4718600 | tf_op jit(solution)/shard_map/ppermute | solution.py:17
  623.7 136.6 %collective-permute-start.11 = (bf16[2,512,768]{2,1,0:T(8,128)(2,1)}, bf16[2,512,768]{2,1,0:T(8,128)(2,1)S(1)}, u32[]{:S(2)}, u32[]{:S(2)}) collective-permute-start(bf16[2,512,768]{2,1,0:T(8,128)(2,1)} %pick_output_2_3.1), channel_id=1, source_target_pairs={{0,2},{1,3},{2,0},{3,1},{4,6},{5,7},{6,4},{7,5},{8,10},{9,11},{10,... | collective-permute-start | bytes 4718600 | tf_op jit(solution)/shard_map/ppermute | solution.py:17
  664.9 95.4 %collective-permute-start.12 = (bf16[2,512,768]{2,1,0:T(8,128)(2,1)}, bf16[2,512,768]{2,1,0:T(8,128)(2,1)S(1)}, u32[]{:S(2)}, u32[]{:S(2)}) collective-permute-start(bf16[2,512,768]{2,1,0:T(8,128)(2,1)} %pick_output_3_3.1), channel_id=1, source_target_pairs={{0,3},{1,2},{2,1},{3,0},{4,7},{5,6},{6,5},{7,4},{8,11},{9,10},{10,... | collective-permute-start | bytes 4718600 | tf_op jit(solution)/shard_map/ppermute | solution.py:17
  671.4 104.8 %collective-permute-start.13 = (bf16[2,512,768]{2,1,0:T(8,128)(2,1)}, bf16[2,512,768]{2,1,0:T(8,128)(2,1)}, u32[]{:S(2)}, u32[]{:S(2)}) collective-permute-start(bf16[2,512,768]{2,1,0:T(8,128)(2,1)} %pick_output_1_3.1), channel_id=1, source_target_pairs={{0,1},{1,0},{2,3},{3,2},{4,5},{5,4},{6,7},{7,6},{8,9},{9,8},{10,11... | collective-permute-start | bytes 4718600 | tf_op jit(solution)/shard_map/ppermute | solution.py:17
  691.1 131.2 %collective-permute-start.14 = (bf16[2,256,768]{2,1,0:T(8,128)(2,1)}, bf16[2,256,768]{2,1,0:T(8,128)(2,1)S(1)}, u32[]{:S(2)}, u32[]{:S(2)}) collective-permute-start(bf16[2,256,768]{2,1,0:T(8,128)(2,1)} %get-tuple-element.24), channel_id=1, source_target_pairs={{0,1},{1,0},{2,3},{3,2},{4,5},{5,4},{6,7},{7,6},{8,9},{9,8},{10,11... | collective-permute-start | bytes 2359304 | tf_op jit(solution)/shard_map/ppermute | solution.py:17
  789.9 92.7 %collective-permute-start.22 = (bf16[2,256,768]{2,1,0:T(8,128)(2,1)}, bf16[2,256,768]{2,1,0:T(8,128)(2,1)S(1)}, u32[]{:S(2)}, u32[]{:S(2)}) collective-permute-start(bf16[2,256,768]{2,1,0:T(8,128)(2,1)} %get-tuple-element.29), channel_id=1, source_target_pairs={{0,1},{1,0},{2,3},{3,2},{4,5},{5,4},{6,7},{7,6},{8,9},{9,8},{10,11... | collective-permute-start | bytes 2359304 | tf_op jit(solution)/shard_map/ppermute | solution.py:17
  812.1 38.1 %collective-permute-start.19 = (bf16[2,512,256]{2,1,0:T(8,128)(2,1)}, bf16[2,512,256]{2,1,0:T(8,128)(2,1)S(1)}, u32[]{:S(2)}, u32[]{:S(2)}) collective-permute-start(bf16[2,512,256]{2,1,0:T(8,128)(2,1)} %pick_output_1_6.1), channel_id=1, source_target_pairs={{0,1},{1,0},{2,3},{3,2},{4,5},{5,4},{6,7},{7,6},{8,9},{9,8},{10,11... | collective-permute-start | bytes 1572872 | tf_op jit(solution)/shard_map/ppermute | solution.py:17
  815.1 35.2 %collective-permute-start.20 = (bf16[2,512,256]{2,1,0:T(8,128)(2,1)}, bf16[2,512,256]{2,1,0:T(8,128)(2,1)S(1)}, u32[]{:S(2)}, u32[]{:S(2)}) collective-permute-start(bf16[2,512,256]{2,1,0:T(8,128)(2,1)} %pick_output_2_6.1), channel_id=1, source_target_pairs={{0,2},{1,3},{2,0},{3,1},{4,6},{5,7},{6,4},{7,5},{8,10},{9,11},{10,... | collective-permute-start | bytes 1572872 | tf_op jit(solution)/shard_map/ppermute | solution.py:17
  819.1 43.1 %collective-permute-start.21 = (bf16[2,512,256]{2,1,0:T(8,128)(2,1)}, bf16[2,512,256]{2,1,0:T(8,128)(2,1)S(1)}, u32[]{:S(2)}, u32[]{:S(2)}) collective-permute-start(bf16[2,512,256]{2,1,0:T(8,128)(2,1)} %pick_output_3_6.1), channel_id=1, source_target_pairs={{0,3},{1,2},{2,1},{3,0},{4,7},{5,6},{6,5},{7,4},{8,11},{9,10},{10,... | collective-permute-start | bytes 1572872 | tf_op jit(solution)/shard_map/ppermute | solution.py:17
  822.6 60.3 %collective-permute-start.15 = (bf16[1,256,768]{2,1,0:T(8,128)(2,1)S(1)}, bf16[1,256,768]{2,1,0:T(8,128)(2,1)S(1)}, u32[]{:S(2)}, u32[]{:S(2)}) collective-permute-start(bf16[1,256,768]{2,1,0:T(8,128)(2,1)S(1)} %slice.56), channel_id=1, source_target_pairs={{0,2},{1,3},{2,0},{3,1},{4,6},{5,7},{6,4},{7,5},{8,10},{9,11},{10,... | collective-permute-start | bytes 1179656 | tf_op jit(solution)/shard_map/ppermute | solution.py:17
  871.1 28.7 %collective-permute-start.24 = (bf16[2,256,256]{2,1,0:T(8,128)(2,1)}, bf16[2,256,256]{2,1,0:T(8,128)(2,1)S(1)}, u32[]{:S(2)}, u32[]{:S(2)}) collective-permute-start(bf16[2,256,256]{2,1,0:T(8,128)(2,1)} %get-tuple-element.31), channel_id=1, source_target_pairs={{0,1},{1,0},{2,3},{3,2},{4,5},{5,4},{6,7},{7,6},{8,9},{9,8},{10,11... | collective-permute-start | bytes 786440 | tf_op jit(solution)/shard_map/ppermute | solution.py:17
  882.8 19.0 %collective-permute-start.23 = (bf16[1,256,768]{2,1,0:T(8,128)(2,1)S(1)}, bf16[1,256,768]{2,1,0:T(8,128)(2,1)S(1)}, u32[]{:S(2)}, u32[]{:S(2)}) collective-permute-start(bf16[1,256,768]{2,1,0:T(8,128)(2,1)S(1)} %slice.58), channel_id=1, source_target_pairs={{0,2},{1,3},{2,0},{3,1},{4,6},{5,7},{6,4},{7,5},{8,10},{9,11},{10,... | collective-permute-start | bytes 1179656 | tf_op jit(solution)/shard_map/ppermute | solution.py:17
  886.7 26.0 %collective-permute-start.16 = (bf16[2,512,256]{2,1,0:T(8,128)(2,1)}, bf16[2,512,256]{2,1,0:T(8,128)(2,1)S(1)}, u32[]{:S(2)}, u32[]{:S(2)}) collective-permute-start(bf16[2,512,256]{2,1,0:T(8,128)(2,1)} %pick_output_1_7.1), channel_id=1, source_target_pairs={{0,1},{1,0},{2,3},{3,2},{4,5},{5,4},{6,7},{7,6},{8,9},{9,8},{10,11... | collective-permute-start | bytes 1572872 | tf_op jit(solution)/shard_map/ppermute | solution.py:17
  891.6 43.9 %collective-permute-start.17 = (bf16[2,512,256]{2,1,0:T(8,128)(2,1)}, bf16[2,512,256]{2,1,0:T(8,128)(2,1)S(1)}, u32[]{:S(2)}, u32[]{:S(2)}) collective-permute-start(bf16[2,512,256]{2,1,0:T(8,128)(2,1)} %pick_output_2_7.1), channel_id=1, source_target_pairs={{0,2},{1,3},{2,0},{3,1},{4,6},{5,7},{6,4},{7,5},{8,10},{9,11},{10,... | collective-permute-start | bytes 1572872 | tf_op jit(solution)/shard_map/ppermute | solution.py:17
  895.4 40.0 %collective-permute-start.18 = (bf16[2,512,256]{2,1,0:T(8,128)(2,1)}, bf16[2,512,256]{2,1,0:T(8,128)(2,1)S(1)}, u32[]{:S(2)}, u32[]{:S(2)}) collective-permute-start(bf16[2,512,256]{2,1,0:T(8,128)(2,1)} %pick_output_3_7.1), channel_id=1, source_target_pairs={{0,3},{1,2},{2,1},{3,0},{4,7},{5,6},{6,5},{7,4},{8,11},{9,10},{10,... | collective-permute-start | bytes 1572872 | tf_op jit(solution)/shard_map/ppermute | solution.py:17
  944.6 18.2 %collective-permute-start.26 = (bf16[2,256,256]{2,1,0:T(8,128)(2,1)}, bf16[2,256,256]{2,1,0:T(8,128)(2,1)S(1)}, u32[]{:S(2)}, u32[]{:S(2)}) collective-permute-start(bf16[2,256,256]{2,1,0:T(8,128)(2,1)} %get-tuple-element.35), channel_id=1, source_target_pairs={{0,1},{1,0},{2,3},{3,2},{4,5},{5,4},{6,7},{7,6},{8,9},{9,8},{10,11... | collective-permute-start | bytes 786440 | tf_op jit(solution)/shard_map/ppermute | solution.py:17
  954.7 9.2 collective-permute-start.25
  963.9 7.1 collective-permute-start.27
  (20 other events, 205.3 us)
Sparse Core Ops, SparseCore 0:
  48.7 133.0 all-gather.2
  183.7 123.0 all-gather.4
  617.8 109.3 reduce-scatter.1

commit v2 on v1

v2 whole, which is shorter than its diff:
```python
import functools

import jax
import jax.numpy as jnp
from jax import lax
from jax.experimental import pallas as pl
from jax.experimental.pallas import tpu as pltpu
from jax.sharding import PartitionSpec as P

adapter_scale_factor = 2.0
f32, bf16 = jnp.float32, jnp.bfloat16
PARAMS = dict(vmem_limit_bytes=56 * 1024 * 1024)


def total_over(axis, send, keep):
    n = lax.axis_size(axis)
    for b in range(n.bit_length() - 1):
        total = (keep.astype(f32) + swap(send, axis, 1 << b).astype(f32)).astype(bf16)
        send, keep = total[1::2], total[0::2]
    return keep[0]


def swap(x, axis, mask):
    n = lax.axis_size(axis)
    return lax.ppermute(x, axis, [(i, i ^ mask) for i in range(n)])


def flipped(value, bits):
    out = 0
    for b in range(bits):
        out = out | (((value >> b) & 1) << (bits - 1 - b))
    return out


def cost(flops, us):
    return pl.CostEstimate(flops=int(us * 1e9), bytes_accessed=0, transcendentals=0)


EST = dict(
    pack_key_value=1,
    stack_factors=1,
    split_columns=1,
    pick_output=1,
    place_qkv=1,
    place_output=200,
    pick_query=1,
    pick_query_last=300,
)
ANY = pl.BlockSpec(memory_space=pl.ANY)
VMEM = pl.BlockSpec(memory_space=pltpu.VMEM)


def merged_t(base, down_t, up):
    update = lax.dot_general(down_t, up, (((0,), (0,)), ((), ())), preferred_element_type=f32)
    return (base.astype(f32) + adapter_scale_factor * update).astype(bf16)


def call(kernel, grid, in_specs, out_specs, out_shape, name, us, scratch=(), alias={}):
    return pl.pallas_call(
        kernel,
        grid_spec=pltpu.PrefetchScalarGridSpec(
            num_scalar_prefetch=1,
            grid=grid,
            in_specs=in_specs,
            out_specs=out_specs,
            scratch_shapes=scratch,
        ),
        out_shape=out_shape,
        input_output_aliases=alias,
        compiler_params=pltpu.CompilerParams(**PARAMS),
        cost_estimate=cost(0, us),
        name=name,
    )


def group_of(s, j, i, per):
    return i[1 + (i[0] ^ s) * per + j]


def pack_key_value(info, key_w, value_w, key_dt, value_dt, key_u, value_u, nt, per):
    rb, width = key_w.shape
    hd = width // (nt * per)

    def kernel(info_ref, kw, vw, kd, vd, ku, vu, *refs):
        outs, (mk, mv) = refs[:nt], refs[nt:]
        mk[...] = merged_t(kw[...], kd[...], ku[...])
        mv[...] = merged_t(vw[...], vd[...], vu[...])
        for s in range(nt):
            for j in range(per):
                at = pl.ds(pl.multiple_of(group_of(s, j, info_ref, per) * hd, hd), hd)
                outs[s][:, (2 * j) * hd : (2 * j + 1) * hd] = mk[:, at]
                outs[s][:, (2 * j + 1) * hd : (2 * j + 2) * hd] = mv[:, at]

    return call(
        kernel,
        (),
        [VMEM] * 6,
        [VMEM] * nt,
        [jax.ShapeDtypeStruct((rb, per * 2 * hd), bf16)] * nt,
        "pack_key_value",
        EST["pack_key_value"],
        [pltpu.VMEM((rb, width), bf16)] * 2,
    )(info, key_w, value_w, key_dt, value_dt, key_u, value_u)


def pick_query(info, query_w, s, j, groups, per, us, after):
    rb, width = query_w.shape
    cols = width // groups
    steps = 4

    def kernel(info_ref, q, *refs):
        refs[-1][...] = q[...]

    return call(
        kernel,
        (steps,),
        [pl.BlockSpec((rb // steps, cols), lambda r, i: (r, group_of(s, j, i, per)))]
        + [ANY] * len(after),
        pl.BlockSpec((rb // steps, cols), lambda r, i: (r, 0)),
        jax.ShapeDtypeStruct((rb, cols), bf16),
        f"pick_query_{s}_{j}",
        us,
    )(info, query_w, *after)


def stack_factors(info, arrays, after):
    def kernel(info_ref, *refs):
        for n in range(len(arrays)):
            refs[-1][0, n] = refs[n][...]

    shape = (1, len(arrays), *arrays[0].shape)
    return call(
        kernel,
        (),
        [VMEM] * len(arrays) + [ANY] * len(after),
        VMEM,
        jax.ShapeDtypeStruct(shape, bf16),
        "stack_factors",
        EST["stack_factors"],
    )(info, *arrays, *after)


def folds(rank, rb, wide):
    return min(wide // rb, rank // 16)


def split_columns(info, weight, tokens, down_t, nd):
    rb, width = weight.shape
    more = tokens.shape[0]
    rank = down_t.shape[0]
    wide = width // nd
    parts = folds(rank, rb, wide)
    few = rank // parts
    rows = rb + more + few

    def kernel(info_ref, w, t, d, out):
        out[0, :rb, :] = w[...]
        out[0, rb : rb + more, :] = t[...]
        for p in range(parts):
            out[0, rb + more :, p * rb : (p + 1) * rb] = d[p * few : (p + 1) * few, :]

    return call(
        kernel,
        (nd,),
        [
            pl.BlockSpec((rb, wide), lambda d, i: (0, d)),
            pl.BlockSpec((more, wide), lambda d, i: (0, d)),
            pl.BlockSpec((rank, rb), lambda d, i: (0, 0)),
        ],
        pl.BlockSpec((1, rows, wide), lambda d, i: (d, 0, 0)),
        jax.ShapeDtypeStruct((nd, rows, wide), bf16),
        "split_columns",
        EST["split_columns"],
    )(info, weight, tokens, down_t)


def pick_output(info, blocks, rb, ups, s, first, count, tile, per, dpg, after):
    parts = per * dpg
    nt, rank, cb = ups.shape
    bits = nt.bit_length() - 1
    width = count * tile
    piece = min(tile, cb)
    pieces = width // piece
    steps = 2
    some = rb // steps if rb // steps % 128 == 0 else rb
    steps = rb // some
    wide = blocks.shape[2]
    parted = folds(rank, rb, wide)
    few = rank // parted
    below = blocks.shape[1] // few - 1

    def kernel(info_ref, x, *rest):
        d, up = rest[:parted], rest[parted : parted + pieces]
        down_t = jnp.concatenate([y[0] for y in d], axis=0)
        rest[-1][0] = merged_t(x[0], down_t, jnp.concatenate([u[0] for u in up], axis=1))

    def down_at(p, l, r, i):
        return (source(l, i), below, p * steps + r)

    def source(l, i):
        return group_of(s, l // dpg, i, per) * dpg + l % dpg

    def up_at(p, l, r, i):
        at = first * tile + p * piece
        return (flipped((at // cb) ^ i[0], bits), 0, at % cb // piece)

    return call(
        kernel,
        (parts, steps),
        [
            pl.BlockSpec((1, some, width), lambda l, r, i: (source(l, i), r, first // count)),
        ]
        + [pl.BlockSpec((1, few, some), functools.partial(down_at, p)) for p in range(parted)]
        + [pl.BlockSpec((1, rank, piece), functools.partial(up_at, p)) for p in range(pieces)]
        + [ANY] * len(after),
        pl.BlockSpec((1, some, width), lambda l, r, i: (l, r, 0)),
        jax.ShapeDtypeStruct((parts, rb, width), bf16),
        f"pick_output_{s}_{first}",
        EST["pick_output"],
    )(info, blocks, *[blocks] * parted, *[ups] * pieces, *after)


def place_qkv(info, blocks, hidden_rows, query, keyval, downs, factors, per, nd, after):
    nt, rank, cb = downs.shape
    rb, gq = query[0][0].shape
    bits = nt.bit_length() - 1
    sources, _, depth = blocks.shape
    some = hidden_rows
    count = sources * some
    tile = keyval[0].shape[1] // per
    wide = gq // tile
    each = wide + 1
    cols = per * each * tile
    piece = min(tile, cb)
    pieces = tile // piece

    def kernel(info_ref, a, d, *refs):
        u, refs = refs[:pieces], refs[pieces:]
        full, send, keep, term = refs[-4:]
        place = pl.program_id(0) // each
        last = lax.rem(pl.program_id(0), each) == wide

        def put(blocks):
            total = jnp.zeros((count, tile), f32)
            for s in range(nt):
                at = pl.ds(pl.multiple_of((info_ref[0] ^ s) * rb, rb), rb)
                full[at, :] = blocks[s]
                rows = a[:, :, at].reshape(count, rb)
                total += jnp.dot(rows, blocks[s], preferred_element_type=f32)
            term[...] = total.astype(bf16)
            for s in range(nd):
                at = pl.ds(pl.multiple_of((info_ref[info_ref.shape[0] - 1] ^ s) * some, some), some)
                (send if s % 2 else keep)[s // 2] = term[at, :]

        for j in range(per):
            q = refs[j * nt : (j + 1) * nt]

            @pl.when(jnp.logical_and(place == j, jnp.logical_not(last)))
            def _():
                up = jnp.concatenate([x[...] for x in u], axis=1)
                put([merged_t(q[s][...], d[flipped(s, bits)], up) for s in range(nt)])

        @pl.when(last)
        def _():
            put([x[...] for x in refs[per * nt : (per + 1) * nt]])

    def column(j, n, i):
        k, w = n // each, jnp.minimum(n % each, wide - 1)
        return (0, jnp.where(k == j, w, jnp.where(k < j, 0, wide - 1)))

    def up_at(p, n, i):
        at = group_of(0, n // each, i, per) * gq + jnp.minimum(n % each, wide - 1) * tile
        block = at // cb + p
        return (block // nt * nt + flipped((block % nt) ^ i[0], bits), at % cb // piece)

    half = jax.ShapeDtypeStruct((nd // 2, count // nd, cols), bf16)
    half_spec = pl.BlockSpec((nd // 2, count // nd, tile), lambda n, i: (0, 0, n))
    return call(
        kernel,
        (per * each,),
        [
            pl.BlockSpec((sources, some, depth), lambda n, i: (0, rb // some, 0)),
            pl.BlockSpec(downs.shape, lambda n, i: (0, 0, 0)),
        ]
        + [pl.BlockSpec((rank, piece), functools.partial(up_at, p)) for p in range(pieces)]
        + [
            pl.BlockSpec((rb, tile), functools.partial(column, j))
            for j in range(per)
            for _ in range(nt)
        ]
        + [pl.BlockSpec((rb, tile), lambda n, i: (0, n // each))] * nt
        + [ANY] * len(after),
        [
            pl.BlockSpec((nt * rb, tile), lambda n, i: (0, n)),
            half_spec,
            half_spec,
        ],
        [jax.ShapeDtypeStruct((nt * rb, cols), bf16), half, half],
        "place_qkv",
        EST["place_qkv"],
        [pltpu.VMEM((count, tile), bf16)],
    )(info, blocks, downs, *[factors] * pieces, *[x for at in query for x in at], *keyval, *after)


def place_output(info, tokens, arrived, before, first, tile, cols, nt, after):
    parts, rb, width = arrived[0].shape
    rows, depth = tokens.shape
    each = rows // nt

    def kernel(info_ref, a, *refs):
        full, send, keep, term = refs[-4:]
        total = jnp.zeros((rows, tile), f32)
        for s in range(nt):
            for l in range(parts):
                at = pl.ds(pl.multiple_of((l * nt + (info_ref[0] ^ s)) * rb, rb), rb)
                x = refs[s][l]
                full[at, :] = x
                total += jnp.dot(a[:, at], x, preferred_element_type=f32)
        term[...] = total.astype(bf16)
        for s in range(nt):
            at = pl.ds(pl.multiple_of((info_ref[0] ^ s) * each, each), each)
            (send if s % 2 else keep)[s // 2] = term[at, :]

    operands = [info, tokens, *arrived]
    alias = {}
    if before is not None:
        alias = {len(operands): 0}
        after = [before, *after]
    half = jax.ShapeDtypeStruct((nt // 2, each, width), bf16)
    half_spec = pl.BlockSpec((nt // 2, each, tile), lambda c, i: (0, 0, c))
    return call(
        kernel,
        (width // tile,),
        [pl.BlockSpec((rows, depth), lambda c, i: (0, 0))]
        + [pl.BlockSpec((parts, rb, tile), lambda c, i: (0, 0, c))] * nt
        + [ANY] * len(after),
        [
            pl.BlockSpec((depth, tile), lambda c, i: (0, first + c)),
            half_spec,
            half_spec,
        ],
        [jax.ShapeDtypeStruct((depth, cols), bf16), half, half],
        f"place_output_{first}",
        EST["place_output"],
        [pltpu.VMEM((rows, tile), bf16)],
        alias,
    )(*operands, *after)


def body(
    hidden,
    context,
    query_weight,
    key_projection_rows,
    value_weight,
    query_lower_factor,
    key_down,
    value_down,
    query_up,
    key_up,
    value_up,
    output_weight,
    output_down,
    output_up,
    slice_group,
):
    groups = slice_group.shape[0]
    nt, nd = lax.axis_size("tensor"), lax.axis_size("dp")
    bits = nt.bit_length() - 1
    per, dpg = groups // nt, nd // groups
    rank, cb = query_up.shape
    place = [lax.axis_index(axis).astype(jnp.int32)[None] for axis in ("tensor", "dp")]
    info = jnp.concatenate((place[0], slice_group, place[1]))

    order = list(range(nt // 2, nt)) + list(range(1, nt // 2)) + [0]

    def exchange(sent):
        return {s: swap(x, "tensor", s) if s else x for s, x in sent.items()}

    keyval = pack_key_value(
        info, key_projection_rows, value_weight, key_down.T, value_down.T, key_up, value_up, nt, per
    )
    got = exchange({s: keyval[s] for s in order})
    keyval = [got[s] for s in range(nt)]
    outgoing = split_columns(info, output_weight, hidden, output_down.T, nd)
    blocks = lax.all_to_all(outgoing, "dp", split_axis=0, concat_axis=0, tiled=True)

    query = []
    for j in range(per):
        sent = {}
        for s in order:
            late = j == 0 and s == 1
            us = EST["pick_query_last" if late else "pick_query"]
            after = keyval[1:] if late else []
            sent[s] = pick_query(info, query_weight, s, j, groups, per, us, after)
        got = exchange(sent)
        query.append([got[s] for s in range(nt)])

    factors = stack_factors(info, (query_up, output_up, query_lower_factor.T), [])
    for b in reversed(range(bits)):
        factors = jnp.concatenate((factors, swap(factors, "tensor", 1 << b)))
    output_ups, query_downs = factors[:, 1], factors[:, 2]
    query_ups = lax.all_gather(factors[:, 0].reshape(nt * rank, cb), "dp", axis=0, tiled=True)

    context_all = lax.all_gather(context, "dp", axis=0, tiled=True)

    cols = blocks.shape[2]
    tile = cols // 8
    chunks = ((0, 3), (3, 3), (6, 1), (7, 1))
    merged_output = None
    sums, done = [], []
    for n, (first, count) in enumerate(chunks):
        last = n == len(chunks) - 1
        after = done[n - 2] if n >= 2 else []
        sent = {
            s: pick_output(
                info, blocks, output_weight.shape[0], output_ups, s, first, count, tile, per, dpg, after if s else []
            )
            for s in order
        }
        got = exchange(sent)
        done.append([got[s] for s in order if s])
        if n == 0:
            merged_qkv, *partial = place_qkv(
                info, blocks, hidden.shape[0], query, keyval, query_downs, query_ups, per, nd, done[0]
            )
            projections = total_over("dp", *partial)
        merged_output, send, keep = place_output(
            info, context_all, [got[s] for s in range(nt)], merged_output, first, tile, cols, nt,
            partial[:1] if n == 1 else sums[:-1] + [projections] if last else [],
        )
        sums.append(total_over("tensor", send, keep))
    attention_output = jnp.concatenate(sums, axis=1)
    return (merged_qkv, merged_output, projections, attention_output)


def solution(mesh):
    rows = P(("dp", "tensor"), None)
    ups = P(None, ("dp", "tensor"))
    placed = (
        P("dp", None),
        P("dp", "tensor"),
        rows,
        rows,
        rows,
        rows,
        rows,
        rows,
        ups,
        P(),
        P(),
        rows,
        rows,
        ups,
        P(),
    )
    return jax.shard_map(
        body,
        mesh=mesh,
        in_specs=placed,
        out_specs=(P("dp", "tensor"), P("tensor", "dp"), P("dp", "tensor"), P("tensor", "dp")),
        check_vma=False,
    )
```

time: 981 us -> 916 us (0.934)
  starting transfers between devices: 215 us -> 105 us
  waiting for transfers between devices: 509 us -> 546 us
  other arithmetic: 8.14 us -> 22.6 us
  Pallas kernels: 227 us -> 216 us
    ppermute x28 -> x34, waiting for transfers between devices: 348 us -> 527 us  [swap(): return lax.ppermute(x, axis, [(i, i ^ mask) for i in range(n)])]
    all_to_all x1, waiting for transfers between devices: 137 us -> 19.5 us  [body(): lax.all_to_all(outgoing, 'dp', split_axis=0, concat_axis=0, tiled=True)]
    ppermute x28 -> x34, starting transfers between devices: 209 us -> 98.6 us  [swap(): return lax.ppermute(x, axis, [(i, i ^ mask) for i in range(n)])]
    all_gather x1, waiting for transfers between devices: 23.2 us -> 0.01 us  [body(): lax.all_gather(factors[:, 0].reshape(nt * rank, cb), 'dp', axis=0, tiled=...]
    pallas_call x26 -> x27, Pallas kernels: 146 us -> 133 us  [the longest x16 74 us: pick_output(): call(kernel, (parts, steps), [pl.BlockSpec((1, some, width), lambda l, r,...]
  transfers between devices with their start and end apart: 32 -> 37, of which waited for: 15 -> 13; matrix products, arithmetic and copies ran while one was open for 1% -> 2% of each run, Pallas kernels for 23% -> 23%
where the time goes in v2:
time: 916 us; the launch traced here: 913 us
  waiting for transfers between devices  546 us (60%)
  Pallas kernels  216 us (24%)
  starting transfers between devices  105 us (11%)
  other arithmetic  22.6 us (2%)
  between operations  14.4 us (2%)
    ppermute x34, waiting for transfers between devices, swap(): return lax.ppermute(x, axis, [(i, i ^ mask) for i in range(n)])  527 us
    ppermute x34, starting transfers between devices, swap(): return lax.ppermute(x, axis, [(i, i ^ mask) for i in range(n)])  98.6 us
    pallas_call x16, Pallas kernels, pick_output(): call(kernel, (parts, steps), [pl.BlockSpec((1, some, width), lambda l, r,...  74 us
    pallas_call x4, Pallas kernels, place_output(): call(kernel, (width // tile,), [pl.BlockSpec((rows, depth), lambda c, i:...  43.5 us
    pallas_call x1, Pallas kernels, place_qkv(): call(kernel, (per * each,), [pl.BlockSpec((sources, some, depth), lambda...  39.2 us
    pallas_call x8, Pallas kernels, pick_query(): call(kernel, (steps,), [pl.BlockSpec((rb // steps, cols), lambda r, i: (r...  35.8 us
    all_to_all x1, waiting for transfers between devices, body(): lax.all_to_all(outgoing, 'dp', split_axis=0, concat_axis=0, tiled=True)  19.5 us
  transfers between devices with their start and end apart: 37, of which 13 were waited for; matrix products, arithmetic and copies ran while one was open for 2% of the time, Pallas kernels for 23%

profile of v2, /device:TPU:0, one launch (start us, length us, event | category | flops | bytes accessed | tf_op | source)
XLA Modules:
  0.0 913.4 jit_solution(17820350117008984117)
XLA Ops:
  14.8 9.3 %collective-permute-done = bf16[1,3,64,512]{3,2,0,1:T(8,128)(2,1)S(1)} collective-permute-done((bf16[1,3,64,512]{3,2,0,1:T(8,128)(2,1)}, bf16[1,3,64,512]{3,2,0,1:T(8,128)(2,1)S(1)}, u32[]{:S(2)}, u32[]{:S(2)}) %collective-permute-start) | collective-permute-done | bytes 196640 | tf_op jit(solution)/shard_map/ppermute | solution.py:25
  25.9 9.5 %collective-permute-done.1 = bf16[2,3,64,512]{3,2,0,1:T(8,128)(2,1)S(1)} collective-permute-done((bf16[2,3,64,512]{3,2,0,1:T(8,128)(2,1)S(1)}, bf16[2,3,64,512]{3,2,0,1:T(8,128)(2,1)S(1)}, u32[]{:S(2)}, u32[]{:S(2)}) %collective-permute-start.1) | collective-permute-done | bytes 393248 | tf_op jit(solution)/shard_map/ppermute | solution.py:25
  46.7 16.8 %split_columns.1 = bf16[8,656,2048]{2,1,0:T(8,128)(2,1)} custom-call(s32[10]{0:T(128)} %pad_add_fusion.info_ref, bf16[512,16384]{1,0:T(8,128)(2,1)} %w.1, bf16[128,16384]{1,0:T(8,128)(2,1)} %t.1, bf16[64,512]{1,0:T(8,128)(2,1)} %bitcast.28), custom_call_target="tpu_custom_call" | custom-call | flops 1000000000 | tf_op jit(solution)/shard_map/split_columns/pallas_call | solution.py:162
  63.6 6.1 all-to-all-start
  96.7 75.4 %collective-permute-done.3.refs_1_.refs_11_ = bf16[512,512]{1,0:T(8,128)(2,1)S(1)} collective-permute-done((bf16[512,512]{1,0:T(8,128)(2,1)}, bf16[512,512]{1,0:T(8,128)(2,1)S(1)}, u32[]{:S(2)}, u32[]{:S(2)}) %collective-permute-start.3) | collective-permute-done | bytes 524320 | tf_op jit(solution)/shard_map/ppermute | solution.py:25
  179.4 139.0 %collective-permute-done.6.refs_3_ = bf16[512,2048]{1,0:T(8,128)(2,1)} collective-permute-done((bf16[512,2048]{1,0:T(8,128)(2,1)}, bf16[512,2048]{1,0:T(8,128)(2,1)}, u32[]{:S(2)}, u32[]{:S(2)}) %collective-permute-start.6) | collective-permute-done | bytes 2097184 | tf_op jit(solution)/shard_map/ppermute | solution.py:25
  318.4 19.5 %all-to-all-done.x.rest_0_.rest_1_.rest_2_.rest_3_.a = bf16[8,656,2048]{2,1,0:T(8,128)(2,1)} async-done(((bf16[8,656,2048]{2,1,0:T(8,128)(2,1)}), bf16[8,656,2048]{2,1,0:T(8,128)(2,1)}, u32[]{:S(2)}, u32[]{:S(2)}) %all-to-all-start) | async-done | bytes 21495840 | tf_op jit(solution)/shard_map/all_to_all | solution.py:386
  337.9 4.9 pick_output_2_0.1
  342.8 4.9 pick_output_3_0.1
  347.7 4.8 pick_output_1_0.1
  352.5 12.5 %collective-permute-start.11 = (bf16[2,512,768]{2,1,0:T(8,128)(2,1)}, bf16[2,512,768]{2,1,0:T(8,128)(2,1)}, u32[]{:S(2)}, u32[]{:S(2)}) collective-permute-start(bf16[2,512,768]{2,1,0:T(8,128)(2,1)} %pick_output_2_0.1), channel_id=1, source_target_pairs={{0,2},{1,3},{2,0},{3,1},{4,6},{5,7},{6,4},{7,5},{8,10},{9,11},{10,... | collective-permute-start | bytes 4718600 | tf_op jit(solution)/shard_map/ppermute | solution.py:25
  366.3 109.4 %collective-permute-done.9.refs_7_ = bf16[512,2048]{1,0:T(8,128)(2,1)} collective-permute-done((bf16[512,2048]{1,0:T(8,128)(2,1)}, bf16[512,2048]{1,0:T(8,128)(2,1)}, u32[]{:S(2)}, u32[]{:S(2)}) %collective-permute-start.9) | collective-permute-done | bytes 2097184 | tf_op jit(solution)/shard_map/ppermute | solution.py:25
  488.9 4.9 pick_output_2_3.1
  493.8 4.9 pick_output_3_3.1
  498.7 4.9 pick_output_1_3.1
  507.9 4.8 pick_output_0_3.1.refs_0_
  512.7 4.9 pick_output_0_0.1.refs_0_
  523.5 98.2 %collective-permute-done.11.refs_13_.rest_5_.refs_2_ = bf16[2,512,768]{2,1,0:T(8,128)(2,1)} collective-permute-done((bf16[2,512,768]{2,1,0:T(8,128)(2,1)}, bf16[2,512,768]{2,1,0:T(8,128)(2,1)}, u32[]{:S(2)}, u32[]{:S(2)}) %collective-permute-start.11) | collective-permute-done | bytes 1572896 | tf_op jit(solution)/shard_map/ppermute | solution.py:25
  621.8 39.2 %place_qkv.1 = (bf16[2048,4608]{1,0:T(8,128)(2,1)}, bf16[4,128,4608]{2,1,0:T(8,128)(2,1)}, bf16[4,128,4608]{2,1,0:T(8,128)(2,1)}) custom-call(s32[10]{0:T(128)} %pad_add_fusion.info_ref, bf16[8,656,2048]{2,1,0:T(8,128)(2,1)} %all-to-all-done.x.rest_0_.rest_1_.rest_2_.rest_3_.a, bf16[4,64,512]{2,1,0:T(8,128)(2,1)} %get-tuple-element.44.d, ...), custom_call_target="tpu_custom_call" | custom-call | flops 1000000000 | tf_op jit(solution)/shard_map/place_qkv/pallas_call | solution.py:278
  661.1 13.5 %place_output_0.1 = (bf16[4096,2048]{1,0:T(8,128)(2,1)}, bf16[2,256,768]{2,1,0:T(8,128)(2,1)}, bf16[2,256,768]{2,1,0:T(8,128)(2,1)}) custom-call(s32[10]{0:T(128)} %pad_add_fusion.info_ref, bf16[1024,4096]{1,0:T(8,128)(2,1)} %all-gather.5.cloned.1.call-done.a, bf16[2,512,768]{2,1,0:T(8,128)(2,1)} %pick_output_0_0.1.refs_0_, ...), custom_call_target="tpu_custom_call" | custom-call | flops 199999995904 | tf_op jit(solution)/shard_map/place_output_0/pallas_call | solution.py:331
  674.6 34.2 %collective-permute-start.23 = (bf16[2,256,768]{2,1,0:T(8,128)(2,1)}, bf16[2,256,768]{2,1,0:T(8,128)(2,1)}, u32[]{:S(2)}, u32[]{:S(2)}) collective-permute-start(bf16[2,256,768]{2,1,0:T(8,128)(2,1)} %get-tuple-element.33), channel_id=1, source_target_pairs={{0,1},{1,0},{2,3},{3,2},{4,5},{5,4},{6,7},{7,6},{8,9},{9,8},{10,11... | collective-permute-start | bytes 2359304 | tf_op jit(solution)/shard_map/ppermute | solution.py:25
  708.9 5.0 add_convert_fusion
  718.3 13.5 %place_output_3.1 = (bf16[4096,2048]{1,0:T(8,128)(2,1)}, bf16[2,256,768]{2,1,0:T(8,128)(2,1)}, bf16[2,256,768]{2,1,0:T(8,128)(2,1)}) custom-call(s32[10]{0:T(128)} %pad_add_fusion.info_ref, bf16[1024,4096]{1,0:T(8,128)(2,1)} %all-gather.5.cloned.1.call-done.a, bf16[2,512,768]{2,1,0:T(8,128)(2,1)} %pick_output_0_3.1.refs_0_, ...), custom_call_target="tpu_custom_call", output_to_operand_aliasing={{0}: (6, {})} | custom-call | flops 199999995904 | tf_op jit(solution)/shard_map/place_output_3/pallas_call | solution.py:331
  778.5 17.9 %collective-permute-done.20.refs_1_ = bf16[2,512,256]{2,1,0:T(8,128)(2,1)S(1)} collective-permute-done((bf16[2,512,256]{2,1,0:T(8,128)(2,1)S(1)}, bf16[2,512,256]{2,1,0:T(8,128)(2,1)S(1)}, u32[]{:S(2)}, u32[]{:S(2)}) %collective-permute-start.20) | collective-permute-done | bytes 524320 | tf_op jit(solution)/shard_map/ppermute | solution.py:25
  801.9 11.0 %collective-permute-done.22.refs_3_ = bf16[2,512,256]{2,1,0:T(8,128)(2,1)S(1)} collective-permute-done((bf16[2,512,256]{2,1,0:T(8,128)(2,1)S(1)}, bf16[2,512,256]{2,1,0:T(8,128)(2,1)S(1)}, u32[]{:S(2)}, u32[]{:S(2)}) %collective-permute-start.22) | collective-permute-done | bytes 524320 | tf_op jit(solution)/shard_map/ppermute | solution.py:25
  814.4 8.2 place_output_6.1
  822.6 24.2 %collective-permute-done.24 = bf16[1,256,768]{2,1,0:T(8,128)(2,1)} collective-permute-done((bf16[1,256,768]{2,1,0:T(8,128)(2,1)}, bf16[1,256,768]{2,1,0:T(8,128)(2,1)}, u32[]{:S(2)}, u32[]{:S(2)}) %collective-permute-start.24) | collective-permute-done | bytes 393248 | tf_op jit(solution)/shard_map/ppermute | solution.py:25
  849.7 16.7 %collective-permute-done.26 = bf16[1,256,768]{2,1,0:T(8,128)(2,1)} collective-permute-done((bf16[1,256,768]{2,1,0:T(8,128)(2,1)}, bf16[1,256,768]{2,1,0:T(8,128)(2,1)}, u32[]{:S(2)}, u32[]{:S(2)}) %collective-permute-start.26) | collective-permute-done | bytes 393248 | tf_op jit(solution)/shard_map/ppermute | solution.py:25
  871.7 8.2 place_output_7.1
  879.9 7.2 collective-permute-start.32
  888.2 8.4 collective-permute-done.32
  897.7 7.6 collective-permute-done.33
  (149 shorter events, 149.2 us)
Async XLA Ops:
  7.2 614.6 %all-gather.3.cloned.1.call-start = ((), (), s32[]{:S(2)}) async-start(), calls=%async_computation.1 | async-start | bytes 2359296 | tf_op jit(solution)/shard_map/all_gather | solution.py:403
  41.9 54.3 %collective-permute-start.2 = (bf16[512,512]{1,0:T(8,128)(2,1)}, bf16[512,512]{1,0:T(8,128)(2,1)S(1)}, u32[]{:S(2)}, u32[]{:S(2)}) collective-permute-start(bf16[512,512]{1,0:T(8,128)(2,1)} %get-tuple-element.23), channel_id=1, source_target_pairs={{0,1},{1,0},{2,3},{3,2},{4,5},{5,4},{6,7},{7,6},{8,9},{9,8},{10,11... | collective-permute-start | bytes 1572872 | tf_op jit(solution)/shard_map/ppermute | solution.py:25
  43.5 128.7 %collective-permute-start.3 = (bf16[512,512]{1,0:T(8,128)(2,1)}, bf16[512,512]{1,0:T(8,128)(2,1)S(1)}, u32[]{:S(2)}, u32[]{:S(2)}) collective-permute-start(bf16[512,512]{1,0:T(8,128)(2,1)} %get-tuple-element.24), channel_id=1, source_target_pairs={{0,2},{1,3},{2,0},{3,1},{4,6},{5,7},{6,4},{7,5},{8,10},{9,11},{10,... | collective-permute-start | bytes 1572872 | tf_op jit(solution)/shard_map/ppermute | solution.py:25
  46.7 125.5 %collective-permute-start.4 = (bf16[512,512]{1,0:T(8,128)(2,1)}, bf16[512,512]{1,0:T(8,128)(2,1)S(1)}, u32[]{:S(2)}, u32[]{:S(2)}) collective-permute-start(bf16[512,512]{1,0:T(8,128)(2,1)} %get-tuple-element.25), channel_id=1, source_target_pairs={{0,3},{1,2},{2,1},{3,0},{4,7},{5,6},{6,5},{7,4},{8,11},{9,10},{10,... | collective-permute-start | bytes 1572872 | tf_op jit(solution)/shard_map/ppermute | solution.py:25
  63.6 274.4 %all-to-all-start = ((bf16[8,656,2048]{2,1,0:T(8,128)(2,1)}), bf16[8,656,2048]{2,1,0:T(8,128)(2,1)}, u32[]{:S(2)}, u32[]{:S(2)}) async-start(bf16[8,656,2048]{2,1,0:T(8,128)(2,1)} %split_columns.1), calls=%async_computation | async-start | bytes 42991616 | tf_op jit(solution)/shard_map/all_to_all | solution.py:386
  69.7 591.4 %all-gather.5.cloned.1.call-start = ((), (), s32[]{:S(2)}) async-start(), calls=%async_computation.2 | async-start | bytes 9437184 | tf_op jit(solution)/shard_map/all_gather | solution.py:405
  74.4 244.0 %collective-permute-start.6 = (bf16[512,2048]{1,0:T(8,128)(2,1)}, bf16[512,2048]{1,0:T(8,128)(2,1)}, u32[]{:S(2)}, u32[]{:S(2)}) collective-permute-start(bf16[512,2048]{1,0:T(8,128)(2,1)} %pick_query_2_0.1), channel_id=1, source_target_pairs={{0,2},{1,3},{2,0},{3,1},{4,6},{5,7},{6,4},{7,5},{8,10},{9,11},{10,... | collective-permute-start | bytes 6291464 | tf_op jit(solution)/shard_map/ppermute | solution.py:25
  80.7 271.8 %collective-permute-start.7 = (bf16[512,2048]{1,0:T(8,128)(2,1)}, bf16[512,2048]{1,0:T(8,128)(2,1)}, u32[]{:S(2)}, u32[]{:S(2)}) collective-permute-start(bf16[512,2048]{1,0:T(8,128)(2,1)} %pick_query_3_0.1), channel_id=1, source_target_pairs={{0,3},{1,2},{2,1},{3,0},{4,7},{5,6},{6,5},{7,4},{8,11},{9,10},{10,... | collective-permute-start | bytes 6291464 | tf_op jit(solution)/shard_map/ppermute | solution.py:25
  96.2 268.9 %collective-permute-start.8 = (bf16[512,2048]{1,0:T(8,128)(2,1)}, bf16[512,2048]{1,0:T(8,128)(2,1)}, u32[]{:S(2)}, u32[]{:S(2)}) collective-permute-start(bf16[512,2048]{1,0:T(8,128)(2,1)} %pick_query_1_1.1), channel_id=1, source_target_pairs={{0,1},{1,0},{2,3},{3,2},{4,5},{5,4},{6,7},{7,6},{8,9},{9,8},{10,11... | collective-permute-start | bytes 6291464 | tf_op jit(solution)/shard_map/ppermute | solution.py:25
  172.2 303.5 %collective-permute-start.9 = (bf16[512,2048]{1,0:T(8,128)(2,1)}, bf16[512,2048]{1,0:T(8,128)(2,1)}, u32[]{:S(2)}, u32[]{:S(2)}) collective-permute-start(bf16[512,2048]{1,0:T(8,128)(2,1)} %pick_query_2_1.1), channel_id=1, source_target_pairs={{0,2},{1,3},{2,0},{3,1},{4,6},{5,7},{6,4},{7,5},{8,10},{9,11},{10,... | collective-permute-start | bytes 6291464 | tf_op jit(solution)/shard_map/ppermute | solution.py:25
  172.2 345.4 %collective-permute-start.10 = (bf16[512,2048]{1,0:T(8,128)(2,1)}, bf16[512,2048]{1,0:T(8,128)(2,1)}, u32[]{:S(2)}, u32[]{:S(2)}) collective-permute-start(bf16[512,2048]{1,0:T(8,128)(2,1)} %pick_query_3_1.1), channel_id=1, source_target_pairs={{0,3},{1,2},{2,1},{3,0},{4,7},{5,6},{6,5},{7,4},{8,11},{9,10},{10,... | collective-permute-start | bytes 6291464 | tf_op jit(solution)/shard_map/ppermute | solution.py:25
  318.4 204.0 %collective-permute-start.5 = (bf16[512,2048]{1,0:T(8,128)(2,1)}, bf16[512,2048]{1,0:T(8,128)(2,1)}, u32[]{:S(2)}, u32[]{:S(2)}) collective-permute-start(bf16[512,2048]{1,0:T(8,128)(2,1)} %pick_query_1_0.1), channel_id=1, source_target_pairs={{0,1},{1,0},{2,3},{3,2},{4,5},{5,4},{6,7},{7,6},{8,9},{9,8},{10,11... | collective-permute-start | bytes 6291464 | tf_op jit(solution)/shard_map/ppermute | solution.py:25
  352.5 269.2 %collective-permute-start.11 = (bf16[2,512,768]{2,1,0:T(8,128)(2,1)}, bf16[2,512,768]{2,1,0:T(8,128)(2,1)}, u32[]{:S(2)}, u32[]{:S(2)}) collective-permute-start(bf16[2,512,768]{2,1,0:T(8,128)(2,1)} %pick_output_2_0.1), channel_id=1, source_target_pairs={{0,2},{1,3},{2,0},{3,1},{4,6},{5,7},{6,4},{7,5},{8,10},{9,11},{10,... | collective-permute-start | bytes 4718600 | tf_op jit(solution)/shard_map/ppermute | solution.py:25
  365.1 256.7 %collective-permute-start.12 = (bf16[2,512,768]{2,1,0:T(8,128)(2,1)}, bf16[2,512,768]{2,1,0:T(8,128)(2,1)}, u32[]{:S(2)}, u32[]{:S(2)}) collective-permute-start(bf16[2,512,768]{2,1,0:T(8,128)(2,1)} %pick_output_3_0.1), channel_id=1, source_target_pairs={{0,3},{1,2},{2,1},{3,0},{4,7},{5,6},{6,5},{7,4},{8,11},{9,10},{10,... | collective-permute-start | bytes 4718600 | tf_op jit(solution)/shard_map/ppermute | solution.py:25
  475.7 146.1 %collective-permute-start.13 = (bf16[2,512,768]{2,1,0:T(8,128)(2,1)}, bf16[2,512,768]{2,1,0:T(8,128)(2,1)}, u32[]{:S(2)}, u32[]{:S(2)}) collective-permute-start(bf16[2,512,768]{2,1,0:T(8,128)(2,1)} %pick_output_1_0.1), channel_id=1, source_target_pairs={{0,1},{1,0},{2,3},{3,2},{4,5},{5,4},{6,7},{7,6},{8,9},{9,8},{10,11... | collective-permute-start | bytes 4718600 | tf_op jit(solution)/shard_map/ppermute | solution.py:25
  517.6 200.7 %collective-permute-start.14 = (bf16[2,512,768]{2,1,0:T(8,128)(2,1)}, bf16[2,512,768]{2,1,0:T(8,128)(2,1)}, u32[]{:S(2)}, u32[]{:S(2)}) collective-permute-start(bf16[2,512,768]{2,1,0:T(8,128)(2,1)} %pick_output_2_3.1), channel_id=1, source_target_pairs={{0,2},{1,3},{2,0},{3,1},{4,6},{5,7},{6,4},{7,5},{8,10},{9,11},{10,... | collective-permute-start | bytes 4718600 | tf_op jit(solution)/shard_map/ppermute | solution.py:25
  522.4 195.9 %collective-permute-start.15 = (bf16[2,512,768]{2,1,0:T(8,128)(2,1)}, bf16[2,512,768]{2,1,0:T(8,128)(2,1)}, u32[]{:S(2)}, u32[]{:S(2)}) collective-permute-start(bf16[2,512,768]{2,1,0:T(8,128)(2,1)} %pick_output_3_3.1), channel_id=1, source_target_pairs={{0,3},{1,2},{2,1},{3,0},{4,7},{5,6},{6,5},{7,4},{8,11},{9,10},{10,... | collective-permute-start | bytes 4718600 | tf_op jit(solution)/shard_map/ppermute | solution.py:25
  621.7 96.5 %collective-permute-start.16 = (bf16[2,512,768]{2,1,0:T(8,128)(2,1)}, bf16[2,512,768]{2,1,0:T(8,128)(2,1)}, u32[]{:S(2)}, u32[]{:S(2)}) collective-permute-start(bf16[2,512,768]{2,1,0:T(8,128)(2,1)} %pick_output_1_3.1), channel_id=1, source_target_pairs={{0,1},{1,0},{2,3},{3,2},{4,5},{5,4},{6,7},{7,6},{8,9},{9,8},{10,11... | collective-permute-start | bytes 4718600 | tf_op jit(solution)/shard_map/ppermute | solution.py:25
  661.0 47.9 %collective-permute-start.27 = (bf16[4,128,4608]{2,1,0:T(8,128)(2,1)}, bf16[4,128,4608]{2,1,0:T(8,128)(2,1)}, u32[]{:S(2)}, u32[]{:S(2)}) collective-permute-start(bf16[4,128,4608]{2,1,0:T(8,128)(2,1)} %get-tuple-element.29.refs_5_), channel_id=1, source_target_pairs={{0,4},{4,0},{8,12},{12,8},{16,20},{20,16},{24,28},{28,24},{1,5},{5... | collective-permute-start | bytes 14155784 | tf_op jit(solution)/shard_map/ppermute | solution.py:25
  674.6 90.3 %collective-permute-start.23 = (bf16[2,256,768]{2,1,0:T(8,128)(2,1)}, bf16[2,256,768]{2,1,0:T(8,128)(2,1)}, u32[]{:S(2)}, u32[]{:S(2)}) collective-permute-start(bf16[2,256,768]{2,1,0:T(8,128)(2,1)} %get-tuple-element.33), channel_id=1, source_target_pairs={{0,1},{1,0},{2,3},{3,2},{4,5},{5,4},{6,7},{7,6},{8,9},{9,8},{10,11... | collective-permute-start | bytes 2359304 | tf_op jit(solution)/shard_map/ppermute | solution.py:25
  716.8 54.2 %collective-permute-start.28 = (bf16[2,128,4608]{2,1,0:T(8,128)(2,1)}, bf16[2,128,4608]{2,1,0:T(8,128)(2,1)}, u32[]{:S(2)}, u32[]{:S(2)}) collective-permute-start(bf16[2,128,4608]{2,1,0:T(8,128)(2,1)} %slice.63), channel_id=1, source_target_pairs={{0,8},{4,12},{8,0},{12,4},{16,24},{20,28},{24,16},{28,20},{1,9},{5... | collective-permute-start | bytes 7077896 | tf_op jit(solution)/shard_map/ppermute | solution.py:25
  731.8 35.4 %collective-permute-start.25 = (bf16[2,256,768]{2,1,0:T(8,128)(2,1)}, bf16[2,256,768]{2,1,0:T(8,128)(2,1)}, u32[]{:S(2)}, u32[]{:S(2)}) collective-permute-start(bf16[2,256,768]{2,1,0:T(8,128)(2,1)} %get-tuple-element.35), channel_id=1, source_target_pairs={{0,1},{1,0},{2,3},{3,2},{4,5},{5,4},{6,7},{7,6},{8,9},{9,8},{10,11... | collective-permute-start | bytes 2359304 | tf_op jit(solution)/shard_map/ppermute | solution.py:25
  739.5 131.4 %collective-permute-start.17 = (bf16[2,512,256]{2,1,0:T(8,128)(2,1)}, bf16[2,512,256]{2,1,0:T(8,128)(2,1)}, u32[]{:S(2)}, u32[]{:S(2)}) collective-permute-start(bf16[2,512,256]{2,1,0:T(8,128)(2,1)} %pick_output_1_7.1), channel_id=1, source_target_pairs={{0,1},{1,0},{2,3},{3,2},{4,5},{5,4},{6,7},{7,6},{8,9},{9,8},{10,11... | collective-permute-start | bytes 1572872 | tf_op jit(solution)/shard_map/ppermute | solution.py:25
  743.8 127.1 %collective-permute-start.18 = (bf16[2,512,256]{2,1,0:T(8,128)(2,1)}, bf16[2,512,256]{2,1,0:T(8,128)(2,1)}, u32[]{:S(2)}, u32[]{:S(2)}) collective-permute-start(bf16[2,512,256]{2,1,0:T(8,128)(2,1)} %pick_output_2_7.1), channel_id=1, source_target_pairs={{0,2},{1,3},{2,0},{3,1},{4,6},{5,7},{6,4},{7,5},{8,10},{9,11},{10,... | collective-permute-start | bytes 1572872 | tf_op jit(solution)/shard_map/ppermute | solution.py:25
  764.9 31.6 %collective-permute-start.20 = (bf16[2,512,256]{2,1,0:T(8,128)(2,1)S(1)}, bf16[2,512,256]{2,1,0:T(8,128)(2,1)S(1)}, u32[]{:S(2)}, u32[]{:S(2)}) collective-permute-start(bf16[2,512,256]{2,1,0:T(8,128)(2,1)S(1)} %copy-done.17), channel_id=1, source_target_pairs={{0,1},{1,0},{2,3},{3,2},{4,5},{5,4},{6,7},{7,6},{8,9},{9,8},{10,11... | collective-permute-start | bytes 1572872 | tf_op jit(solution)/shard_map/ppermute | solution.py:25
  767.2 31.6 %collective-permute-start.21 = (bf16[2,512,256]{2,1,0:T(8,128)(2,1)S(1)}, bf16[2,512,256]{2,1,0:T(8,128)(2,1)S(1)}, u32[]{:S(2)}, u32[]{:S(2)}) collective-permute-start(bf16[2,512,256]{2,1,0:T(8,128)(2,1)S(1)} %copy-done.16), channel_id=1, source_target_pairs={{0,2},{1,3},{2,0},{3,1},{4,6},{5,7},{6,4},{7,5},{8,10},{9,11},{10,... | collective-permute-start | bytes 1572872 | tf_op jit(solution)/shard_map/ppermute | solution.py:25
  771.1 41.7 %collective-permute-start.22 = (bf16[2,512,256]{2,1,0:T(8,128)(2,1)S(1)}, bf16[2,512,256]{2,1,0:T(8,128)(2,1)S(1)}, u32[]{:S(2)}, u32[]{:S(2)}) collective-permute-start(bf16[2,512,256]{2,1,0:T(8,128)(2,1)S(1)} %copy-done.15), channel_id=1, source_target_pairs={{0,3},{1,2},{2,1},{3,0},{4,7},{5,6},{6,5},{7,4},{8,11},{9,10},{10,... | collective-permute-start | bytes 1572872 | tf_op jit(solution)/shard_map/ppermute | solution.py:25
  796.5 50.3 %collective-permute-start.24 = (bf16[1,256,768]{2,1,0:T(8,128)(2,1)}, bf16[1,256,768]{2,1,0:T(8,128)(2,1)}, u32[]{:S(2)}, u32[]{:S(2)}) collective-permute-start(bf16[1,256,768]{2,1,0:T(8,128)(2,1)} %slice.74), channel_id=1, source_target_pairs={{0,2},{1,3},{2,0},{3,1},{4,6},{5,7},{6,4},{7,5},{8,10},{9,11},{10,... | collective-permute-start | bytes 1179656 | tf_op jit(solution)/shard_map/ppermute | solution.py:25
  798.8 67.7 %collective-permute-start.26 = (bf16[1,256,768]{2,1,0:T(8,128)(2,1)}, bf16[1,256,768]{2,1,0:T(8,128)(2,1)}, u32[]{:S(2)}, u32[]{:S(2)}) collective-permute-start(bf16[1,256,768]{2,1,0:T(8,128)(2,1)} %slice.76), channel_id=1, source_target_pairs={{0,2},{1,3},{2,0},{3,1},{4,6},{5,7},{6,4},{7,5},{8,10},{9,11},{10,... | collective-permute-start | bytes 1179656 | tf_op jit(solution)/shard_map/ppermute | solution.py:25
  812.9 55.4 %collective-permute-start.29 = (bf16[1,128,4608]{2,1,0:T(8,128)(2,1)}, bf16[1,128,4608]{2,1,0:T(8,128)(2,1)}, u32[]{:S(2)}, u32[]{:S(2)}) collective-permute-start(bf16[1,128,4608]{2,1,0:T(8,128)(2,1)} %slice.78), channel_id=1, source_target_pairs={{0,16},{4,20},{8,24},{12,28},{16,0},{20,4},{24,8},{28,12},{1,17},{... | collective-permute-start | bytes 3538952 | tf_op jit(solution)/shard_map/ppermute | solution.py:25
  846.8 24.1 %collective-permute-start.19 = (bf16[2,512,256]{2,1,0:T(8,128)(2,1)S(1)}, bf16[2,512,256]{2,1,0:T(8,128)(2,1)S(1)}, u32[]{:S(2)}, u32[]{:S(2)}) collective-permute-start(bf16[2,512,256]{2,1,0:T(8,128)(2,1)S(1)} %copy-done.14), channel_id=1, source_target_pairs={{0,3},{1,2},{2,1},{3,0},{4,7},{5,6},{6,5},{7,4},{8,11},{9,10},{10,... | collective-permute-start | bytes 1572872 | tf_op jit(solution)/shard_map/ppermute | solution.py:25
  866.4 20.6 %collective-permute-start.30 = (bf16[2,256,256]{2,1,0:T(8,128)(2,1)}, bf16[2,256,256]{2,1,0:T(8,128)(2,1)}, u32[]{:S(2)}, u32[]{:S(2)}) collective-permute-start(bf16[2,256,256]{2,1,0:T(8,128)(2,1)} %get-tuple-element.39), channel_id=1, source_target_pairs={{0,1},{1,0},{2,3},{3,2},{4,5},{5,4},{6,7},{7,6},{8,9},{9,8},{10,11... | collective-permute-start | bytes 786440 | tf_op jit(solution)/shard_map/ppermute | solution.py:25
  (30 other events, 469.3 us)
Sparse Core Ops, SparseCore 0:
  37.5 29.8 all-gather.2
  82.8 164.4 all-gather.4

commit v3 on v2

--- a/solution.py
+++ b/solution.py
@@ -25,20 +25,12 @@
     return lax.ppermute(x, axis, [(i, i ^ mask) for i in range(n)])
 
 
-def flipped(value, bits):
-    out = 0
-    for b in range(bits):
-        out = out | (((value >> b) & 1) << (bits - 1 - b))
-    return out
-
-
 def cost(flops, us):
     return pl.CostEstimate(flops=int(us * 1e9), bytes_accessed=0, transcendentals=0)
 
 
 EST = dict(
     pack_key_value=1,
-    stack_factors=1,
     split_columns=1,
     pick_output=1,
     place_qkv=1,
@@ -77,30 +69,34 @@
     return i[1 + (i[0] ^ s) * per + j]
 
 
-def pack_key_value(info, key_w, value_w, key_dt, value_dt, key_u, value_u, nt, per):
+def pack_key_value(info, key_w, value_w, key_dt, value_dt, key_u, value_u, riders, nt, per):
     rb, width = key_w.shape
     hd = width // (nt * per)
+    some, wide = riders[0].shape
+    count = len(riders)
 
     def kernel(info_ref, kw, vw, kd, vd, ku, vu, *refs):
-        outs, (mk, mv) = refs[:nt], refs[nt:]
+        outs, (mk, mv) = refs[count : count + nt], refs[count + nt :]
         mk[...] = merged_t(kw[...], kd[...], ku[...])
         mv[...] = merged_t(vw[...], vd[...], vu[...])
         for s in range(nt):
             for j in range(per):
                 at = pl.ds(pl.multiple_of(group_of(s, j, info_ref, per) * hd, hd), hd)
-                outs[s][:, (2 * j) * hd : (2 * j + 1) * hd] = mk[:, at]
-                outs[s][:, (2 * j + 1) * hd : (2 * j + 2) * hd] = mv[:, at]
+                outs[s][:rb, (2 * j) * hd : (2 * j + 1) * hd] = mk[:, at]
+                outs[s][:rb, (2 * j + 1) * hd : (2 * j + 2) * hd] = mv[:, at]
+            for n in range(count):
+                outs[s][rb + n * some : rb + (n + 1) * some, :wide] = refs[n][...]
 
     return call(
         kernel,
         (),
-        [VMEM] * 6,
+        [VMEM] * (6 + count),
         [VMEM] * nt,
-        [jax.ShapeDtypeStruct((rb, per * 2 * hd), bf16)] * nt,
+        [jax.ShapeDtypeStruct((rb + count * some, per * 2 * hd), bf16)] * nt,
         "pack_key_value",
         EST["pack_key_value"],
         [pltpu.VMEM((rb, width), bf16)] * 2,
-    )(info, key_w, value_w, key_dt, value_dt, key_u, value_u)
+    )(info, key_w, value_w, key_dt, value_dt, key_u, value_u, *riders)
 
 
 def pick_query(info, query_w, s, j, groups, per, us, after):
@@ -123,41 +119,27 @@
     )(info, query_w, *after)
 
 
-def stack_factors(info, arrays, after):
-    def kernel(info_ref, *refs):
-        for n in range(len(arrays)):
-            refs[-1][0, n] = refs[n][...]
-
-    shape = (1, len(arrays), *arrays[0].shape)
-    return call(
-        kernel,
-        (),
-        [VMEM] * len(arrays) + [ANY] * len(after),
-        VMEM,
-        jax.ShapeDtypeStruct(shape, bf16),
-        "stack_factors",
-        EST["stack_factors"],
-    )(info, *arrays, *after)
-
-
 def folds(rank, rb, wide):
     return min(wide // rb, rank // 16)
 
 
-def split_columns(info, weight, tokens, down_t, nd):
+def split_columns(info, weight, tokens, factors, nd):
     rb, width = weight.shape
     more = tokens.shape[0]
-    rank = down_t.shape[0]
+    rank = factors[0].shape[0]
     wide = width // nd
     parts = folds(rank, rb, wide)
     few = rank // parts
-    rows = rb + more + few
-
-    def kernel(info_ref, w, t, d, out):
+    rows = rb + more + len(factors) * few
+
+    def kernel(info_ref, w, t, *refs):
+        out = refs[-1]
         out[0, :rb, :] = w[...]
         out[0, rb : rb + more, :] = t[...]
-        for p in range(parts):
-            out[0, rb + more :, p * rb : (p + 1) * rb] = d[p * few : (p + 1) * few, :]
+        for n in range(len(factors)):
+            at = rb + more + n * few
+            for p in range(parts):
+                out[0, at : at + few, p * rb : (p + 1) * rb] = refs[n][p * few : (p + 1) * few, :]
 
     return call(
         kernel,
@@ -165,65 +147,66 @@
         [
             pl.BlockSpec((rb, wide), lambda d, i: (0, d)),
             pl.BlockSpec((more, wide), lambda d, i: (0, d)),
-            pl.BlockSpec((rank, rb), lambda d, i: (0, 0)),
-        ],
+        ]
+        + [pl.BlockSpec((rank, rb), lambda d, i: (0, 0))] * len(factors),
         pl.BlockSpec((1, rows, wide), lambda d, i: (d, 0, 0)),
         jax.ShapeDtypeStruct((nd, rows, wide), bf16),
         "split_columns",
         EST["split_columns"],
-    )(info, weight, tokens, down_t)
+    )(info, weight, tokens, *factors)
 
 
 def pick_output(info, blocks, rb, ups, s, first, count, tile, per, dpg, after):
     parts = per * dpg
     nt, rank, cb = ups.shape
-    bits = nt.bit_length() - 1
     width = count * tile
     piece = min(tile, cb)
     pieces = width // piece
-    steps = 2
-    some = rb // steps if rb // steps % 128 == 0 else rb
-    steps = rb // some
-    wide = blocks.shape[2]
-    parted = folds(rank, rb, wide)
+    parted = folds(rank, rb, blocks.shape[2])
     few = rank // parted
-    below = blocks.shape[1] // few - 1
-
-    def kernel(info_ref, x, *rest):
-        d, up = rest[:parted], rest[parted : parted + pieces]
+    end = blocks.shape[1] // few
+    more = 0 if first else rank
+
+    def kernel(info_ref, x, *refs):
+        d, r = refs[:parted], refs[parted : 2 * parted]
+        up, out = refs[2 * parted : 2 * parted + pieces], refs[-1]
         down_t = jnp.concatenate([y[0] for y in d], axis=0)
-        rest[-1][0] = merged_t(x[0], down_t, jnp.concatenate([u[0] for u in up], axis=1))
-
-    def down_at(p, l, r, i):
-        return (source(l, i), below, p * steps + r)
+        out[0, :rb, :] = merged_t(x[0], down_t, jnp.concatenate([u[0] for u in up], axis=1))
+        if more:
+            for p in range(parted):
+                out[0, rb + p * few : rb + (p + 1) * few, :cb] = r[p][0]
 
     def source(l, i):
         return group_of(s, l // dpg, i, per) * dpg + l % dpg
 
-    def up_at(p, l, r, i):
+    def factor_at(row, p, l, i):
+        return (source(l, i), row, p)
+
+    def up_at(p, l, i):
         at = first * tile + p * piece
-        return (flipped((at // cb) ^ i[0], bits), 0, at % cb // piece)
-
-    return call(
-        kernel,
-        (parts, steps),
-        [
-            pl.BlockSpec((1, some, width), lambda l, r, i: (source(l, i), r, first // count)),
+        return ((at // cb) ^ i[0], 0, at % cb // piece)
+
+    return call(
+        kernel,
+        (parts,),
+        [pl.BlockSpec((1, rb, width), lambda l, i: (source(l, i), 0, first // count))]
+        + [
+            pl.BlockSpec((1, few, cb), functools.partial(factor_at, row, p))
+            for row in (end - 2, end - 1)
+            for p in range(parted)
         ]
-        + [pl.BlockSpec((1, few, some), functools.partial(down_at, p)) for p in range(parted)]
         + [pl.BlockSpec((1, rank, piece), functools.partial(up_at, p)) for p in range(pieces)]
         + [ANY] * len(after),
-        pl.BlockSpec((1, some, width), lambda l, r, i: (l, r, 0)),
-        jax.ShapeDtypeStruct((parts, rb, width), bf16),
+        pl.BlockSpec((1, rb + more, width), lambda l, i: (l, 0, 0)),
+        jax.ShapeDtypeStruct((parts, rb + more, width), bf16),
         f"pick_output_{s}_{first}",
         EST["pick_output"],
-    )(info, blocks, *[blocks] * parted, *[ups] * pieces, *after)
-
-
-def place_qkv(info, blocks, hidden_rows, query, keyval, downs, factors, per, nd, after):
+    )(info, blocks, *[blocks] * (2 * parted), *[ups] * pieces, *after)
+
+
+def place_qkv(info, blocks, hidden_rows, query, keyval, downs, ups, per, dpg, nd):
     nt, rank, cb = downs.shape
     rb, gq = query[0][0].shape
-    bits = nt.bit_length() - 1
     sources, _, depth = blocks.shape
     some = hidden_rows
     count = sources * some
@@ -257,8 +240,8 @@
 
             @pl.when(jnp.logical_and(place == j, jnp.logical_not(last)))
             def _():
-                up = jnp.concatenate([x[...] for x in u], axis=1)
-                put([merged_t(q[s][...], d[flipped(s, bits)], up) for s in range(nt)])
+                up = jnp.concatenate([x[0, 0] for x in u], axis=1)
+                put([merged_t(q[s][...], d[s], up) for s in range(nt)])
 
         @pl.when(last)
         def _():
@@ -269,9 +252,9 @@
         return (0, jnp.where(k == j, w, jnp.where(k < j, 0, wide - 1)))
 
     def up_at(p, n, i):
-        at = group_of(0, n // each, i, per) * gq + jnp.minimum(n % each, wide - 1) * tile
+        at = jnp.minimum(n % each, wide - 1) * tile
         block = at // cb + p
-        return (block // nt * nt + flipped((block % nt) ^ i[0], bits), at % cb // piece)
+        return ((block % nt) ^ i[0], (n // each) * dpg + block // nt, 0, at % cb // piece)
 
     half = jax.ShapeDtypeStruct((nd // 2, count // nd, cols), bf16)
     half_spec = pl.BlockSpec((nd // 2, count // nd, tile), lambda n, i: (0, 0, n))
@@ -282,14 +265,13 @@
             pl.BlockSpec((sources, some, depth), lambda n, i: (0, rb // some, 0)),
             pl.BlockSpec(downs.shape, lambda n, i: (0, 0, 0)),
         ]
-        + [pl.BlockSpec((rank, piece), functools.partial(up_at, p)) for p in range(pieces)]
+        + [pl.BlockSpec((1, 1, rank, piece), functools.partial(up_at, p)) for p in range(pieces)]
         + [
             pl.BlockSpec((rb, tile), functools.partial(column, j))
             for j in range(per)
             for _ in range(nt)
         ]
-        + [pl.BlockSpec((rb, tile), lambda n, i: (0, n // each))] * nt
-        + [ANY] * len(after),
+        + [pl.BlockSpec((rb, tile), lambda n, i: (0, n // each))] * nt,
         [
             pl.BlockSpec((nt * rb, tile), lambda n, i: (0, n)),
             half_spec,
@@ -299,11 +281,11 @@
         "place_qkv",
         EST["place_qkv"],
         [pltpu.VMEM((count, tile), bf16)],
-    )(info, blocks, downs, *[factors] * pieces, *[x for at in query for x in at], *keyval, *after)
-
-
-def place_output(info, tokens, arrived, before, first, tile, cols, nt, after):
-    parts, rb, width = arrived[0].shape
+    )(info, blocks, downs, *[ups] * pieces, *[x for at in query for x in at], *keyval)
+
+
+def place_output(info, tokens, arrived, rb, before, first, tile, cols, nt, after):
+    parts, _, width = arrived[0].shape
     rows, depth = tokens.shape
     each = rows // nt
 
@@ -366,7 +348,6 @@
 ):
     groups = slice_group.shape[0]
     nt, nd = lax.axis_size("tensor"), lax.axis_size("dp")
-    bits = nt.bit_length() - 1
     per, dpg = groups // nt, nd // groups
     rank, cb = query_up.shape
     place = [lax.axis_index(axis).astype(jnp.int32)[None] for axis in ("tensor", "dp")]
@@ -378,11 +359,23 @@
         return {s: swap(x, "tensor", s) if s else x for s, x in sent.items()}
 
     keyval = pack_key_value(
-        info, key_projection_rows, value_weight, key_down.T, value_down.T, key_up, value_up, nt, per
+        info,
+        key_projection_rows,
+        value_weight,
+        key_down.T,
+        value_down.T,
+        key_up,
+        value_up,
+        (output_up, query_lower_factor.T),
+        nt,
+        per,
     )
     got = exchange({s: keyval[s] for s in order})
     keyval = [got[s] for s in range(nt)]
-    outgoing = split_columns(info, output_weight, hidden, output_down.T, nd)
+    rb = query_weight.shape[0]
+    output_ups = jnp.stack([x[rb : rb + rank, :cb] for x in keyval])
+    query_downs = jnp.stack([x[rb + rank :, :rb] for x in keyval])
+    outgoing = split_columns(info, output_weight, hidden, (output_down.T, query_up), nd)
     blocks = lax.all_to_all(outgoing, "dp", split_axis=0, concat_axis=0, tiled=True)
 
     query = []
@@ -396,12 +389,6 @@
         got = exchange(sent)
         query.append([got[s] for s in range(nt)])
 
-    factors = stack_factors(info, (query_up, output_up, query_lower_factor.T), [])
-    for b in reversed(range(bits)):
-        factors = jnp.concatenate((factors, swap(factors, "tensor", 1 << b)))
-    output_ups, query_downs = factors[:, 1], factors[:, 2]
-    query_ups = lax.all_gather(factors[:, 0].reshape(nt * rank, cb), "dp", axis=0, tiled=True)
-
     context_all = lax.all_gather(context, "dp", axis=0, tiled=True)
 
     cols = blocks.shape[2]
@@ -411,22 +398,29 @@
     sums, done = [], []
     for n, (first, count) in enumerate(chunks):
         last = n == len(chunks) - 1
-        after = done[n - 2] if n >= 2 else []
-        sent = {
-            s: pick_output(
-                info, blocks, output_weight.shape[0], output_ups, s, first, count, tile, per, dpg, after if s else []
+        sent = {}
+        for s in order:
+            after = []
+            if s and n == 0:
+                after = query[0][1:] + (query[-1][1:] if s == 1 else [])
+            elif s and last:
+                after = picked
+            elif s and n >= 2:
+                after = done[n - 2]
+            sent[s] = pick_output(
+                info, blocks, rb, output_ups, s, first, count, tile, per, dpg, after
             )
-            for s in order
-        }
+        picked = [sent[s] for s in order if s]
         got = exchange(sent)
         done.append([got[s] for s in order if s])
         if n == 0:
+            query_ups = jnp.stack([got[s][:, rb:, :cb] for s in range(nt)])
             merged_qkv, *partial = place_qkv(
-                info, blocks, hidden.shape[0], query, keyval, query_downs, query_ups, per, nd, done[0]
+                info, blocks, hidden.shape[0], query, keyval, query_downs, query_ups, per, dpg, nd
             )
             projections = total_over("dp", *partial)
         merged_output, send, keep = place_output(
-            info, context_all, [got[s] for s in range(nt)], merged_output, first, tile, cols, nt,
+            info, context_all, [got[s] for s in range(nt)], rb, merged_output, first, tile, cols, nt,
             partial[:1] if n == 1 else sums[:-1] + [projections] if last else [],
         )
         sums.append(total_over("tensor", send, keep))

time: 916 us -> 906 us (0.989)
  Pallas kernels: 216 us -> 196 us
  starting transfers between devices: 105 us -> 123 us
  waiting for transfers between devices: 546 us -> 528 us
  local copies, waits for them, and re-layouts: 8.98 us -> 19.4 us
    ppermute x34 -> x32, waiting for transfers between devices: 527 us -> 468 us  [swap(): return lax.ppermute(x, axis, [(i, i ^ mask) for i in range(n)])]
    all_to_all x1, waiting for transfers between devices: 19.5 us -> 60.5 us  [body(): lax.all_to_all(outgoing, 'dp', split_axis=0, concat_axis=0, tiled=True)]
    pallas_call x18 -> x17, Pallas kernels: 80.7 us -> 61.1 us  [the longest x16 56.4 us: pick_output(): call(kernel, (parts,), [pl.BlockSpec((1, rb, width), lambda l, i: (source...]
    ppermute x34 -> x32, starting transfers between devices: 98.6 us -> 116 us  [swap(): return lax.ppermute(x, axis, [(i, i ^ mask) for i in range(n)])]
    another operation x0 -> x8, local copies, waits for them, and re-layouts: none -> 9.64 us  [the longest x4 5.98 us: body(): output_ups = jnp.stack([x[rb:rb + rank, :cb] for x in keyval])]
  transfers between devices with their start and end apart: 37 -> 34, of which waited for: 13 -> 16; matrix products, arithmetic and copies ran while one was open for 2% -> 4% of each run, Pallas kernels for 23% -> 21%
where the time goes in v3:
time: 906 us; the launch traced here: 903 us
  waiting for transfers between devices  528 us (58%)
  Pallas kernels  196 us (22%)
  starting transfers between devices  123 us (14%)
  other arithmetic  22.9 us (3%)
  local copies, waits for them, and re-layouts  19.4 us (2%)
  between operations  14.4 us (2%)
    ppermute x32, waiting for transfers between devices, swap(): return lax.ppermute(x, axis, [(i, i ^ mask) for i in range(n)])  468 us
    ppermute x32, starting transfers between devices, swap(): return lax.ppermute(x, axis, [(i, i ^ mask) for i in range(n)])  116 us
    all_to_all x1, waiting for transfers between devices, body(): lax.all_to_all(outgoing, 'dp', split_axis=0, concat_axis=0, tiled=True)  60.5 us
    pallas_call x16, Pallas kernels, pick_output(): call(kernel, (parts,), [pl.BlockSpec((1, rb, width), lambda l, i: (source...  56.4 us
    pallas_call x4, Pallas kernels, place_output(): call(kernel, (width // tile,), [pl.BlockSpec((rows, depth), lambda c, i:...  43.2 us
    pallas_call x1, Pallas kernels, place_qkv(): call(kernel, (per * each,), [pl.BlockSpec((sources, some, depth), lambda...  38.7 us
    pallas_call x8, Pallas kernels, pick_query(): call(kernel, (steps,), [pl.BlockSpec((rb // steps, cols), lambda r, i: (r...  35.9 us
  transfers between devices with their start and end apart: 34, of which 16 were waited for; matrix products, arithmetic and copies ran while one was open for 4% of the time, Pallas kernels for 21%

profile of v3, /device:TPU:0, one launch (start us, length us, event | category | flops | bytes accessed | tf_op | source)
XLA Modules:
  0.0 903.3 jit_solution(17922499037193415543)
XLA Ops:
  8.4 4.7 pack_key_value.1
  13.1 5.0 collective-permute-start.2
  18.7 16.9 %split_columns.1 = bf16[8,672,2048]{2,1,0:T(8,128)(2,1)} custom-call(s32[10]{0:T(128)} %pad_add_fusion.info_ref, bf16[512,16384]{1,0:T(8,128)(2,1)} %w.1, bf16[128,16384]{1,0:T(8,128)(2,1)} %t.1, bf16[64,512]{1,0:T(8,128)(2,1)} %bitcast.42, bf16[64,512]{1,0:T(8,128)(2,1)} %refs_1_.1), custom_call_target="tpu_custom_call" | custom-call | flops 1000000000 | tf_op jit(solution)/shard_map/split_columns/pallas_call | solution.py:144
  35.7 6.2 all-to-all-start
  48.7 4.5 pick_query_3_0.1
  54.7 110.6 %collective-permute-done.1.refs_1_.refs_11_ = bf16[640,512]{1,0:T(8,128)(2,1)S(1)} collective-permute-done((bf16[640,512]{1,0:T(8,128)(2,1)}, bf16[640,512]{1,0:T(8,128)(2,1)S(1)}, u32[]{:S(2)}, u32[]{:S(2)}) %collective-permute-start.1) | collective-permute-done | bytes 655392 | tf_op jit(solution)/shard_map/ppermute | solution.py:25
  171.4 4.5 pick_query_1_1.1
  177.9 4.5 pick_query_2_1.1
  183.6 4.5 pick_query_3_1.1
  188.1 22.2 %collective-permute-done.4.refs_12_.refs_3_ = bf16[512,2048]{1,0:T(8,128)(2,1)} collective-permute-done((bf16[512,2048]{1,0:T(8,128)(2,1)}, bf16[512,2048]{1,0:T(8,128)(2,1)}, u32[]{:S(2)}, u32[]{:S(2)}) %collective-permute-start.4) | collective-permute-done | bytes 2097184 | tf_op jit(solution)/shard_map/ppermute | solution.py:25
  219.7 35.5 %collective-permute-done.3.refs_11_.refs_2_ = bf16[512,2048]{1,0:T(8,128)(2,1)S(1)} collective-permute-done((bf16[512,2048]{1,0:T(8,128)(2,1)}, bf16[512,2048]{1,0:T(8,128)(2,1)S(1)}, u32[]{:S(2)}, u32[]{:S(2)}) %collective-permute-start.3) | collective-permute-done | bytes 2097184 | tf_op jit(solution)/shard_map/ppermute | solution.py:25
  255.2 60.5 %all-to-all-done.x.refs_0_.refs_1_.refs_2_.refs_3_.refs_4_.refs_5_.refs_6_.refs_7_.a = bf16[8,672,2048]{2,1,0:T(8,128)(2,1)} async-done(((bf16[8,672,2048]{2,1,0:T(8,128)(2,1)}), bf16[8,672,2048]{2,1,0:T(8,128)(2,1)}, u32[]{:S(2)}, u32[]{:S(2)}) %all-to-all-start) | async-done | bytes 22020128 | tf_op jit(solution)/shard_map/all_to_all | solution.py:379
  327.2 138.8 %collective-permute-done.7.refs_15_.refs_7_ = bf16[512,2048]{1,0:T(8,128)(2,1)} collective-permute-done((bf16[512,2048]{1,0:T(8,128)(2,1)}, bf16[512,2048]{1,0:T(8,128)(2,1)}, u32[]{:S(2)}, u32[]{:S(2)}) %collective-permute-start.7) | collective-permute-done | bytes 2097184 | tf_op jit(solution)/shard_map/ppermute | solution.py:25
  469.8 45.5 %collective-permute-start.9 = (bf16[2,576,768]{2,1,0:T(8,128)(2,1)}, bf16[2,576,768]{2,1,0:T(8,128)(2,1)}, u32[]{:S(2)}, u32[]{:S(2)}) collective-permute-start(bf16[2,576,768]{2,1,0:T(8,128)(2,1)} %pick_output_1_0.1), channel_id=1, source_target_pairs={{0,1},{1,0},{2,3},{3,2},{4,5},{5,4},{6,7},{7,6},{8,9},{9,8},{10,11... | collective-permute-start | bytes 5308424 | tf_op jit(solution)/shard_map/ppermute | solution.py:25
  515.3 4.5 pick_query_0_0.1.refs_1_
  519.8 4.6 pick_query_0_1.1.refs_5_
  556.9 31.6 %collective-permute-done.10.refs_9_.refs_2_ = bf16[2,576,768]{2,1,0:T(8,128)(2,1)} collective-permute-done((bf16[2,576,768]{2,1,0:T(8,128)(2,1)}, bf16[2,576,768]{2,1,0:T(8,128)(2,1)}, u32[]{:S(2)}, u32[]{:S(2)}) %collective-permute-start.10) | collective-permute-done | bytes 1769504 | tf_op jit(solution)/shard_map/ppermute | solution.py:25
  589.4 6.2 collective-permute-done.9.refs_11_.refs_1_
  597.4 38.7 %place_qkv.1 = (bf16[2048,4608]{1,0:T(8,128)(2,1)}, bf16[4,128,4608]{2,1,0:T(8,128)(2,1)}, bf16[4,128,4608]{2,1,0:T(8,128)(2,1)}) custom-call(s32[10]{0:T(128)} %pad_add_fusion.info_ref, bf16[8,672,2048]{2,1,0:T(8,128)(2,1)} %all-to-all-done.x.refs_0_.refs_1_.refs_2_.refs_3_.refs_4_.refs_5_.refs_6_.refs_7_.a, bf16[4,64,512]{2,1,0:T(8,128)(2,1)} %pad_maximum_fusion.2.d, ...), custom_call_target="tpu_custom_call" | custom-call | flops 1000000000 | tf_op jit(solution)/shard_map/place_qkv/pallas_call | solution.py:261
  636.2 13.5 %place_output_0.1 = (bf16[4096,2048]{1,0:T(8,128)(2,1)}, bf16[2,256,768]{2,1,0:T(8,128)(2,1)}, bf16[2,256,768]{2,1,0:T(8,128)(2,1)}) custom-call(s32[10]{0:T(128)} %pad_add_fusion.info_ref, bf16[1024,4096]{1,0:T(8,128)(2,1)} %all-gather.2.cloned.1.call-done.a, bf16[2,576,768]{2,1,0:T(8,128)(2,1)} %pick_output_0_0.1.refs_0_, ...), custom_call_target="tpu_custom_call" | custom-call | flops 199999995904 | tf_op jit(solution)/shard_map/place_output_0/pallas_call | solution.py:313
  649.7 5.0 add_convert_fusion
  659.1 35.1 %collective-permute-done.18.refs_1_ = bf16[2,512,768]{2,1,0:T(8,128)(2,1)} collective-permute-done((bf16[2,512,768]{2,1,0:T(8,128)(2,1)}, bf16[2,512,768]{2,1,0:T(8,128)(2,1)}, u32[]{:S(2)}, u32[]{:S(2)}) %collective-permute-start.18) | collective-permute-done | bytes 1572896 | tf_op jit(solution)/shard_map/ppermute | solution.py:25
  694.2 13.6 %place_output_3.1 = (bf16[4096,2048]{1,0:T(8,128)(2,1)}, bf16[2,256,768]{2,1,0:T(8,128)(2,1)}, bf16[2,256,768]{2,1,0:T(8,128)(2,1)}) custom-call(s32[10]{0:T(128)} %pad_add_fusion.info_ref, bf16[1024,4096]{1,0:T(8,128)(2,1)} %all-gather.2.cloned.1.call-done.a, bf16[2,512,768]{2,1,0:T(8,128)(2,1)} %pick_output_0_3.1.refs_0_, ...), custom_call_target="tpu_custom_call", output_to_operand_aliasing={{0}: (6, {})} | custom-call | flops 199999995904 | tf_op jit(solution)/shard_map/place_output_3/pallas_call | solution.py:313
  707.8 27.1 %collective-permute-start.23 = (bf16[2,256,768]{2,1,0:T(8,128)(2,1)}, bf16[2,256,768]{2,1,0:T(8,128)(2,1)}, u32[]{:S(2)}, u32[]{:S(2)}) collective-permute-start(bf16[2,256,768]{2,1,0:T(8,128)(2,1)} %get-tuple-element.35), channel_id=1, source_target_pairs={{0,1},{1,0},{2,3},{3,2},{4,5},{5,4},{6,7},{7,6},{8,9},{9,8},{10,11... | collective-permute-start | bytes 2359304 | tf_op jit(solution)/shard_map/ppermute | solution.py:25
  780.6 9.2 %collective-permute-done.17.refs_3_ = bf16[2,512,256]{2,1,0:T(8,128)(2,1)S(1)} collective-permute-done((bf16[2,512,256]{2,1,0:T(8,128)(2,1)S(1)}, bf16[2,512,256]{2,1,0:T(8,128)(2,1)S(1)}, u32[]{:S(2)}, u32[]{:S(2)}) %collective-permute-start.17) | collective-permute-done | bytes 524320 | tf_op jit(solution)/shard_map/ppermute | solution.py:25
  791.3 8.1 place_output_6.1
  799.4 48.3 %collective-permute-done.22 = bf16[1,256,768]{2,1,0:T(8,128)(2,1)} collective-permute-done((bf16[1,256,768]{2,1,0:T(8,128)(2,1)}, bf16[1,256,768]{2,1,0:T(8,128)(2,1)}, u32[]{:S(2)}, u32[]{:S(2)}) %collective-permute-start.22) | collective-permute-done | bytes 393248 | tf_op jit(solution)/shard_map/ppermute | solution.py:25
  851.0 10.7 %collective-permute-done.24 = bf16[1,256,768]{2,1,0:T(8,128)(2,1)} collective-permute-done((bf16[1,256,768]{2,1,0:T(8,128)(2,1)}, bf16[1,256,768]{2,1,0:T(8,128)(2,1)}, u32[]{:S(2)}, u32[]{:S(2)}) %collective-permute-start.24) | collective-permute-done | bytes 393248 | tf_op jit(solution)/shard_map/ppermute | solution.py:25
  866.9 8.1 place_output_7.1
  875.1 4.6 collective-permute-start.30
  881.0 6.2 collective-permute-done.30
  890.7 4.7 collective-permute-done.31
  (151 shorter events, 145.6 us)
Async XLA Ops:
  13.1 41.5 %collective-permute-start.2 = (bf16[640,512]{1,0:T(8,128)(2,1)}, bf16[640,512]{1,0:T(8,128)(2,1)S(1)}, u32[]{:S(2)}, u32[]{:S(2)}) collective-permute-start(bf16[640,512]{1,0:T(8,128)(2,1)} %get-tuple-element.26), channel_id=1, source_target_pairs={{0,3},{1,2},{2,1},{3,0},{4,7},{5,6},{6,5},{7,4},{8,11},{9,10},{10,... | collective-permute-start | bytes 1966088 | tf_op jit(solution)/shard_map/ppermute | solution.py:25
  18.2 147.1 %collective-permute-start.1 = (bf16[640,512]{1,0:T(8,128)(2,1)}, bf16[640,512]{1,0:T(8,128)(2,1)S(1)}, u32[]{:S(2)}, u32[]{:S(2)}) collective-permute-start(bf16[640,512]{1,0:T(8,128)(2,1)} %get-tuple-element.25), channel_id=1, source_target_pairs={{0,2},{1,3},{2,0},{3,1},{4,6},{5,7},{6,4},{7,5},{8,10},{9,11},{10,... | collective-permute-start | bytes 1966088 | tf_op jit(solution)/shard_map/ppermute | solution.py:25
  18.2 147.1 %collective-permute-start = (bf16[640,512]{1,0:T(8,128)(2,1)}, bf16[640,512]{1,0:T(8,128)(2,1)S(1)}, u32[]{:S(2)}, u32[]{:S(2)}) collective-permute-start(bf16[640,512]{1,0:T(8,128)(2,1)} %get-tuple-element.24), channel_id=1, source_target_pairs={{0,1},{1,0},{2,3},{3,2},{4,5},{5,4},{6,7},{7,6},{8,9},{9,8},{10,11... | collective-permute-start | bytes 1966088 | tf_op jit(solution)/shard_map/ppermute | solution.py:25
  35.7 280.0 %all-to-all-start = ((bf16[8,672,2048]{2,1,0:T(8,128)(2,1)}), bf16[8,672,2048]{2,1,0:T(8,128)(2,1)}, u32[]{:S(2)}, u32[]{:S(2)}) async-start(bf16[8,672,2048]{2,1,0:T(8,128)(2,1)} %split_columns.1), calls=%async_computation | async-start | bytes 44040192 | tf_op jit(solution)/shard_map/all_to_all | solution.py:379
  41.9 594.3 %all-gather.2.cloned.1.call-start = ((), (), s32[]{:S(2)}) async-start(), calls=%async_computation.1 | async-start | bytes 9437184 | tf_op jit(solution)/shard_map/all_gather | solution.py:392
  46.4 164.0 %collective-permute-start.4 = (bf16[512,2048]{1,0:T(8,128)(2,1)}, bf16[512,2048]{1,0:T(8,128)(2,1)}, u32[]{:S(2)}, u32[]{:S(2)}) collective-permute-start(bf16[512,2048]{1,0:T(8,128)(2,1)} %pick_query_2_0.1), channel_id=1, source_target_pairs={{0,2},{1,3},{2,0},{3,1},{4,6},{5,7},{6,4},{7,5},{8,10},{9,11},{10,... | collective-permute-start | bytes 6291464 | tf_op jit(solution)/shard_map/ppermute | solution.py:25
  53.2 166.6 %collective-permute-start.5 = (bf16[512,2048]{1,0:T(8,128)(2,1)}, bf16[512,2048]{1,0:T(8,128)(2,1)}, u32[]{:S(2)}, u32[]{:S(2)}) collective-permute-start(bf16[512,2048]{1,0:T(8,128)(2,1)} %pick_query_3_0.1), channel_id=1, source_target_pairs={{0,3},{1,2},{2,1},{3,0},{4,7},{5,6},{6,5},{7,4},{8,11},{9,10},{10,... | collective-permute-start | bytes 6291464 | tf_op jit(solution)/shard_map/ppermute | solution.py:25
  171.4 83.8 %collective-permute-start.3 = (bf16[512,2048]{1,0:T(8,128)(2,1)}, bf16[512,2048]{1,0:T(8,128)(2,1)S(1)}, u32[]{:S(2)}, u32[]{:S(2)}) collective-permute-start(bf16[512,2048]{1,0:T(8,128)(2,1)} %pick_query_1_0.1), channel_id=1, source_target_pairs={{0,1},{1,0},{2,3},{3,2},{4,5},{5,4},{6,7},{7,6},{8,9},{9,8},{10,11... | collective-permute-start | bytes 6291464 | tf_op jit(solution)/shard_map/ppermute | solution.py:25
  175.9 151.3 %collective-permute-start.6 = (bf16[512,2048]{1,0:T(8,128)(2,1)}, bf16[512,2048]{1,0:T(8,128)(2,1)}, u32[]{:S(2)}, u32[]{:S(2)}) collective-permute-start(bf16[512,2048]{1,0:T(8,128)(2,1)} %pick_query_1_1.1), channel_id=1, source_target_pairs={{0,1},{1,0},{2,3},{3,2},{4,5},{5,4},{6,7},{7,6},{8,9},{9,8},{10,11... | collective-permute-start | bytes 6291464 | tf_op jit(solution)/shard_map/ppermute | solution.py:25
  182.4 283.6 %collective-permute-start.7 = (bf16[512,2048]{1,0:T(8,128)(2,1)}, bf16[512,2048]{1,0:T(8,128)(2,1)}, u32[]{:S(2)}, u32[]{:S(2)}) collective-permute-start(bf16[512,2048]{1,0:T(8,128)(2,1)} %pick_query_2_1.1), channel_id=1, source_target_pairs={{0,2},{1,3},{2,0},{3,1},{4,6},{5,7},{6,4},{7,5},{8,10},{9,11},{10,... | collective-permute-start | bytes 6291464 | tf_op jit(solution)/shard_map/ppermute | solution.py:25
  210.3 255.7 %collective-permute-start.8 = (bf16[512,2048]{1,0:T(8,128)(2,1)}, bf16[512,2048]{1,0:T(8,128)(2,1)}, u32[]{:S(2)}, u32[]{:S(2)}) collective-permute-start(bf16[512,2048]{1,0:T(8,128)(2,1)} %pick_query_3_1.1), channel_id=1, source_target_pairs={{0,3},{1,2},{2,1},{3,0},{4,7},{5,6},{6,5},{7,4},{8,11},{9,10},{10,... | collective-permute-start | bytes 6291464 | tf_op jit(solution)/shard_map/ppermute | solution.py:25
  319.5 235.2 %collective-permute-start.11 = (bf16[2,576,768]{2,1,0:T(8,128)(2,1)}, bf16[2,576,768]{2,1,0:T(8,128)(2,1)}, u32[]{:S(2)}, u32[]{:S(2)}) collective-permute-start(bf16[2,576,768]{2,1,0:T(8,128)(2,1)} %pick_output_3_0.1), channel_id=1, source_target_pairs={{0,3},{1,2},{2,1},{3,0},{4,7},{5,6},{6,5},{7,4},{8,11},{9,10},{10,... | collective-permute-start | bytes 5308424 | tf_op jit(solution)/shard_map/ppermute | solution.py:25
  327.2 261.3 %collective-permute-start.10 = (bf16[2,576,768]{2,1,0:T(8,128)(2,1)}, bf16[2,576,768]{2,1,0:T(8,128)(2,1)}, u32[]{:S(2)}, u32[]{:S(2)}) collective-permute-start(bf16[2,576,768]{2,1,0:T(8,128)(2,1)} %pick_output_2_0.1), channel_id=1, source_target_pairs={{0,2},{1,3},{2,0},{3,1},{4,6},{5,7},{6,4},{7,5},{8,10},{9,11},{10,... | collective-permute-start | bytes 5308424 | tf_op jit(solution)/shard_map/ppermute | solution.py:25
  469.8 125.8 %collective-permute-start.9 = (bf16[2,576,768]{2,1,0:T(8,128)(2,1)}, bf16[2,576,768]{2,1,0:T(8,128)(2,1)}, u32[]{:S(2)}, u32[]{:S(2)}) collective-permute-start(bf16[2,576,768]{2,1,0:T(8,128)(2,1)} %pick_output_1_0.1), channel_id=1, source_target_pairs={{0,1},{1,0},{2,3},{3,2},{4,5},{5,4},{6,7},{7,6},{8,9},{9,8},{10,11... | collective-permute-start | bytes 5308424 | tf_op jit(solution)/shard_map/ppermute | solution.py:25
  529.0 165.2 %collective-permute-start.18 = (bf16[2,512,768]{2,1,0:T(8,128)(2,1)}, bf16[2,512,768]{2,1,0:T(8,128)(2,1)}, u32[]{:S(2)}, u32[]{:S(2)}) collective-permute-start(bf16[2,512,768]{2,1,0:T(8,128)(2,1)} %pick_output_1_3.1), channel_id=1, source_target_pairs={{0,1},{1,0},{2,3},{3,2},{4,5},{5,4},{6,7},{7,6},{8,9},{9,8},{10,11... | collective-permute-start | bytes 4718600 | tf_op jit(solution)/shard_map/ppermute | solution.py:25
  532.9 161.3 %collective-permute-start.19 = (bf16[2,512,768]{2,1,0:T(8,128)(2,1)}, bf16[2,512,768]{2,1,0:T(8,128)(2,1)}, u32[]{:S(2)}, u32[]{:S(2)}) collective-permute-start(bf16[2,512,768]{2,1,0:T(8,128)(2,1)} %pick_output_2_3.1), channel_id=1, source_target_pairs={{0,2},{1,3},{2,0},{3,1},{4,6},{5,7},{6,4},{7,5},{8,10},{9,11},{10,... | collective-permute-start | bytes 4718600 | tf_op jit(solution)/shard_map/ppermute | solution.py:25
  554.8 139.4 %collective-permute-start.20 = (bf16[2,512,768]{2,1,0:T(8,128)(2,1)}, bf16[2,512,768]{2,1,0:T(8,128)(2,1)}, u32[]{:S(2)}, u32[]{:S(2)}) collective-permute-start(bf16[2,512,768]{2,1,0:T(8,128)(2,1)} %pick_output_3_3.1), channel_id=1, source_target_pairs={{0,3},{1,2},{2,1},{3,0},{4,7},{5,6},{6,5},{7,4},{8,11},{9,10},{10,... | collective-permute-start | bytes 4718600 | tf_op jit(solution)/shard_map/ppermute | solution.py:25
  636.1 13.6 %collective-permute-start.25 = (bf16[4,128,4608]{2,1,0:T(8,128)(2,1)}, bf16[4,128,4608]{2,1,0:T(8,128)(2,1)}, u32[]{:S(2)}, u32[]{:S(2)}) collective-permute-start(bf16[4,128,4608]{2,1,0:T(8,128)(2,1)} %get-tuple-element.29.refs_5_), channel_id=1, source_target_pairs={{0,4},{4,0},{8,12},{12,8},{16,20},{20,16},{24,28},{28,24},{1,5},{5... | collective-permute-start | bytes 14155784 | tf_op jit(solution)/shard_map/ppermute | solution.py:25
  649.7 107.7 %collective-permute-start.21 = (bf16[2,256,768]{2,1,0:T(8,128)(2,1)}, bf16[2,256,768]{2,1,0:T(8,128)(2,1)}, u32[]{:S(2)}, u32[]{:S(2)}) collective-permute-start(bf16[2,256,768]{2,1,0:T(8,128)(2,1)} %get-tuple-element.33), channel_id=1, source_target_pairs={{0,1},{1,0},{2,3},{3,2},{4,5},{5,4},{6,7},{7,6},{8,9},{9,8},{10,11... | collective-permute-start | bytes 2359304 | tf_op jit(solution)/shard_map/ppermute | solution.py:25
  657.5 109.6 %collective-permute-start.26 = (bf16[2,128,4608]{2,1,0:T(8,128)(2,1)}, bf16[2,128,4608]{2,1,0:T(8,128)(2,1)}, u32[]{:S(2)}, u32[]{:S(2)}) collective-permute-start(bf16[2,128,4608]{2,1,0:T(8,128)(2,1)} %slice.99), channel_id=1, source_target_pairs={{0,8},{4,12},{8,0},{12,4},{16,24},{20,28},{24,16},{28,20},{1,9},{5... | collective-permute-start | bytes 7077896 | tf_op jit(solution)/shard_map/ppermute | solution.py:25
  707.8 57.1 %collective-permute-start.23 = (bf16[2,256,768]{2,1,0:T(8,128)(2,1)}, bf16[2,256,768]{2,1,0:T(8,128)(2,1)}, u32[]{:S(2)}, u32[]{:S(2)}) collective-permute-start(bf16[2,256,768]{2,1,0:T(8,128)(2,1)} %get-tuple-element.35), channel_id=1, source_target_pairs={{0,1},{1,0},{2,3},{3,2},{4,5},{5,4},{6,7},{7,6},{8,9},{9,8},{10,11... | collective-permute-start | bytes 2359304 | tf_op jit(solution)/shard_map/ppermute | solution.py:25
  738.0 39.7 %collective-permute-start.15 = (bf16[2,512,256]{2,1,0:T(8,128)(2,1)}, bf16[2,512,256]{2,1,0:T(8,128)(2,1)}, u32[]{:S(2)}, u32[]{:S(2)}) collective-permute-start(bf16[2,512,256]{2,1,0:T(8,128)(2,1)} %pick_output_1_6.1.refs_11_), channel_id=1, source_target_pairs={{0,1},{1,0},{2,3},{3,2},{4,5},{5,4},{6,7},{7,6},{8,9},{9,8},{10,11... | collective-permute-start | bytes 1572872 | tf_op jit(solution)/shard_map/ppermute | solution.py:25
  741.2 37.2 %collective-permute-start.16 = (bf16[2,512,256]{2,1,0:T(8,128)(2,1)}, bf16[2,512,256]{2,1,0:T(8,128)(2,1)}, u32[]{:S(2)}, u32[]{:S(2)}) collective-permute-start(bf16[2,512,256]{2,1,0:T(8,128)(2,1)} %pick_output_2_6.1.refs_9_), channel_id=1, source_target_pairs={{0,2},{1,3},{2,0},{3,1},{4,6},{5,7},{6,4},{7,5},{8,10},{9,11},{10,... | collective-permute-start | bytes 1572872 | tf_op jit(solution)/shard_map/ppermute | solution.py:25
  757.4 32.4 %collective-permute-start.17 = (bf16[2,512,256]{2,1,0:T(8,128)(2,1)S(1)}, bf16[2,512,256]{2,1,0:T(8,128)(2,1)S(1)}, u32[]{:S(2)}, u32[]{:S(2)}) collective-permute-start(bf16[2,512,256]{2,1,0:T(8,128)(2,1)S(1)} %copy-done.4), channel_id=1, source_target_pairs={{0,3},{1,2},{2,1},{3,0},{4,7},{5,6},{6,5},{7,4},{8,11},{9,10},{10,... | collective-permute-start | bytes 1572872 | tf_op jit(solution)/shard_map/ppermute | solution.py:25
  764.9 101.3 %collective-permute-start.12 = (bf16[2,512,256]{2,1,0:T(8,128)(2,1)}, bf16[2,512,256]{2,1,0:T(8,128)(2,1)}, u32[]{:S(2)}, u32[]{:S(2)}) collective-permute-start(bf16[2,512,256]{2,1,0:T(8,128)(2,1)} %pick_output_1_7.1), channel_id=1, source_target_pairs={{0,1},{1,0},{2,3},{3,2},{4,5},{5,4},{6,7},{7,6},{8,9},{9,8},{10,11... | collective-permute-start | bytes 1572872 | tf_op jit(solution)/shard_map/ppermute | solution.py:25
  767.2 98.9 %collective-permute-start.13 = (bf16[2,512,256]{2,1,0:T(8,128)(2,1)}, bf16[2,512,256]{2,1,0:T(8,128)(2,1)}, u32[]{:S(2)}, u32[]{:S(2)}) collective-permute-start(bf16[2,512,256]{2,1,0:T(8,128)(2,1)} %pick_output_2_7.1), channel_id=1, source_target_pairs={{0,2},{1,3},{2,0},{3,1},{4,6},{5,7},{6,4},{7,5},{8,10},{9,11},{10,... | collective-permute-start | bytes 1572872 | tf_op jit(solution)/shard_map/ppermute | solution.py:25
  777.7 70.0 %collective-permute-start.22 = (bf16[1,256,768]{2,1,0:T(8,128)(2,1)}, bf16[1,256,768]{2,1,0:T(8,128)(2,1)}, u32[]{:S(2)}, u32[]{:S(2)}) collective-permute-start(bf16[1,256,768]{2,1,0:T(8,128)(2,1)} %slice.117), channel_id=1, source_target_pairs={{0,2},{1,3},{2,0},{3,1},{4,6},{5,7},{6,4},{7,5},{8,10},{9,11},{10,... | collective-permute-start | bytes 1179656 | tf_op jit(solution)/shard_map/ppermute | solution.py:25
  778.4 83.4 %collective-permute-start.24 = (bf16[1,256,768]{2,1,0:T(8,128)(2,1)}, bf16[1,256,768]{2,1,0:T(8,128)(2,1)}, u32[]{:S(2)}, u32[]{:S(2)}) collective-permute-start(bf16[1,256,768]{2,1,0:T(8,128)(2,1)} %slice.119), channel_id=1, source_target_pairs={{0,2},{1,3},{2,0},{3,1},{4,6},{5,7},{6,4},{7,5},{8,10},{9,11},{10,... | collective-permute-start | bytes 1179656 | tf_op jit(solution)/shard_map/ppermute | solution.py:25
  789.8 73.8 %collective-permute-start.27 = (bf16[1,128,4608]{2,1,0:T(8,128)(2,1)}, bf16[1,128,4608]{2,1,0:T(8,128)(2,1)}, u32[]{:S(2)}, u32[]{:S(2)}) collective-permute-start(bf16[1,128,4608]{2,1,0:T(8,128)(2,1)} %slice.121), channel_id=1, source_target_pairs={{0,16},{4,20},{8,24},{12,28},{16,0},{20,4},{24,8},{28,12},{1,17},{... | collective-permute-start | bytes 3538952 | tf_op jit(solution)/shard_map/ppermute | solution.py:25
  847.7 18.4 %collective-permute-start.14 = (bf16[2,512,256]{2,1,0:T(8,128)(2,1)S(1)}, bf16[2,512,256]{2,1,0:T(8,128)(2,1)S(1)}, u32[]{:S(2)}, u32[]{:S(2)}) collective-permute-start(bf16[2,512,256]{2,1,0:T(8,128)(2,1)S(1)} %copy-done.16), channel_id=1, source_target_pairs={{0,3},{1,2},{2,1},{3,0},{4,7},{5,6},{6,5},{7,4},{8,11},{9,10},{10,... | collective-permute-start | bytes 1572872 | tf_op jit(solution)/shard_map/ppermute | solution.py:25
  861.7 18.0 %collective-permute-start.28 = (bf16[2,256,256]{2,1,0:T(8,128)(2,1)}, bf16[2,256,256]{2,1,0:T(8,128)(2,1)}, u32[]{:S(2)}, u32[]{:S(2)}) collective-permute-start(bf16[2,256,256]{2,1,0:T(8,128)(2,1)} %get-tuple-element.39), channel_id=1, source_target_pairs={{0,1},{1,0},{2,3},{3,2},{4,5},{5,4},{6,7},{7,6},{8,9},{9,8},{10,11... | collective-permute-start | bytes 786440 | tf_op jit(solution)/shard_map/ppermute | solution.py:25
  875.1 12.1 %collective-permute-start.30 = (bf16[2,256,256]{2,1,0:T(8,128)(2,1)}, bf16[2,256,256]{2,1,0:T(8,128)(2,1)S(1)}, u32[]{:S(2)}, u32[]{:S(2)}) collective-permute-start(bf16[2,256,256]{2,1,0:T(8,128)(2,1)} %get-tuple-element.41), channel_id=1, source_target_pairs={{0,1},{1,0},{2,3},{3,2},{4,5},{5,4},{6,7},{7,6},{8,9},{9,8},{10,11... | collective-permute-start | bytes 786440 | tf_op jit(solution)/shard_map/ppermute | solution.py:25
  (28 other events, 576.8 us)
Sparse Core Ops, SparseCore 0:
  54.8 167.4 all-gather.1

commit v4 on v3

--- a/solution.py
+++ b/solution.py
@@ -317,7 +317,7 @@
         + [pl.BlockSpec((parts, rb, tile), lambda c, i: (0, 0, c))] * nt
         + [ANY] * len(after),
         [
-            pl.BlockSpec((depth, tile), lambda c, i: (0, first + c)),
+            pl.BlockSpec((depth, tile), lambda c, i: (0, first // tile + c)),
             half_spec,
             half_spec,
         ],
@@ -392,8 +392,10 @@
     context_all = lax.all_gather(context, "dp", axis=0, tiled=True)
 
     cols = blocks.shape[2]
-    tile = cols // 8
+    tile = max(128, cols // 16)
     chunks = ((0, 3), (3, 3), (6, 1), (7, 1))
+    if cols // tile == 16:
+        chunks = ((0, 6), (6, 6), (12, 3), (15, 1))
     merged_output = None
     sums, done = [], []
     for n, (first, count) in enumerate(chunks):
@@ -420,7 +422,8 @@
             )
             projections = total_over("dp", *partial)
         merged_output, send, keep = place_output(
-            info, context_all, [got[s] for s in range(nt)], rb, merged_output, first, tile, cols, nt,
+            info, context_all, [got[s] for s in range(nt)], rb, merged_output, first * tile,
+            tile * (count if count < 6 else 2), cols, nt,
             partial[:1] if n == 1 else sums[:-1] + [projections] if last else [],
         )
         sums.append(total_over("tensor", send, keep))

time: 906 us -> 902 us (level)
  transfers between devices with their start and end apart: 34 -> 34, of which waited for: 16 -> 16; matrix products, arithmetic and copies ran while one was open for 4% -> 4% of each run, Pallas kernels for 21% -> 22%
where the time goes in v4:
time: 902 us; the launch traced here: 899 us
  waiting for transfers between devices  523 us (58%)
  Pallas kernels  199 us (22%)
  starting transfers between devices  122 us (14%)
  other arithmetic  22.9 us (3%)
  local copies, waits for them, and re-layouts  18 us (2%)
  between operations  14.4 us (2%)
    ppermute x32, waiting for transfers between devices, swap(): return lax.ppermute(x, axis, [(i, i ^ mask) for i in range(n)])  463 us
    ppermute x32, starting transfers between devices, swap(): return lax.ppermute(x, axis, [(i, i ^ mask) for i in range(n)])  116 us
    all_to_all x1, waiting for transfers between devices, body(): lax.all_to_all(outgoing, 'dp', split_axis=0, concat_axis=0, tiled=True)  60.4 us
    pallas_call x16, Pallas kernels, pick_output(): call(kernel, (parts,), [pl.BlockSpec((1, rb, width), lambda l, i: (source...  56.9 us
    pallas_call x4, Pallas kernels, place_output(): call(kernel, (width // tile,), [pl.BlockSpec((rows, depth), lambda c, i:...  45.7 us
    pallas_call x1, Pallas kernels, place_qkv(): call(kernel, (per * each,), [pl.BlockSpec((sources, some, depth), lambda...  38.7 us
    pallas_call x8, Pallas kernels, pick_query(): call(kernel, (steps,), [pl.BlockSpec((rb // steps, cols), lambda r, i: (r...  35.9 us
  transfers between devices with their start and end apart: 34, of which 16 were waited for; matrix products, arithmetic and copies ran while one was open for 4% of the time, Pallas kernels for 22%

profile of v4, /device:TPU:0, one launch (start us, length us, event | category | flops | bytes accessed | tf_op | source)
XLA Modules:
  0.0 899.4 jit_solution(3024921374622748413)
XLA Ops:
  8.4 4.7 pack_key_value.1
  13.2 5.0 collective-permute-start.2
  18.8 16.9 %split_columns.1 = bf16[8,672,2048]{2,1,0:T(8,128)(2,1)} custom-call(s32[10]{0:T(128)} %pad_add_fusion.info_ref, bf16[512,16384]{1,0:T(8,128)(2,1)} %w.1, bf16[128,16384]{1,0:T(8,128)(2,1)} %t.1, bf16[64,512]{1,0:T(8,128)(2,1)} %bitcast.42, bf16[64,512]{1,0:T(8,128)(2,1)} %refs_1_.1), custom_call_target="tpu_custom_call" | custom-call | flops 1000000000 | tf_op jit(solution)/shard_map/split_columns/pallas_call | solution.py:144
  35.7 6.1 all-to-all-start
  41.9 4.5 pick_query_2_0.1
  48.7 4.5 pick_query_3_0.1
  54.7 110.6 %collective-permute-done.1.refs_1_.refs_11_ = bf16[640,512]{1,0:T(8,128)(2,1)S(1)} collective-permute-done((bf16[640,512]{1,0:T(8,128)(2,1)}, bf16[640,512]{1,0:T(8,128)(2,1)S(1)}, u32[]{:S(2)}, u32[]{:S(2)}) %collective-permute-start.1) | collective-permute-done | bytes 655392 | tf_op jit(solution)/shard_map/ppermute | solution.py:25
  171.4 4.5 pick_query_1_1.1
  177.9 4.5 pick_query_2_1.1
  183.6 4.5 pick_query_3_1.1
  188.1 22.3 %collective-permute-done.4.refs_15_.refs_3_ = bf16[512,2048]{1,0:T(8,128)(2,1)} collective-permute-done((bf16[512,2048]{1,0:T(8,128)(2,1)}, bf16[512,2048]{1,0:T(8,128)(2,1)}, u32[]{:S(2)}, u32[]{:S(2)}) %collective-permute-start.4) | collective-permute-done | bytes 2097184 | tf_op jit(solution)/shard_map/ppermute | solution.py:25
  219.7 35.5 %collective-permute-done.3.refs_14_.refs_2_ = bf16[512,2048]{1,0:T(8,128)(2,1)S(1)} collective-permute-done((bf16[512,2048]{1,0:T(8,128)(2,1)}, bf16[512,2048]{1,0:T(8,128)(2,1)S(1)}, u32[]{:S(2)}, u32[]{:S(2)}) %collective-permute-start.3) | collective-permute-done | bytes 2097184 | tf_op jit(solution)/shard_map/ppermute | solution.py:25
  255.3 60.4 %all-to-all-done.x.refs_0_.refs_1_.refs_2_.refs_3_.refs_4_.refs_5_.refs_6_.refs_7_.a = bf16[8,672,2048]{2,1,0:T(8,128)(2,1)} async-done(((bf16[8,672,2048]{2,1,0:T(8,128)(2,1)}), bf16[8,672,2048]{2,1,0:T(8,128)(2,1)}, u32[]{:S(2)}, u32[]{:S(2)}) %all-to-all-start) | async-done | bytes 22020128 | tf_op jit(solution)/shard_map/all_to_all | solution.py:379
  327.5 138.6 %collective-permute-done.7.refs_18_.refs_7_ = bf16[512,2048]{1,0:T(8,128)(2,1)} collective-permute-done((bf16[512,2048]{1,0:T(8,128)(2,1)}, bf16[512,2048]{1,0:T(8,128)(2,1)}, u32[]{:S(2)}, u32[]{:S(2)}) %collective-permute-start.7) | collective-permute-done | bytes 2097184 | tf_op jit(solution)/shard_map/ppermute | solution.py:25
  469.9 45.6 %collective-permute-start.9 = (bf16[2,576,768]{2,1,0:T(8,128)(2,1)}, bf16[2,576,768]{2,1,0:T(8,128)(2,1)}, u32[]{:S(2)}, u32[]{:S(2)}) collective-permute-start(bf16[2,576,768]{2,1,0:T(8,128)(2,1)} %pick_output_1_0.1), channel_id=1, source_target_pairs={{0,1},{1,0},{2,3},{3,2},{4,5},{5,4},{6,7},{7,6},{8,9},{9,8},{10,11... | collective-permute-start | bytes 5308424 | tf_op jit(solution)/shard_map/ppermute | solution.py:25
  515.5 4.5 pick_query_0_0.1.refs_1_
  519.9 4.6 pick_query_0_1.1.refs_5_
  557.4 31.1 %collective-permute-done.10.refs_11_.refs_2_ = bf16[2,576,768]{2,1,0:T(8,128)(2,1)} collective-permute-done((bf16[2,576,768]{2,1,0:T(8,128)(2,1)}, bf16[2,576,768]{2,1,0:T(8,128)(2,1)}, u32[]{:S(2)}, u32[]{:S(2)}) %collective-permute-start.10) | collective-permute-done | bytes 1769504 | tf_op jit(solution)/shard_map/ppermute | solution.py:25
  589.4 6.5 collective-permute-done.9.refs_13_.refs_1_
  597.7 38.7 %place_qkv.1 = (bf16[2048,4608]{1,0:T(8,128)(2,1)}, bf16[4,128,4608]{2,1,0:T(8,128)(2,1)}, bf16[4,128,4608]{2,1,0:T(8,128)(2,1)}) custom-call(s32[10]{0:T(128)} %pad_add_fusion.info_ref, bf16[8,672,2048]{2,1,0:T(8,128)(2,1)} %all-to-all-done.x.refs_0_.refs_1_.refs_2_.refs_3_.refs_4_.refs_5_.refs_6_.refs_7_.a, bf16[4,64,512]{2,1,0:T(8,128)(2,1)} %pad_maximum_fusion.2.d, ...), custom_call_target="tpu_custom_call" | custom-call | flops 1000000000 | tf_op jit(solution)/shard_map/place_qkv/pallas_call | solution.py:261
  636.5 13.6 %place_output_0.1 = (bf16[4096,2048]{1,0:T(8,128)(2,1)}, bf16[2,256,768]{2,1,0:T(8,128)(2,1)}, bf16[2,256,768]{2,1,0:T(8,128)(2,1)}) custom-call(s32[10]{0:T(128)} %pad_add_fusion.info_ref, bf16[1024,4096]{1,0:T(8,128)(2,1)} %all-gather.2.cloned.1.call-done.a, bf16[2,576,768]{2,1,0:T(8,128)(2,1)} %pick_output_0_0.1.refs_0_, ...), custom_call_target="tpu_custom_call" | custom-call | flops 199999995904 | tf_op jit(solution)/shard_map/place_output_0/pallas_call | solution.py:313
  650.1 5.0 add_convert_fusion
  659.4 35.0 %collective-permute-done.18.refs_1_ = bf16[2,512,768]{2,1,0:T(8,128)(2,1)} collective-permute-done((bf16[2,512,768]{2,1,0:T(8,128)(2,1)}, bf16[2,512,768]{2,1,0:T(8,128)(2,1)}, u32[]{:S(2)}, u32[]{:S(2)}) %collective-permute-start.18) | collective-permute-done | bytes 1572896 | tf_op jit(solution)/shard_map/ppermute | solution.py:25
  694.3 13.6 %place_output_768.1 = (bf16[4096,2048]{1,0:T(8,128)(2,1)}, bf16[2,256,768]{2,1,0:T(8,128)(2,1)}, bf16[2,256,768]{2,1,0:T(8,128)(2,1)}) custom-call(s32[10]{0:T(128)} %pad_add_fusion.info_ref, bf16[1024,4096]{1,0:T(8,128)(2,1)} %all-gather.2.cloned.1.call-done.a, bf16[2,512,768]{2,1,0:T(8,128)(2,1)} %pick_output_0_6.1.refs_0_, ...), custom_call_target="tpu_custom_call", output_to_operand_aliasing={{0}: (6, {})} | custom-call | flops 199999995904 | tf_op jit(solution)/shard_map/place_output_768/pallas_call | solution.py:313
  707.9 27.0 %collective-permute-start.23 = (bf16[2,256,768]{2,1,0:T(8,128)(2,1)}, bf16[2,256,768]{2,1,0:T(8,128)(2,1)}, u32[]{:S(2)}, u32[]{:S(2)}) collective-permute-start(bf16[2,256,768]{2,1,0:T(8,128)(2,1)} %get-tuple-element.35), channel_id=1, source_target_pairs={{0,1},{1,0},{2,3},{3,2},{4,5},{5,4},{6,7},{7,6},{8,9},{9,8},{10,11... | collective-permute-start | bytes 2359304 | tf_op jit(solution)/shard_map/ppermute | solution.py:25
  761.1 9.4 %collective-permute-done.23 = bf16[2,256,768]{2,1,0:T(8,128)(2,1)} collective-permute-done((bf16[2,256,768]{2,1,0:T(8,128)(2,1)}, bf16[2,256,768]{2,1,0:T(8,128)(2,1)}, u32[]{:S(2)}, u32[]{:S(2)}) %collective-permute-start.23) | collective-permute-done | bytes 786464 | tf_op jit(solution)/shard_map/ppermute | solution.py:25
  779.3 9.7 %collective-permute-done.15.refs_1_ = bf16[2,512,384]{2,1,0:T(8,128)(2,1)} collective-permute-done((bf16[2,512,384]{2,1,0:T(8,128)(2,1)}, bf16[2,512,384]{2,1,0:T(8,128)(2,1)}, u32[]{:S(2)}, u32[]{:S(2)}) %collective-permute-start.15) | collective-permute-done | bytes 786464 | tf_op jit(solution)/shard_map/ppermute | solution.py:25
  791.9 14.8 %collective-permute-done.17.refs_3_ = bf16[2,512,384]{2,1,0:T(8,128)(2,1)S(1)} collective-permute-done((bf16[2,512,384]{2,1,0:T(8,128)(2,1)S(1)}, bf16[2,512,384]{2,1,0:T(8,128)(2,1)S(1)}, u32[]{:S(2)}, u32[]{:S(2)}) %collective-permute-start.17) | collective-permute-done | bytes 786464 | tf_op jit(solution)/shard_map/ppermute | solution.py:25
  808.2 10.9 %place_output_1536.1 = (bf16[4096,2048]{1,0:T(8,128)(2,1)}, bf16[2,256,384]{2,1,0:T(8,128)(2,1)}, bf16[2,256,384]{2,1,0:T(8,128)(2,1)}) custom-call(s32[10]{0:T(128)} %pad_add_fusion.info_ref, bf16[1024,4096]{1,0:T(8,128)(2,1)} %all-gather.2.cloned.1.call-done.a, bf16[2,512,384]{2,1,0:T(8,128)(2,1)} %pick_output_0_12.1.refs_0_, ...), custom_call_target="tpu_custom_call", output_to_operand_aliasing={{0}: (6, {})} | custom-call | flops 199999995904 | tf_op jit(solution)/shard_map/place_output_1536/pallas_call | solution.py:313
  819.1 31.3 %collective-permute-done.22 = bf16[1,256,768]{2,1,0:T(8,128)(2,1)} collective-permute-done((bf16[1,256,768]{2,1,0:T(8,128)(2,1)}, bf16[1,256,768]{2,1,0:T(8,128)(2,1)}, u32[]{:S(2)}, u32[]{:S(2)}) %collective-permute-start.22) | collective-permute-done | bytes 393248 | tf_op jit(solution)/shard_map/ppermute | solution.py:25
  854.7 9.8 %collective-permute-done.24 = bf16[1,256,768]{2,1,0:T(8,128)(2,1)} collective-permute-done((bf16[1,256,768]{2,1,0:T(8,128)(2,1)}, bf16[1,256,768]{2,1,0:T(8,128)(2,1)}, u32[]{:S(2)}, u32[]{:S(2)}) %collective-permute-start.24) | collective-permute-done | bytes 393248 | tf_op jit(solution)/shard_map/ppermute | solution.py:25
  869.6 7.6 place_output_1920.1
  (151 shorter events, 144.2 us)
Async XLA Ops:
  13.2 41.5 %collective-permute-start.2 = (bf16[640,512]{1,0:T(8,128)(2,1)}, bf16[640,512]{1,0:T(8,128)(2,1)S(1)}, u32[]{:S(2)}, u32[]{:S(2)}) collective-permute-start(bf16[640,512]{1,0:T(8,128)(2,1)} %get-tuple-element.26), channel_id=1, source_target_pairs={{0,3},{1,2},{2,1},{3,0},{4,7},{5,6},{6,5},{7,4},{8,11},{9,10},{10,... | collective-permute-start | bytes 1966088 | tf_op jit(solution)/shard_map/ppermute | solution.py:25
  18.2 147.1 %collective-permute-start.1 = (bf16[640,512]{1,0:T(8,128)(2,1)}, bf16[640,512]{1,0:T(8,128)(2,1)S(1)}, u32[]{:S(2)}, u32[]{:S(2)}) collective-permute-start(bf16[640,512]{1,0:T(8,128)(2,1)} %get-tuple-element.25), channel_id=1, source_target_pairs={{0,2},{1,3},{2,0},{3,1},{4,6},{5,7},{6,4},{7,5},{8,10},{9,11},{10,... | collective-permute-start | bytes 1966088 | tf_op jit(solution)/shard_map/ppermute | solution.py:25
  18.2 147.1 %collective-permute-start = (bf16[640,512]{1,0:T(8,128)(2,1)}, bf16[640,512]{1,0:T(8,128)(2,1)S(1)}, u32[]{:S(2)}, u32[]{:S(2)}) collective-permute-start(bf16[640,512]{1,0:T(8,128)(2,1)} %get-tuple-element.24), channel_id=1, source_target_pairs={{0,1},{1,0},{2,3},{3,2},{4,5},{5,4},{6,7},{7,6},{8,9},{9,8},{10,11... | collective-permute-start | bytes 1966088 | tf_op jit(solution)/shard_map/ppermute | solution.py:25
  35.7 280.0 %all-to-all-start = ((bf16[8,672,2048]{2,1,0:T(8,128)(2,1)}), bf16[8,672,2048]{2,1,0:T(8,128)(2,1)}, u32[]{:S(2)}, u32[]{:S(2)}) async-start(bf16[8,672,2048]{2,1,0:T(8,128)(2,1)} %split_columns.1), calls=%async_computation | async-start | bytes 44040192 | tf_op jit(solution)/shard_map/all_to_all | solution.py:379
  41.8 594.6 %all-gather.2.cloned.1.call-start = ((), (), s32[]{:S(2)}) async-start(), calls=%async_computation.1 | async-start | bytes 9437184 | tf_op jit(solution)/shard_map/all_gather | solution.py:392
  46.4 164.0 %collective-permute-start.4 = (bf16[512,2048]{1,0:T(8,128)(2,1)}, bf16[512,2048]{1,0:T(8,128)(2,1)}, u32[]{:S(2)}, u32[]{:S(2)}) collective-permute-start(bf16[512,2048]{1,0:T(8,128)(2,1)} %pick_query_2_0.1), channel_id=1, source_target_pairs={{0,2},{1,3},{2,0},{3,1},{4,6},{5,7},{6,4},{7,5},{8,10},{9,11},{10,... | collective-permute-start | bytes 6291464 | tf_op jit(solution)/shard_map/ppermute | solution.py:25
  53.2 166.5 %collective-permute-start.5 = (bf16[512,2048]{1,0:T(8,128)(2,1)}, bf16[512,2048]{1,0:T(8,128)(2,1)}, u32[]{:S(2)}, u32[]{:S(2)}) collective-permute-start(bf16[512,2048]{1,0:T(8,128)(2,1)} %pick_query_3_0.1), channel_id=1, source_target_pairs={{0,3},{1,2},{2,1},{3,0},{4,7},{5,6},{6,5},{7,4},{8,11},{9,10},{10,... | collective-permute-start | bytes 6291464 | tf_op jit(solution)/shard_map/ppermute | solution.py:25
  171.4 83.8 %collective-permute-start.3 = (bf16[512,2048]{1,0:T(8,128)(2,1)}, bf16[512,2048]{1,0:T(8,128)(2,1)S(1)}, u32[]{:S(2)}, u32[]{:S(2)}) collective-permute-start(bf16[512,2048]{1,0:T(8,128)(2,1)} %pick_query_1_0.1), channel_id=1, source_target_pairs={{0,1},{1,0},{2,3},{3,2},{4,5},{5,4},{6,7},{7,6},{8,9},{9,8},{10,11... | collective-permute-start | bytes 6291464 | tf_op jit(solution)/shard_map/ppermute | solution.py:25
  175.9 151.6 %collective-permute-start.6 = (bf16[512,2048]{1,0:T(8,128)(2,1)}, bf16[512,2048]{1,0:T(8,128)(2,1)}, u32[]{:S(2)}, u32[]{:S(2)}) collective-permute-start(bf16[512,2048]{1,0:T(8,128)(2,1)} %pick_query_1_1.1), channel_id=1, source_target_pairs={{0,1},{1,0},{2,3},{3,2},{4,5},{5,4},{6,7},{7,6},{8,9},{9,8},{10,11... | collective-permute-start | bytes 6291464 | tf_op jit(solution)/shard_map/ppermute | solution.py:25
  182.4 283.6 %collective-permute-start.7 = (bf16[512,2048]{1,0:T(8,128)(2,1)}, bf16[512,2048]{1,0:T(8,128)(2,1)}, u32[]{:S(2)}, u32[]{:S(2)}) collective-permute-start(bf16[512,2048]{1,0:T(8,128)(2,1)} %pick_query_2_1.1), channel_id=1, source_target_pairs={{0,2},{1,3},{2,0},{3,1},{4,6},{5,7},{6,4},{7,5},{8,10},{9,11},{10,... | collective-permute-start | bytes 6291464 | tf_op jit(solution)/shard_map/ppermute | solution.py:25
  210.4 255.7 %collective-permute-start.8 = (bf16[512,2048]{1,0:T(8,128)(2,1)}, bf16[512,2048]{1,0:T(8,128)(2,1)}, u32[]{:S(2)}, u32[]{:S(2)}) collective-permute-start(bf16[512,2048]{1,0:T(8,128)(2,1)} %pick_query_3_1.1), channel_id=1, source_target_pairs={{0,3},{1,2},{2,1},{3,0},{4,7},{5,6},{6,5},{7,4},{8,11},{9,10},{10,... | collective-permute-start | bytes 6291464 | tf_op jit(solution)/shard_map/ppermute | solution.py:25
  319.6 235.7 %collective-permute-start.11 = (bf16[2,576,768]{2,1,0:T(8,128)(2,1)}, bf16[2,576,768]{2,1,0:T(8,128)(2,1)}, u32[]{:S(2)}, u32[]{:S(2)}) collective-permute-start(bf16[2,576,768]{2,1,0:T(8,128)(2,1)} %pick_output_3_0.1), channel_id=1, source_target_pairs={{0,3},{1,2},{2,1},{3,0},{4,7},{5,6},{6,5},{7,4},{8,11},{9,10},{10,... | collective-permute-start | bytes 5308424 | tf_op jit(solution)/shard_map/ppermute | solution.py:25
  327.4 261.1 %collective-permute-start.10 = (bf16[2,576,768]{2,1,0:T(8,128)(2,1)}, bf16[2,576,768]{2,1,0:T(8,128)(2,1)}, u32[]{:S(2)}, u32[]{:S(2)}) collective-permute-start(bf16[2,576,768]{2,1,0:T(8,128)(2,1)} %pick_output_2_0.1), channel_id=1, source_target_pairs={{0,2},{1,3},{2,0},{3,1},{4,6},{5,7},{6,4},{7,5},{8,10},{9,11},{10,... | collective-permute-start | bytes 5308424 | tf_op jit(solution)/shard_map/ppermute | solution.py:25
  469.9 126.0 %collective-permute-start.9 = (bf16[2,576,768]{2,1,0:T(8,128)(2,1)}, bf16[2,576,768]{2,1,0:T(8,128)(2,1)}, u32[]{:S(2)}, u32[]{:S(2)}) collective-permute-start(bf16[2,576,768]{2,1,0:T(8,128)(2,1)} %pick_output_1_0.1), channel_id=1, source_target_pairs={{0,1},{1,0},{2,3},{3,2},{4,5},{5,4},{6,7},{7,6},{8,9},{9,8},{10,11... | collective-permute-start | bytes 5308424 | tf_op jit(solution)/shard_map/ppermute | solution.py:25
  529.2 165.2 %collective-permute-start.18 = (bf16[2,512,768]{2,1,0:T(8,128)(2,1)}, bf16[2,512,768]{2,1,0:T(8,128)(2,1)}, u32[]{:S(2)}, u32[]{:S(2)}) collective-permute-start(bf16[2,512,768]{2,1,0:T(8,128)(2,1)} %pick_output_1_6.1), channel_id=1, source_target_pairs={{0,1},{1,0},{2,3},{3,2},{4,5},{5,4},{6,7},{7,6},{8,9},{9,8},{10,11... | collective-permute-start | bytes 4718600 | tf_op jit(solution)/shard_map/ppermute | solution.py:25
  533.1 161.2 %collective-permute-start.19 = (bf16[2,512,768]{2,1,0:T(8,128)(2,1)}, bf16[2,512,768]{2,1,0:T(8,128)(2,1)}, u32[]{:S(2)}, u32[]{:S(2)}) collective-permute-start(bf16[2,512,768]{2,1,0:T(8,128)(2,1)} %pick_output_2_6.1), channel_id=1, source_target_pairs={{0,2},{1,3},{2,0},{3,1},{4,6},{5,7},{6,4},{7,5},{8,10},{9,11},{10,... | collective-permute-start | bytes 4718600 | tf_op jit(solution)/shard_map/ppermute | solution.py:25
  555.3 139.1 %collective-permute-start.20 = (bf16[2,512,768]{2,1,0:T(8,128)(2,1)}, bf16[2,512,768]{2,1,0:T(8,128)(2,1)}, u32[]{:S(2)}, u32[]{:S(2)}) collective-permute-start(bf16[2,512,768]{2,1,0:T(8,128)(2,1)} %pick_output_3_6.1), channel_id=1, source_target_pairs={{0,3},{1,2},{2,1},{3,0},{4,7},{5,6},{6,5},{7,4},{8,11},{9,10},{10,... | collective-permute-start | bytes 4718600 | tf_op jit(solution)/shard_map/ppermute | solution.py:25
  636.4 13.7 %collective-permute-start.25 = (bf16[4,128,4608]{2,1,0:T(8,128)(2,1)}, bf16[4,128,4608]{2,1,0:T(8,128)(2,1)}, u32[]{:S(2)}, u32[]{:S(2)}) collective-permute-start(bf16[4,128,4608]{2,1,0:T(8,128)(2,1)} %get-tuple-element.29.refs_5_), channel_id=1, source_target_pairs={{0,4},{4,0},{8,12},{12,8},{16,20},{20,16},{24,28},{28,24},{1,5},{5... | collective-permute-start | bytes 14155784 | tf_op jit(solution)/shard_map/ppermute | solution.py:25
  650.0 107.4 %collective-permute-start.21 = (bf16[2,256,768]{2,1,0:T(8,128)(2,1)}, bf16[2,256,768]{2,1,0:T(8,128)(2,1)}, u32[]{:S(2)}, u32[]{:S(2)}) collective-permute-start(bf16[2,256,768]{2,1,0:T(8,128)(2,1)} %get-tuple-element.33), channel_id=1, source_target_pairs={{0,1},{1,0},{2,3},{3,2},{4,5},{5,4},{6,7},{7,6},{8,9},{9,8},{10,11... | collective-permute-start | bytes 2359304 | tf_op jit(solution)/shard_map/ppermute | solution.py:25
  657.9 114.8 %collective-permute-start.26 = (bf16[2,128,4608]{2,1,0:T(8,128)(2,1)}, bf16[2,128,4608]{2,1,0:T(8,128)(2,1)}, u32[]{:S(2)}, u32[]{:S(2)}) collective-permute-start(bf16[2,128,4608]{2,1,0:T(8,128)(2,1)} %slice.99), channel_id=1, source_target_pairs={{0,8},{4,12},{8,0},{12,4},{16,24},{20,28},{24,16},{28,20},{1,9},{5... | collective-permute-start | bytes 7077896 | tf_op jit(solution)/shard_map/ppermute | solution.py:25
  707.9 62.6 %collective-permute-start.23 = (bf16[2,256,768]{2,1,0:T(8,128)(2,1)}, bf16[2,256,768]{2,1,0:T(8,128)(2,1)}, u32[]{:S(2)}, u32[]{:S(2)}) collective-permute-start(bf16[2,256,768]{2,1,0:T(8,128)(2,1)} %get-tuple-element.35), channel_id=1, source_target_pairs={{0,1},{1,0},{2,3},{3,2},{4,5},{5,4},{6,7},{7,6},{8,9},{9,8},{10,11... | collective-permute-start | bytes 2359304 | tf_op jit(solution)/shard_map/ppermute | solution.py:25
  738.2 50.7 %collective-permute-start.15 = (bf16[2,512,384]{2,1,0:T(8,128)(2,1)}, bf16[2,512,384]{2,1,0:T(8,128)(2,1)}, u32[]{:S(2)}, u32[]{:S(2)}) collective-permute-start(bf16[2,512,384]{2,1,0:T(8,128)(2,1)} %pick_output_1_12.1.refs_11_), channel_id=1, source_target_pairs={{0,1},{1,0},{2,3},{3,2},{4,5},{5,4},{6,7},{7,6},{8,9},{9,8},{10,11... | collective-permute-start | bytes 2359304 | tf_op jit(solution)/shard_map/ppermute | solution.py:25
  741.6 48.1 %collective-permute-start.16 = (bf16[2,512,384]{2,1,0:T(8,128)(2,1)}, bf16[2,512,384]{2,1,0:T(8,128)(2,1)}, u32[]{:S(2)}, u32[]{:S(2)}) collective-permute-start(bf16[2,512,384]{2,1,0:T(8,128)(2,1)} %pick_output_2_12.1.refs_9_), channel_id=1, source_target_pairs={{0,2},{1,3},{2,0},{3,1},{4,6},{5,7},{6,4},{7,5},{8,10},{9,11},{10,... | collective-permute-start | bytes 2359304 | tf_op jit(solution)/shard_map/ppermute | solution.py:25
  757.5 49.2 %collective-permute-start.17 = (bf16[2,512,384]{2,1,0:T(8,128)(2,1)S(1)}, bf16[2,512,384]{2,1,0:T(8,128)(2,1)S(1)}, u32[]{:S(2)}, u32[]{:S(2)}) collective-permute-start(bf16[2,512,384]{2,1,0:T(8,128)(2,1)S(1)} %copy-done.2), channel_id=1, source_target_pairs={{0,3},{1,2},{2,1},{3,0},{4,7},{5,6},{6,5},{7,4},{8,11},{9,10},{10,... | collective-permute-start | bytes 2359304 | tf_op jit(solution)/shard_map/ppermute | solution.py:25
  770.5 98.4 %collective-permute-start.12 = (bf16[2,512,128]{2,1,0:T(8,128)(2,1)}, bf16[2,512,128]{2,1,0:T(8,128)(2,1)}, u32[]{:S(2)}, u32[]{:S(2)}) collective-permute-start(bf16[2,512,128]{2,1,0:T(8,128)(2,1)} %pick_output_1_15.1), channel_id=1, source_target_pairs={{0,1},{1,0},{2,3},{3,2},{4,5},{5,4},{6,7},{7,6},{8,9},{9,8},{10,11... | collective-permute-start | bytes 786440 | tf_op jit(solution)/shard_map/ppermute | solution.py:25
  772.9 96.0 %collective-permute-start.13 = (bf16[2,512,128]{2,1,0:T(8,128)(2,1)}, bf16[2,512,128]{2,1,0:T(8,128)(2,1)}, u32[]{:S(2)}, u32[]{:S(2)}) collective-permute-start(bf16[2,512,128]{2,1,0:T(8,128)(2,1)} %pick_output_2_15.1), channel_id=1, source_target_pairs={{0,2},{1,3},{2,0},{3,1},{4,6},{5,7},{6,4},{7,5},{8,10},{9,11},{10,... | collective-permute-start | bytes 786440 | tf_op jit(solution)/shard_map/ppermute | solution.py:25
  789.0 61.5 %collective-permute-start.22 = (bf16[1,256,768]{2,1,0:T(8,128)(2,1)}, bf16[1,256,768]{2,1,0:T(8,128)(2,1)}, u32[]{:S(2)}, u32[]{:S(2)}) collective-permute-start(bf16[1,256,768]{2,1,0:T(8,128)(2,1)} %slice.117), channel_id=1, source_target_pairs={{0,2},{1,3},{2,0},{3,1},{4,6},{5,7},{6,4},{7,5},{8,10},{9,11},{10,... | collective-permute-start | bytes 1179656 | tf_op jit(solution)/shard_map/ppermute | solution.py:25
  789.6 74.8 %collective-permute-start.24 = (bf16[1,256,768]{2,1,0:T(8,128)(2,1)}, bf16[1,256,768]{2,1,0:T(8,128)(2,1)}, u32[]{:S(2)}, u32[]{:S(2)}) collective-permute-start(bf16[1,256,768]{2,1,0:T(8,128)(2,1)} %slice.119), channel_id=1, source_target_pairs={{0,2},{1,3},{2,0},{3,1},{4,6},{5,7},{6,4},{7,5},{8,10},{9,11},{10,... | collective-permute-start | bytes 1179656 | tf_op jit(solution)/shard_map/ppermute | solution.py:25
  806.6 59.7 %collective-permute-start.27 = (bf16[1,128,4608]{2,1,0:T(8,128)(2,1)}, bf16[1,128,4608]{2,1,0:T(8,128)(2,1)}, u32[]{:S(2)}, u32[]{:S(2)}) collective-permute-start(bf16[1,128,4608]{2,1,0:T(8,128)(2,1)} %slice.121), channel_id=1, source_target_pairs={{0,16},{4,20},{8,24},{12,28},{16,0},{20,4},{24,8},{28,12},{1,17},{... | collective-permute-start | bytes 3538952 | tf_op jit(solution)/shard_map/ppermute | solution.py:25
  850.4 18.5 %collective-permute-start.14 = (bf16[2,512,128]{2,1,0:T(8,128)(2,1)S(1)}, bf16[2,512,128]{2,1,0:T(8,128)(2,1)S(1)}, u32[]{:S(2)}, u32[]{:S(2)}) collective-permute-start(bf16[2,512,128]{2,1,0:T(8,128)(2,1)S(1)} %copy-done.17), channel_id=1, source_target_pairs={{0,3},{1,2},{2,1},{3,0},{4,7},{5,6},{6,5},{7,4},{8,11},{9,10},{10,... | collective-permute-start | bytes 786440 | tf_op jit(solution)/shard_map/ppermute | solution.py:25
  864.5 14.8 %collective-permute-start.28 = (bf16[2,256,384]{2,1,0:T(8,128)(2,1)}, bf16[2,256,384]{2,1,0:T(8,128)(2,1)}, u32[]{:S(2)}, u32[]{:S(2)}) collective-permute-start(bf16[2,256,384]{2,1,0:T(8,128)(2,1)} %get-tuple-element.39), channel_id=1, source_target_pairs={{0,1},{1,0},{2,3},{3,2},{4,5},{5,4},{6,7},{7,6},{8,9},{9,8},{10,11... | collective-permute-start | bytes 1179656 | tf_op jit(solution)/shard_map/ppermute | solution.py:25
  880.4 8.7 collective-permute-start.29
  (28 other events, 547.4 us)
Sparse Core Ops, SparseCore 0:
  54.8 167.4 all-gather.1

commit v5 on v4

--- a/solution.py
+++ b/solution.py
@@ -398,6 +398,7 @@
         chunks = ((0, 6), (6, 6), (12, 3), (15, 1))
     merged_output = None
     sums, done = [], []
+    picks, arrived = [], []
     for n, (first, count) in enumerate(chunks):
         last = n == len(chunks) - 1
         sent = {}
@@ -413,8 +414,12 @@
                 info, blocks, rb, output_ups, s, first, count, tile, per, dpg, after
             )
         picked = [sent[s] for s in order if s]
+        picks.append(picked)
         got = exchange(sent)
+        arrived.append(got)
         done.append([got[s] for s in order if s])
+    for n, (first, count) in enumerate(chunks):
+        last, got = n == len(chunks) - 1, arrived[n]
         if n == 0:
             query_ups = jnp.stack([got[s][:, rb:, :cb] for s in range(nt)])
             merged_qkv, *partial = place_qkv(
@@ -424,7 +429,7 @@
         merged_output, send, keep = place_output(
             info, context_all, [got[s] for s in range(nt)], rb, merged_output, first * tile,
             tile * (count if count < 6 else 2), cols, nt,
-            partial[:1] if n == 1 else sums[:-1] + [projections] if last else [],
+            partial[:1] + picks[2] if n == 1 else sums[:-1] + [projections] if last else [],
         )
         sums.append(total_over("tensor", send, keep))
     attention_output = jnp.concatenate(sums, axis=1)

time: 902 us -> 901 us (level)
  starting transfers between devices: 122 us -> 133 us
  waiting for transfers between devices: 523 us -> 512 us
    ppermute x32, starting transfers between devices: 116 us -> 127 us  [swap(): return lax.ppermute(x, axis, [(i, i ^ mask) for i in range(n)])]
    ppermute x32, waiting for transfers between devices: 463 us -> 452 us  [swap(): return lax.ppermute(x, axis, [(i, i ^ mask) for i in range(n)])]
where the time goes in v5:
time: 901 us; the launch traced here: 899 us
  waiting for transfers between devices  512 us (57%)
  Pallas kernels  199 us (22%)
  starting transfers between devices  133 us (15%)
  other arithmetic  21.5 us (2%)
  local copies, waits for them, and re-layouts  18.2 us (2%)
  between operations  14.4 us (2%)
    ppermute x32, waiting for transfers between devices, swap(): return lax.ppermute(x, axis, [(i, i ^ mask) for i in range(n)])  452 us
    ppermute x32, starting transfers between devices, swap(): return lax.ppermute(x, axis, [(i, i ^ mask) for i in range(n)])  127 us
    all_to_all x1, waiting for transfers between devices, body(): lax.all_to_all(outgoing, 'dp', split_axis=0, concat_axis=0, tiled=True)  60.4 us
    pallas_call x16, Pallas kernels, pick_output(): call(kernel, (parts,), [pl.BlockSpec((1, rb, width), lambda l, i: (source...  57.5 us
    pallas_call x4, Pallas kernels, place_output(): call(kernel, (width // tile,), [pl.BlockSpec((rows, depth), lambda c, i:...  45.5 us
    pallas_call x1, Pallas kernels, place_qkv(): call(kernel, (per * each,), [pl.BlockSpec((sources, some, depth), lambda...  38.7 us
    pallas_call x8, Pallas kernels, pick_query(): call(kernel, (steps,), [pl.BlockSpec((rb // steps, cols), lambda r, i: (r...  36 us
  transfers between devices with their start and end apart: 34, of which 16 were waited for; matrix products, arithmetic and copies ran while one was open for 4% of the time, Pallas kernels for 22%

profile of v5, /device:TPU:0, one launch (start us, length us, event | category | flops | bytes accessed | tf_op | source)
XLA Modules:
  0.0 899.0 jit_solution(18101653329351142811)
XLA Ops:
  8.5 4.7 pack_key_value.1
  13.2 5.1 collective-permute-start.2
  18.8 16.9 %split_columns.1 = bf16[8,672,2048]{2,1,0:T(8,128)(2,1)} custom-call(s32[10]{0:T(128)} %pad_add_fusion.info_ref, bf16[512,16384]{1,0:T(8,128)(2,1)} %w.1, bf16[128,16384]{1,0:T(8,128)(2,1)} %t.1, bf16[64,512]{1,0:T(8,128)(2,1)} %bitcast.44, bf16[64,512]{1,0:T(8,128)(2,1)} %refs_1_.1), custom_call_target="tpu_custom_call" | custom-call | flops 1000000000 | tf_op jit(solution)/shard_map/split_columns/pallas_call | solution.py:144
  35.7 6.1 all-to-all-start
  41.9 4.5 pick_query_2_0.1
  48.7 4.5 pick_query_3_0.1
  54.7 110.6 %collective-permute-done.1.refs_1_.refs_11_ = bf16[640,512]{1,0:T(8,128)(2,1)S(1)} collective-permute-done((bf16[640,512]{1,0:T(8,128)(2,1)}, bf16[640,512]{1,0:T(8,128)(2,1)S(1)}, u32[]{:S(2)}, u32[]{:S(2)}) %collective-permute-start.1) | collective-permute-done | bytes 655392 | tf_op jit(solution)/shard_map/ppermute | solution.py:25
  167.0 4.5 pick_query_1_0.1
  171.5 4.5 pick_query_1_1.1
  178.0 4.5 pick_query_2_1.1
  183.7 4.5 pick_query_3_1.1
  188.2 22.2 %collective-permute-done.4.refs_15_.refs_3_ = bf16[512,2048]{1,0:T(8,128)(2,1)} collective-permute-done((bf16[512,2048]{1,0:T(8,128)(2,1)}, bf16[512,2048]{1,0:T(8,128)(2,1)}, u32[]{:S(2)}, u32[]{:S(2)}) %collective-permute-start.4) | collective-permute-done | bytes 2097184 | tf_op jit(solution)/shard_map/ppermute | solution.py:25
  219.8 35.4 %collective-permute-done.3.refs_14_.refs_2_ = bf16[512,2048]{1,0:T(8,128)(2,1)S(1)} collective-permute-done((bf16[512,2048]{1,0:T(8,128)(2,1)}, bf16[512,2048]{1,0:T(8,128)(2,1)S(1)}, u32[]{:S(2)}, u32[]{:S(2)}) %collective-permute-start.3) | collective-permute-done | bytes 2097184 | tf_op jit(solution)/shard_map/ppermute | solution.py:25
  255.3 60.4 %all-to-all-done.x.refs_0_.refs_1_.refs_2_.refs_3_.refs_4_.refs_5_.refs_6_.refs_7_.a = bf16[8,672,2048]{2,1,0:T(8,128)(2,1)} async-done(((bf16[8,672,2048]{2,1,0:T(8,128)(2,1)}), bf16[8,672,2048]{2,1,0:T(8,128)(2,1)}, u32[]{:S(2)}, u32[]{:S(2)}) %all-to-all-start) | async-done | bytes 22020128 | tf_op jit(solution)/shard_map/all_to_all | solution.py:379
  327.5 138.6 %collective-permute-done.7.refs_18_.refs_7_ = bf16[512,2048]{1,0:T(8,128)(2,1)} collective-permute-done((bf16[512,2048]{1,0:T(8,128)(2,1)}, bf16[512,2048]{1,0:T(8,128)(2,1)}, u32[]{:S(2)}, u32[]{:S(2)}) %collective-permute-start.7) | collective-permute-done | bytes 2097184 | tf_op jit(solution)/shard_map/ppermute | solution.py:25
  469.9 45.6 %collective-permute-start.9 = (bf16[2,576,768]{2,1,0:T(8,128)(2,1)}, bf16[2,576,768]{2,1,0:T(8,128)(2,1)}, u32[]{:S(2)}, u32[]{:S(2)}) collective-permute-start(bf16[2,576,768]{2,1,0:T(8,128)(2,1)} %pick_output_1_0.1), channel_id=1, source_target_pairs={{0,1},{1,0},{2,3},{3,2},{4,5},{5,4},{6,7},{7,6},{8,9},{9,8},{10,11... | collective-permute-start | bytes 5308424 | tf_op jit(solution)/shard_map/ppermute | solution.py:25
  515.5 4.5 pick_query_0_0.1.refs_1_
  520.0 4.6 pick_query_0_1.1.refs_5_
  551.2 37.3 %collective-permute-done.10.refs_11_.refs_2_ = bf16[2,576,768]{2,1,0:T(8,128)(2,1)} collective-permute-done((bf16[2,576,768]{2,1,0:T(8,128)(2,1)}, bf16[2,576,768]{2,1,0:T(8,128)(2,1)}, u32[]{:S(2)}, u32[]{:S(2)}) %collective-permute-start.10) | collective-permute-done | bytes 1769504 | tf_op jit(solution)/shard_map/ppermute | solution.py:25
  589.4 6.5 collective-permute-done.9.refs_13_.refs_1_
  597.8 38.7 %place_qkv.1 = (bf16[2048,4608]{1,0:T(8,128)(2,1)}, bf16[4,128,4608]{2,1,0:T(8,128)(2,1)}, bf16[4,128,4608]{2,1,0:T(8,128)(2,1)}) custom-call(s32[10]{0:T(128)} %pad_add_fusion.info_ref, bf16[8,672,2048]{2,1,0:T(8,128)(2,1)} %all-to-all-done.x.refs_0_.refs_1_.refs_2_.refs_3_.refs_4_.refs_5_.refs_6_.refs_7_.a, bf16[4,64,512]{2,1,0:T(8,128)(2,1)} %pad_maximum_fusion.2.d, ...), custom_call_target="tpu_custom_call" | custom-call | flops 1000000000 | tf_op jit(solution)/shard_map/place_qkv/pallas_call | solution.py:261
  636.6 13.4 %place_output_0.1 = (bf16[4096,2048]{1,0:T(8,128)(2,1)}, bf16[2,256,768]{2,1,0:T(8,128)(2,1)}, bf16[2,256,768]{2,1,0:T(8,128)(2,1)}) custom-call(s32[10]{0:T(128)} %pad_add_fusion.info_ref, bf16[1024,4096]{1,0:T(8,128)(2,1)} %all-gather.2.cloned.1.call-done.a, bf16[2,576,768]{2,1,0:T(8,128)(2,1)} %pick_output_0_0.1.refs_0_, ...), custom_call_target="tpu_custom_call" | custom-call | flops 199999995904 | tf_op jit(solution)/shard_map/place_output_0/pallas_call | solution.py:313
  668.6 25.7 %collective-permute-done.18.refs_1_ = bf16[2,512,768]{2,1,0:T(8,128)(2,1)} collective-permute-done((bf16[2,512,768]{2,1,0:T(8,128)(2,1)}, bf16[2,512,768]{2,1,0:T(8,128)(2,1)}, u32[]{:S(2)}, u32[]{:S(2)}) %collective-permute-start.18) | collective-permute-done | bytes 1572896 | tf_op jit(solution)/shard_map/ppermute | solution.py:25
  694.4 13.6 %place_output_768.1 = (bf16[4096,2048]{1,0:T(8,128)(2,1)}, bf16[2,256,768]{2,1,0:T(8,128)(2,1)}, bf16[2,256,768]{2,1,0:T(8,128)(2,1)}) custom-call(s32[10]{0:T(128)} %pad_add_fusion.info_ref, bf16[1024,4096]{1,0:T(8,128)(2,1)} %all-gather.2.cloned.1.call-done.a, bf16[2,512,768]{2,1,0:T(8,128)(2,1)} %pick_output_0_6.1.refs_0_, ...), custom_call_target="tpu_custom_call", output_to_operand_aliasing={{0}: (6, {})} | custom-call | flops 199999995904 | tf_op jit(solution)/shard_map/place_output_768/pallas_call | solution.py:313
  707.9 26.9 %collective-permute-start.23 = (bf16[2,256,768]{2,1,0:T(8,128)(2,1)}, bf16[2,256,768]{2,1,0:T(8,128)(2,1)}, u32[]{:S(2)}, u32[]{:S(2)}) collective-permute-start(bf16[2,256,768]{2,1,0:T(8,128)(2,1)} %get-tuple-element.35), channel_id=1, source_target_pairs={{0,1},{1,0},{2,3},{3,2},{4,5},{5,4},{6,7},{7,6},{8,9},{9,8},{10,11... | collective-permute-start | bytes 2359304 | tf_op jit(solution)/shard_map/ppermute | solution.py:25
  757.4 13.1 %collective-permute-done.23 = bf16[2,256,768]{2,1,0:T(8,128)(2,1)} collective-permute-done((bf16[2,256,768]{2,1,0:T(8,128)(2,1)}, bf16[2,256,768]{2,1,0:T(8,128)(2,1)}, u32[]{:S(2)}, u32[]{:S(2)}) %collective-permute-start.23) | collective-permute-done | bytes 786464 | tf_op jit(solution)/shard_map/ppermute | solution.py:25
  779.4 9.5 %collective-permute-done.15.refs_1_ = bf16[2,512,384]{2,1,0:T(8,128)(2,1)} collective-permute-done((bf16[2,512,384]{2,1,0:T(8,128)(2,1)}, bf16[2,512,384]{2,1,0:T(8,128)(2,1)}, u32[]{:S(2)}, u32[]{:S(2)}) %collective-permute-start.15) | collective-permute-done | bytes 786464 | tf_op jit(solution)/shard_map/ppermute | solution.py:25
  788.9 13.9 %collective-permute-start.22 = (bf16[1,256,768]{2,1,0:T(8,128)(2,1)}, bf16[1,256,768]{2,1,0:T(8,128)(2,1)}, u32[]{:S(2)}, u32[]{:S(2)}) collective-permute-start(bf16[1,256,768]{2,1,0:T(8,128)(2,1)} %slice.117), channel_id=1, source_target_pairs={{0,2},{1,3},{2,0},{3,1},{4,6},{5,7},{6,4},{7,5},{8,10},{9,11},{10,... | collective-permute-start | bytes 1179656 | tf_op jit(solution)/shard_map/ppermute | solution.py:25
  808.2 11.0 %place_output_1536.1 = (bf16[4096,2048]{1,0:T(8,128)(2,1)}, bf16[2,256,384]{2,1,0:T(8,128)(2,1)}, bf16[2,256,384]{2,1,0:T(8,128)(2,1)}) custom-call(s32[10]{0:T(128)} %pad_add_fusion.info_ref, bf16[1024,4096]{1,0:T(8,128)(2,1)} %all-gather.2.cloned.1.call-done.a, bf16[2,512,384]{2,1,0:T(8,128)(2,1)} %pick_output_0_12.1.refs_0_, ...), custom_call_target="tpu_custom_call", output_to_operand_aliasing={{0}: (6, {})} | custom-call | flops 199999995904 | tf_op jit(solution)/shard_map/place_output_1536/pallas_call | solution.py:313
  819.2 30.9 %collective-permute-done.22 = bf16[1,256,768]{2,1,0:T(8,128)(2,1)} collective-permute-done((bf16[1,256,768]{2,1,0:T(8,128)(2,1)}, bf16[1,256,768]{2,1,0:T(8,128)(2,1)}, u32[]{:S(2)}, u32[]{:S(2)}) %collective-permute-start.22) | collective-permute-done | bytes 393248 | tf_op jit(solution)/shard_map/ppermute | solution.py:25
  854.4 9.8 %collective-permute-done.24 = bf16[1,256,768]{2,1,0:T(8,128)(2,1)} collective-permute-done((bf16[1,256,768]{2,1,0:T(8,128)(2,1)}, bf16[1,256,768]{2,1,0:T(8,128)(2,1)}, u32[]{:S(2)}, u32[]{:S(2)}) %collective-permute-start.24) | collective-permute-done | bytes 393248 | tf_op jit(solution)/shard_map/ppermute | solution.py:25
  869.3 7.5 place_output_1920.1
  (156 shorter events, 145.2 us)
Async XLA Ops:
  13.2 41.5 %collective-permute-start.2 = (bf16[640,512]{1,0:T(8,128)(2,1)}, bf16[640,512]{1,0:T(8,128)(2,1)S(1)}, u32[]{:S(2)}, u32[]{:S(2)}) collective-permute-start(bf16[640,512]{1,0:T(8,128)(2,1)} %get-tuple-element.26), channel_id=1, source_target_pairs={{0,3},{1,2},{2,1},{3,0},{4,7},{5,6},{6,5},{7,4},{8,11},{9,10},{10,... | collective-permute-start | bytes 1966088 | tf_op jit(solution)/shard_map/ppermute | solution.py:25
  18.2 147.1 %collective-permute-start.1 = (bf16[640,512]{1,0:T(8,128)(2,1)}, bf16[640,512]{1,0:T(8,128)(2,1)S(1)}, u32[]{:S(2)}, u32[]{:S(2)}) collective-permute-start(bf16[640,512]{1,0:T(8,128)(2,1)} %get-tuple-element.25), channel_id=1, source_target_pairs={{0,2},{1,3},{2,0},{3,1},{4,6},{5,7},{6,4},{7,5},{8,10},{9,11},{10,... | collective-permute-start | bytes 1966088 | tf_op jit(solution)/shard_map/ppermute | solution.py:25
  18.2 147.1 %collective-permute-start = (bf16[640,512]{1,0:T(8,128)(2,1)}, bf16[640,512]{1,0:T(8,128)(2,1)S(1)}, u32[]{:S(2)}, u32[]{:S(2)}) collective-permute-start(bf16[640,512]{1,0:T(8,128)(2,1)} %get-tuple-element.24), channel_id=1, source_target_pairs={{0,1},{1,0},{2,3},{3,2},{4,5},{5,4},{6,7},{7,6},{8,9},{9,8},{10,11... | collective-permute-start | bytes 1966088 | tf_op jit(solution)/shard_map/ppermute | solution.py:25
  35.7 280.0 %all-to-all-start = ((bf16[8,672,2048]{2,1,0:T(8,128)(2,1)}), bf16[8,672,2048]{2,1,0:T(8,128)(2,1)}, u32[]{:S(2)}, u32[]{:S(2)}) async-start(bf16[8,672,2048]{2,1,0:T(8,128)(2,1)} %split_columns.1), calls=%async_computation | async-start | bytes 44040192 | tf_op jit(solution)/shard_map/all_to_all | solution.py:379
  41.9 594.7 %all-gather.2.cloned.1.call-start = ((), (), s32[]{:S(2)}) async-start(), calls=%async_computation.1 | async-start | bytes 9437184 | tf_op jit(solution)/shard_map/all_gather | solution.py:392
  46.4 164.0 %collective-permute-start.4 = (bf16[512,2048]{1,0:T(8,128)(2,1)}, bf16[512,2048]{1,0:T(8,128)(2,1)}, u32[]{:S(2)}, u32[]{:S(2)}) collective-permute-start(bf16[512,2048]{1,0:T(8,128)(2,1)} %pick_query_2_0.1), channel_id=1, source_target_pairs={{0,2},{1,3},{2,0},{3,1},{4,6},{5,7},{6,4},{7,5},{8,10},{9,11},{10,... | collective-permute-start | bytes 6291464 | tf_op jit(solution)/shard_map/ppermute | solution.py:25
  53.2 166.6 %collective-permute-start.5 = (bf16[512,2048]{1,0:T(8,128)(2,1)}, bf16[512,2048]{1,0:T(8,128)(2,1)}, u32[]{:S(2)}, u32[]{:S(2)}) collective-permute-start(bf16[512,2048]{1,0:T(8,128)(2,1)} %pick_query_3_0.1), channel_id=1, source_target_pairs={{0,3},{1,2},{2,1},{3,0},{4,7},{5,6},{6,5},{7,4},{8,11},{9,10},{10,... | collective-permute-start | bytes 6291464 | tf_op jit(solution)/shard_map/ppermute | solution.py:25
  171.4 83.8 %collective-permute-start.3 = (bf16[512,2048]{1,0:T(8,128)(2,1)}, bf16[512,2048]{1,0:T(8,128)(2,1)S(1)}, u32[]{:S(2)}, u32[]{:S(2)}) collective-permute-start(bf16[512,2048]{1,0:T(8,128)(2,1)} %pick_query_1_0.1), channel_id=1, source_target_pairs={{0,1},{1,0},{2,3},{3,2},{4,5},{5,4},{6,7},{7,6},{8,9},{9,8},{10,11... | collective-permute-start | bytes 6291464 | tf_op jit(solution)/shard_map/ppermute | solution.py:25
  176.0 151.5 %collective-permute-start.6 = (bf16[512,2048]{1,0:T(8,128)(2,1)}, bf16[512,2048]{1,0:T(8,128)(2,1)}, u32[]{:S(2)}, u32[]{:S(2)}) collective-permute-start(bf16[512,2048]{1,0:T(8,128)(2,1)} %pick_query_1_1.1), channel_id=1, source_target_pairs={{0,1},{1,0},{2,3},{3,2},{4,5},{5,4},{6,7},{7,6},{8,9},{9,8},{10,11... | collective-permute-start | bytes 6291464 | tf_op jit(solution)/shard_map/ppermute | solution.py:25
  182.5 283.6 %collective-permute-start.7 = (bf16[512,2048]{1,0:T(8,128)(2,1)}, bf16[512,2048]{1,0:T(8,128)(2,1)}, u32[]{:S(2)}, u32[]{:S(2)}) collective-permute-start(bf16[512,2048]{1,0:T(8,128)(2,1)} %pick_query_2_1.1), channel_id=1, source_target_pairs={{0,2},{1,3},{2,0},{3,1},{4,6},{5,7},{6,4},{7,5},{8,10},{9,11},{10,... | collective-permute-start | bytes 6291464 | tf_op jit(solution)/shard_map/ppermute | solution.py:25
  210.4 255.7 %collective-permute-start.8 = (bf16[512,2048]{1,0:T(8,128)(2,1)}, bf16[512,2048]{1,0:T(8,128)(2,1)}, u32[]{:S(2)}, u32[]{:S(2)}) collective-permute-start(bf16[512,2048]{1,0:T(8,128)(2,1)} %pick_query_3_1.1), channel_id=1, source_target_pairs={{0,3},{1,2},{2,1},{3,0},{4,7},{5,6},{6,5},{7,4},{8,11},{9,10},{10,... | collective-permute-start | bytes 6291464 | tf_op jit(solution)/shard_map/ppermute | solution.py:25
  319.6 229.5 %collective-permute-start.11 = (bf16[2,576,768]{2,1,0:T(8,128)(2,1)}, bf16[2,576,768]{2,1,0:T(8,128)(2,1)}, u32[]{:S(2)}, u32[]{:S(2)}) collective-permute-start(bf16[2,576,768]{2,1,0:T(8,128)(2,1)} %pick_output_3_0.1), channel_id=1, source_target_pairs={{0,3},{1,2},{2,1},{3,0},{4,7},{5,6},{6,5},{7,4},{8,11},{9,10},{10,... | collective-permute-start | bytes 5308424 | tf_op jit(solution)/shard_map/ppermute | solution.py:25
  327.4 261.1 %collective-permute-start.10 = (bf16[2,576,768]{2,1,0:T(8,128)(2,1)}, bf16[2,576,768]{2,1,0:T(8,128)(2,1)}, u32[]{:S(2)}, u32[]{:S(2)}) collective-permute-start(bf16[2,576,768]{2,1,0:T(8,128)(2,1)} %pick_output_2_0.1), channel_id=1, source_target_pairs={{0,2},{1,3},{2,0},{3,1},{4,6},{5,7},{6,4},{7,5},{8,10},{9,11},{10,... | collective-permute-start | bytes 5308424 | tf_op jit(solution)/shard_map/ppermute | solution.py:25
  469.9 126.0 %collective-permute-start.9 = (bf16[2,576,768]{2,1,0:T(8,128)(2,1)}, bf16[2,576,768]{2,1,0:T(8,128)(2,1)}, u32[]{:S(2)}, u32[]{:S(2)}) collective-permute-start(bf16[2,576,768]{2,1,0:T(8,128)(2,1)} %pick_output_1_0.1), channel_id=1, source_target_pairs={{0,1},{1,0},{2,3},{3,2},{4,5},{5,4},{6,7},{7,6},{8,9},{9,8},{10,11... | collective-permute-start | bytes 5308424 | tf_op jit(solution)/shard_map/ppermute | solution.py:25
  529.3 165.1 %collective-permute-start.18 = (bf16[2,512,768]{2,1,0:T(8,128)(2,1)}, bf16[2,512,768]{2,1,0:T(8,128)(2,1)}, u32[]{:S(2)}, u32[]{:S(2)}) collective-permute-start(bf16[2,512,768]{2,1,0:T(8,128)(2,1)} %pick_output_1_6.1), channel_id=1, source_target_pairs={{0,1},{1,0},{2,3},{3,2},{4,5},{5,4},{6,7},{7,6},{8,9},{9,8},{10,11... | collective-permute-start | bytes 4718600 | tf_op jit(solution)/shard_map/ppermute | solution.py:25
  533.2 161.1 %collective-permute-start.19 = (bf16[2,512,768]{2,1,0:T(8,128)(2,1)}, bf16[2,512,768]{2,1,0:T(8,128)(2,1)}, u32[]{:S(2)}, u32[]{:S(2)}) collective-permute-start(bf16[2,512,768]{2,1,0:T(8,128)(2,1)} %pick_output_2_6.1), channel_id=1, source_target_pairs={{0,2},{1,3},{2,0},{3,1},{4,6},{5,7},{6,4},{7,5},{8,10},{9,11},{10,... | collective-permute-start | bytes 4718600 | tf_op jit(solution)/shard_map/ppermute | solution.py:25
  549.1 145.3 %collective-permute-start.20 = (bf16[2,512,768]{2,1,0:T(8,128)(2,1)}, bf16[2,512,768]{2,1,0:T(8,128)(2,1)}, u32[]{:S(2)}, u32[]{:S(2)}) collective-permute-start(bf16[2,512,768]{2,1,0:T(8,128)(2,1)} %pick_output_3_6.1), channel_id=1, source_target_pairs={{0,3},{1,2},{2,1},{3,0},{4,7},{5,6},{6,5},{7,4},{8,11},{9,10},{10,... | collective-permute-start | bytes 4718600 | tf_op jit(solution)/shard_map/ppermute | solution.py:25
  636.5 24.2 %collective-permute-start.25 = (bf16[4,128,4608]{2,1,0:T(8,128)(2,1)}, bf16[4,128,4608]{2,1,0:T(8,128)(2,1)}, u32[]{:S(2)}, u32[]{:S(2)}) collective-permute-start(bf16[4,128,4608]{2,1,0:T(8,128)(2,1)} %get-tuple-element.29.refs_5_), channel_id=1, source_target_pairs={{0,4},{4,0},{8,12},{12,8},{16,20},{20,16},{24,28},{28,24},{1,5},{5... | collective-permute-start | bytes 14155784 | tf_op jit(solution)/shard_map/ppermute | solution.py:25
  650.0 103.8 %collective-permute-start.21 = (bf16[2,256,768]{2,1,0:T(8,128)(2,1)}, bf16[2,256,768]{2,1,0:T(8,128)(2,1)}, u32[]{:S(2)}, u32[]{:S(2)}) collective-permute-start(bf16[2,256,768]{2,1,0:T(8,128)(2,1)} %get-tuple-element.33), channel_id=1, source_target_pairs={{0,1},{1,0},{2,3},{3,2},{4,5},{5,4},{6,7},{7,6},{8,9},{9,8},{10,11... | collective-permute-start | bytes 2359304 | tf_op jit(solution)/shard_map/ppermute | solution.py:25
  667.2 105.5 %collective-permute-start.26 = (bf16[2,128,4608]{2,1,0:T(8,128)(2,1)}, bf16[2,128,4608]{2,1,0:T(8,128)(2,1)}, u32[]{:S(2)}, u32[]{:S(2)}) collective-permute-start(bf16[2,128,4608]{2,1,0:T(8,128)(2,1)} %slice.99), channel_id=1, source_target_pairs={{0,8},{4,12},{8,0},{12,4},{16,24},{20,28},{24,16},{28,20},{1,9},{5... | collective-permute-start | bytes 7077896 | tf_op jit(solution)/shard_map/ppermute | solution.py:25
  707.9 62.6 %collective-permute-start.23 = (bf16[2,256,768]{2,1,0:T(8,128)(2,1)}, bf16[2,256,768]{2,1,0:T(8,128)(2,1)}, u32[]{:S(2)}, u32[]{:S(2)}) collective-permute-start(bf16[2,256,768]{2,1,0:T(8,128)(2,1)} %get-tuple-element.35), channel_id=1, source_target_pairs={{0,1},{1,0},{2,3},{3,2},{4,5},{5,4},{6,7},{7,6},{8,9},{9,8},{10,11... | collective-permute-start | bytes 2359304 | tf_op jit(solution)/shard_map/ppermute | solution.py:25
  741.2 47.7 %collective-permute-start.15 = (bf16[2,512,384]{2,1,0:T(8,128)(2,1)}, bf16[2,512,384]{2,1,0:T(8,128)(2,1)}, u32[]{:S(2)}, u32[]{:S(2)}) collective-permute-start(bf16[2,512,384]{2,1,0:T(8,128)(2,1)} %pick_output_1_12.1.refs_11_.refs_8_), channel_id=1, source_target_pairs={{0,1},{1,0},{2,3},{3,2},{4,5},{5,4},{6,7},{7,6},{8,9},{9,8},{10,11... | collective-permute-start | bytes 2359304 | tf_op jit(solution)/shard_map/ppermute | solution.py:25
  741.2 61.7 %collective-permute-start.16 = (bf16[2,512,384]{2,1,0:T(8,128)(2,1)}, bf16[2,512,384]{2,1,0:T(8,128)(2,1)}, u32[]{:S(2)}, u32[]{:S(2)}) collective-permute-start(bf16[2,512,384]{2,1,0:T(8,128)(2,1)} %pick_output_2_12.1.refs_9_.refs_6_), channel_id=1, source_target_pairs={{0,2},{1,3},{2,0},{3,1},{4,6},{5,7},{6,4},{7,5},{8,10},{9,11},{10,... | collective-permute-start | bytes 2359304 | tf_op jit(solution)/shard_map/ppermute | solution.py:25
  753.8 52.9 %collective-permute-start.17 = (bf16[2,512,384]{2,1,0:T(8,128)(2,1)S(1)}, bf16[2,512,384]{2,1,0:T(8,128)(2,1)S(1)}, u32[]{:S(2)}, u32[]{:S(2)}) collective-permute-start(bf16[2,512,384]{2,1,0:T(8,128)(2,1)S(1)} %copy-done.2), channel_id=1, source_target_pairs={{0,3},{1,2},{2,1},{3,0},{4,7},{5,6},{6,5},{7,4},{8,11},{9,10},{10,... | collective-permute-start | bytes 2359304 | tf_op jit(solution)/shard_map/ppermute | solution.py:25
  770.5 98.0 %collective-permute-start.12 = (bf16[2,512,128]{2,1,0:T(8,128)(2,1)}, bf16[2,512,128]{2,1,0:T(8,128)(2,1)}, u32[]{:S(2)}, u32[]{:S(2)}) collective-permute-start(bf16[2,512,128]{2,1,0:T(8,128)(2,1)} %pick_output_1_15.1), channel_id=1, source_target_pairs={{0,1},{1,0},{2,3},{3,2},{4,5},{5,4},{6,7},{7,6},{8,9},{9,8},{10,11... | collective-permute-start | bytes 786440 | tf_op jit(solution)/shard_map/ppermute | solution.py:25
  772.9 95.6 %collective-permute-start.13 = (bf16[2,512,128]{2,1,0:T(8,128)(2,1)}, bf16[2,512,128]{2,1,0:T(8,128)(2,1)}, u32[]{:S(2)}, u32[]{:S(2)}) collective-permute-start(bf16[2,512,128]{2,1,0:T(8,128)(2,1)} %pick_output_2_15.1), channel_id=1, source_target_pairs={{0,2},{1,3},{2,0},{3,1},{4,6},{5,7},{6,4},{7,5},{8,10},{9,11},{10,... | collective-permute-start | bytes 786440 | tf_op jit(solution)/shard_map/ppermute | solution.py:25
  788.9 61.2 %collective-permute-start.22 = (bf16[1,256,768]{2,1,0:T(8,128)(2,1)}, bf16[1,256,768]{2,1,0:T(8,128)(2,1)}, u32[]{:S(2)}, u32[]{:S(2)}) collective-permute-start(bf16[1,256,768]{2,1,0:T(8,128)(2,1)} %slice.117), channel_id=1, source_target_pairs={{0,2},{1,3},{2,0},{3,1},{4,6},{5,7},{6,4},{7,5},{8,10},{9,11},{10,... | collective-permute-start | bytes 1179656 | tf_op jit(solution)/shard_map/ppermute | solution.py:25
  802.9 61.3 %collective-permute-start.24 = (bf16[1,256,768]{2,1,0:T(8,128)(2,1)}, bf16[1,256,768]{2,1,0:T(8,128)(2,1)}, u32[]{:S(2)}, u32[]{:S(2)}) collective-permute-start(bf16[1,256,768]{2,1,0:T(8,128)(2,1)} %slice.119), channel_id=1, source_target_pairs={{0,2},{1,3},{2,0},{3,1},{4,6},{5,7},{6,4},{7,5},{8,10},{9,11},{10,... | collective-permute-start | bytes 1179656 | tf_op jit(solution)/shard_map/ppermute | solution.py:25
  806.7 59.3 %collective-permute-start.27 = (bf16[1,128,4608]{2,1,0:T(8,128)(2,1)}, bf16[1,128,4608]{2,1,0:T(8,128)(2,1)}, u32[]{:S(2)}, u32[]{:S(2)}) collective-permute-start(bf16[1,128,4608]{2,1,0:T(8,128)(2,1)} %slice.121), channel_id=1, source_target_pairs={{0,16},{4,20},{8,24},{12,28},{16,0},{20,4},{24,8},{28,12},{1,17},{... | collective-permute-start | bytes 3538952 | tf_op jit(solution)/shard_map/ppermute | solution.py:25
  850.1 18.5 %collective-permute-start.14 = (bf16[2,512,128]{2,1,0:T(8,128)(2,1)S(1)}, bf16[2,512,128]{2,1,0:T(8,128)(2,1)S(1)}, u32[]{:S(2)}, u32[]{:S(2)}) collective-permute-start(bf16[2,512,128]{2,1,0:T(8,128)(2,1)S(1)} %copy-done.17), channel_id=1, source_target_pairs={{0,3},{1,2},{2,1},{3,0},{4,7},{5,6},{6,5},{7,4},{8,11},{9,10},{10,... | collective-permute-start | bytes 786440 | tf_op jit(solution)/shard_map/ppermute | solution.py:25
  864.1 14.7 %collective-permute-start.28 = (bf16[2,256,384]{2,1,0:T(8,128)(2,1)}, bf16[2,256,384]{2,1,0:T(8,128)(2,1)}, u32[]{:S(2)}, u32[]{:S(2)}) collective-permute-start(bf16[2,256,384]{2,1,0:T(8,128)(2,1)} %get-tuple-element.39), channel_id=1, source_target_pairs={{0,1},{1,0},{2,3},{3,2},{4,5},{5,4},{6,7},{7,6},{8,9},{9,8},{10,11... | collective-permute-start | bytes 1179656 | tf_op jit(solution)/shard_map/ppermute | solution.py:25
  880.0 8.7 collective-permute-start.29
  (30 other events, 571.7 us)
Sparse Core Ops, SparseCore 0:
  54.8 167.4 all-gather.1
